TPU v7x, 128 devices: a whole 4x4x4 slice. The times are simulated.
128 devices in a mesh: head: 4 (over y_lo, core), blk: 32 (over x, y_hi, z).
Axes of the slice: x: 4, y: 4 (y_hi: 2, y_lo: 2; y = y_hi * 2 + y_lo), z: 4, core: 2. Of those that a mesh axis runs over, the one named last changes fastest.
Arguments:
- x_ckpt: bfloat16 [32768, 5120], P(('blk', 'head')), may hold values from -6 to 6
- w_query: bfloat16 [5120, 2560], P('blk', 'head'), may hold values from -0.078125 to 0.078125
- w_key: bfloat16 [5120, 512], P('blk', 'head'), may hold values from -0.078125 to 0.078125
- w_value: bfloat16 [5120, 512], P('blk', 'head'), may hold values from -0.078125 to 0.078125
- dout_seq: bfloat16 [32768, 2560], P(('blk', 'head')), may hold values from -192 to 192
- out_heads: bfloat16 [32768, 2560], P('blk', 'head'), may hold values from -4 to 4
- lse_heads: float32 [32768, 20], P('blk', 'head'), may hold values from 6.5 to 9
- span_order: int32 [256], replicated, may hold values from 0 to 255, each once
Outputs:
- grad_query: bfloat16 [32768, 2560], P(('blk', 'head'))
- grad_key: bfloat16 [32768, 512], P(('blk', 'head'))
- grad_value: bfloat16 [32768, 512], P(('blk', 'head'))
Inputs may be any that keep to these rules, and one draw needn't show every extreme that they name: `span_order`: each span number appears once.
All inputs are finite; a program needn't handle non-finite values.
Results may differ from a plain program's by a relative error of at most 0.018.
The roundings to bfloat16 on the way count: a program that leaves them out, or rounds other values in their place, can miss the bound.
Values may be sent and summed in bfloat16 or wider, within the bound.
No kernel may reach another device: no remote copies, remote signals or barrier semaphores. Data moves between devices by JAX's collectives and lax.ppermute only.
A program may use at most 128 MiB of HBM per device.

v0:
```python
import jax
import jax.numpy as jnp
from jax import lax
from jax.sharding import PartitionSpec as P

HD = 128
REACH = 2


def from_behind(block, axis, distance):
    devices = range(lax.axis_size(axis))
    route = [((i - distance) % len(devices), i) for i in devices]
    return lax.ppermute(block, axis, route)


def local(x_ckpt, w_query, w_key, w_value, dout_seq, out_heads, lse_heads, span_order):
    x_group = lax.all_gather(x_ckpt, "head", axis=0, tiled=True)
    group_len = x_group.shape[0]
    query_cols = w_query.shape[1]
    kv_cols = w_key.shape[1]
    pieces = (
        lax.all_gather(w_query, "blk", axis=0, tiled=True),
        lax.all_gather(w_key, "blk", axis=0, tiled=True),
        lax.all_gather(w_value, "blk", axis=0, tiled=True),
    )
    query_f, keys_f, values_f = tuple(
        (jnp.dot(x_group, piece, preferred_element_type=jnp.float32) for piece in pieces)
    )
    query = query_f.astype(jnp.bfloat16)
    keys = keys_f.astype(jnp.bfloat16)
    values = values_f.astype(jnp.bfloat16)
    grad_out = lax.all_to_all(dout_seq, "head", split_axis=1, concat_axis=0, tiled=True)
    local_heads = query_cols // HD
    local_kv = kv_cols // HD
    delta = jnp.sum(
        (grad_out.astype(jnp.float32) * out_heads.astype(jnp.float32)).reshape(
            group_len, local_heads, HD
        ),
        axis=2,
    )
    block_index = lax.axis_index("blk")
    block_count = lax.axis_size("blk")
    span_len = x_ckpt.shape[0] // 2
    spans_per = group_len // span_len

    def group_pos(group):
        span_ids = lax.dynamic_slice_in_dim(span_order, group * spans_per, spans_per)
        return (
            span_ids[:, None] * span_len + jnp.arange(span_len, dtype=jnp.int32)[None, :]
        ).reshape(group_len)

    query_pos = group_pos(block_index)
    scale = HD ** (-0.5)
    contract_rows = (((0,), (0,)), ((), ()))
    contract_cols = (((1,), (1,)), ((), ()))

    def tile(key_block, value_block, key_pos):
        visible = key_pos[None, :] <= query_pos[:, None]
        query_grads = []
        key_acc = jnp.zeros((group_len, HD), jnp.float32)
        value_acc = jnp.zeros((group_len, HD), jnp.float32)
        for member in range(local_heads // local_kv):
            query_head = query[:, member * HD : (member + 1) * HD]
            grad_head = grad_out[:, member * HD : (member + 1) * HD]
            attn_score = (
                lax.dot_general(
                    query_head, key_block, contract_cols, preferred_element_type=jnp.float32
                )
                * scale
            )
            attn_prob = jnp.where(visible, jnp.exp(attn_score - lse_heads[:, member][:, None]), 0.0)
            prob_half = attn_prob.astype(jnp.bfloat16)
            value_acc = value_acc + lax.dot_general(
                prob_half, grad_head, contract_rows, preferred_element_type=jnp.float32
            )
            grad_prob = lax.dot_general(
                grad_head, value_block, contract_cols, preferred_element_type=jnp.float32
            )
            score_half = (attn_prob * (grad_prob - delta[:, member][:, None]) * scale).astype(
                jnp.bfloat16
            )
            query_grads.append(jnp.dot(score_half, key_block, preferred_element_type=jnp.float32))
            key_acc = key_acc + lax.dot_general(
                score_half, query_head, contract_rows, preferred_element_type=jnp.float32
            )
        return (jnp.concatenate(query_grads, axis=1), key_acc, value_acc)

    grad_q, own_k, own_v = tile(keys, values, query_pos)
    contrib_list = [(own_k, own_v)]
    visiting = (keys, values)
    for cycle_step in range(1, REACH + 1):
        visiting = from_behind((visiting[0], visiting[1]), "blk", 1)
        part_q, part_k, part_v = tile(
            visiting[0], visiting[1], group_pos((block_index - cycle_step) % block_count)
        )
        grad_q = grad_q + part_q
        contrib_list.append((part_k, part_v))
    returned = contrib_list[REACH]
    for cycle_step in range(REACH, 0, -1):
        arrived = from_behind(returned, "blk", -1)
        returned = (
            arrived[0] + contrib_list[cycle_step - 1][0],
            arrived[1] + contrib_list[cycle_step - 1][1],
        )
    grad_k, grad_v = returned
    grad_query, grad_key, grad_value = (
        lax.all_to_all(
            grad_q.astype(jnp.bfloat16), "head", split_axis=0, concat_axis=1, tiled=True
        ),
        lax.all_to_all(
            grad_k.astype(jnp.bfloat16), "head", split_axis=0, concat_axis=1, tiled=True
        ),
        lax.all_to_all(
            grad_v.astype(jnp.bfloat16), "head", split_axis=0, concat_axis=1, tiled=True
        ),
    )
    return (grad_query, grad_key, grad_value)


def solution(mesh):
    return jax.shard_map(
        local,
        mesh=mesh,
        in_specs=(
            P(("blk", "head"), None),
            P("blk", "head"),
            P("blk", "head"),
            P("blk", "head"),
            P(("blk", "head"), None),
            P("blk", "head"),
            P("blk", "head"),
            P(),
        ),
        out_specs=(P(("blk", "head"), None), P(("blk", "head"), None), P(("blk", "head"), None)),
        check_vma=False,
    )
```

profile of v0, /device:TPU:1, one launch (start us, length us, event | category | flops | bytes accessed | tf_op | source)
XLA Modules:
  0.0 539.5 jit_solution(11388304336693866262)
XLA Ops:
  9.4 2.4 copy.50
  11.8 4.9 all-to-all-start
  19.2 14.4 %all-to-all-done = bf16[256,4,640]{0,2,1:T(8,128)(2,1)S(1)} async-done(((bf16[256,4,640]{0,2,1:T(8,128)(2,1)}), bf16[256,4,640]{0,2,1:T(8,128)(2,1)S(1)}, u32[]{:S(2)}, u32[]{:S(2)}) %all-to-all-start) | async-done | bytes 1310752 | tf_op jit(solution)/shard_map/all_to_all | solution.py:32
  34.8 1.8 convert_multiply_fusion
  36.9 43.5 %all-gather.9.cloned.1.call-done = bf16[5120,128]{1,0:T(8,128)(2,1)} async-done(((bf16[160,128]{1,0:T(8,128)(2,1)}), bf16[5120,128]{1,0:T(8,128)(2,1)}) %all-gather.9.cloned.1.call-update) | async-done | bytes 1310736 | tf_op jit(solution)/shard_map/all_gather | solution.py:23
  80.4 99.4 %all-gather.5.cloned.1.call-done = bf16[1024,5120]{1,0:T(8,128)(2,1)} async-done(((bf16[256,5120]{1,0:T(8,128)(2,1)}), bf16[1024,5120]{1,0:T(8,128)(2,1)}) %all-gather.5.cloned.1.call-update) | async-done | bytes 10485776 | tf_op jit(solution)/shard_map/all_gather | solution.py:17
  179.8 7.2 %convolution_convert_fusion.2 = bf16[1024,128]{1,0:T(8,128)(2,1)S(1)} fusion(bf16[1024,5120]{1,0:T(8,128)(2,1)} %all-gather.5.cloned.1.call-done, bf16[5120,128]{1,0:T(8,128)(2,1)} %all-gather.9.cloned.1.call-done), kind=kOutput, calls=%fused_computation.120 | convolution fusion | flops 1342308352 | bytes 12058624 | tf_op jit(solution)/shard_map/dot_general | solution.py:27
  188.3 88.1 %all-gather.7.cloned.1.call-done = bf16[5120,640]{1,0:T(8,128)(2,1)} async-done(((bf16[160,640]{1,0:T(8,128)(2,1)}), bf16[5120,640]{1,0:T(8,128)(2,1)}) %all-gather.7.cloned.1.call-update) | async-done | bytes 6553616 | tf_op jit(solution)/shard_map/all_gather | solution.py:22
  276.4 12.9 %convolution_convert_fusion = bf16[1024,640]{1,0:T(8,128)(2,1)S(1)} fusion(bf16[1024,5120]{1,0:T(8,128)(2,1)} %all-gather.5.cloned.1.call-done, bf16[5120,640]{1,0:T(8,128)(2,1)} %all-gather.7.cloned.1.call-done), kind=kOutput, calls=%fused_computation.92 | convolution fusion | flops 6711541760 | bytes 18350080 | tf_op jit(solution)/shard_map/dot_general | solution.py:27
  289.3 2.8 fusion.128
  292.0 2.8 fusion.143
  294.8 2.7 fusion.158
  297.5 2.7 fusion.173
  300.2 2.8 fusion.191
  303.0 40.5 %all-gather.11.cloned.1.call-done = bf16[5120,128]{1,0:T(8,128)(2,1)} async-done(((bf16[160,128]{1,0:T(8,128)(2,1)}), bf16[5120,128]{1,0:T(8,128)(2,1)}) %all-gather.11.cloned.1.call-update) | async-done | bytes 1310736 | tf_op jit(solution)/shard_map/all_gather | solution.py:24
  343.5 7.3 %convolution_convert_fusion.1 = bf16[1024,128]{1,0:T(8,128)(2,1)S(1)} fusion(bf16[1024,5120]{1,0:T(8,128)(2,1)} %all-gather.5.cloned.1.call-done, bf16[5120,128]{1,0:T(8,128)(2,1)} %all-gather.11.cloned.1.call-done), kind=kOutput, calls=%fused_computation.119 | convolution fusion | flops 1342308352 | bytes 12058624 | tf_op jit(solution)/shard_map/dot_general | solution.py:27
  351.4 2.0 fusion.29
  355.5 1.9 fusion.23
  358.2 2.0 fusion.25
  362.3 2.0 fusion.27
  370.2 2.1 fusion.21
  372.4 2.3 fusion.109
  382.3 2.2 fusion.19
  388.9 2.3 fusion.82
  391.1 1.9 fusion.17
  393.8 2.0 fusion.15
  398.1 2.0 fusion.13
  401.5 2.4 fusion.11
  407.5 14.5 %collective-permute-done.2 = bf16[1024,128]{1,0:T(8,128)(2,1)S(1)} collective-permute-done((bf16[1024,128]{1,0:T(8,128)(2,1)S(1)}, bf16[1024,128]{1,0:T(8,128)(2,1)S(1)}, u32[]{:S(2)}, u32[]{:S(2)}) %collective-permute-start.2) | collective-permute-done | bytes 262176 | tf_op jit(solution)/shard_map/ppermute | solution.py:13
  426.4 2.1 fusion.9
  434.4 2.3 fusion.97
  436.7 1.9 fusion.7
  439.4 2.0 fusion.5
  442.1 2.2 fusion.3
  445.1 2.0 fusion.1
  447.0 1.6 convolution_add_fusion.8
  455.1 8.1 %all-to-all-start.1 = ((bf16[4,256,640]{2,1,0:T(8,128)(2,1)}), bf16[4,256,640]{2,1,0:T(8,128)(2,1)}, u32[]{:S(2)}, u32[]{:S(2)}) async-start(bf16[4,256,640]{2,1,0:T(8,128)(2,1)} %add_convert_fusion), calls=%async_computation.1 | async-start | bytes 2621440 | tf_op jit(solution)/shard_map/all_to_all | solution.py:107
  463.2 7.1 %collective-permute-done.6 = f32[1024,128]{1,0:T(8,128)} collective-permute-done((f32[1024,128]{1,0:T(8,128)}, f32[1024,128]{1,0:T(8,128)}, u32[]{:S(2)}, u32[]{:S(2)}) %collective-permute-start.6) | collective-permute-done | bytes 524320 | tf_op jit(solution)/shard_map/ppermute | solution.py:13
  470.2 4.7 fusion.112
  474.9 6.8 %collective-permute-start.7 = (f32[1024,128]{1,0:T(8,128)}, f32[1024,128]{1,0:T(8,128)}, u32[]{:S(2)}, u32[]{:S(2)}) collective-permute-start(f32[1024,128]{1,0:T(8,128)} %fusion.112), channel_id=1, source_target_pairs={{1,0},{2,1},{3,2},{4,3},{5,4},{6,5},{7,6},{8,7},{9,8},{10,9},{11,1... | collective-permute-start | bytes 1572872 | tf_op jit(solution)/shard_map/ppermute | solution.py:13
  481.7 1.6 fusion.75
  484.1 25.3 %all-to-all-done.1 = bf16[4,256,640]{2,1,0:T(8,128)(2,1)} async-done(((bf16[4,256,640]{2,1,0:T(8,128)(2,1)}), bf16[4,256,640]{2,1,0:T(8,128)(2,1)}, u32[]{:S(2)}, u32[]{:S(2)}) %all-to-all-start.1) | async-done | bytes 1310752 | tf_op jit(solution)/shard_map/all_to_all | solution.py:107
  509.4 2.5 copy.87
  511.8 1.8 add_convert_fusion.1
  513.6 3.8 all-to-all-start.3
  518.2 4.4 all-to-all-done.3
  522.6 4.2 all-to-all-start.2
  527.6 4.4 all-to-all-done.2
  (129 shorter events, 60.6 us)
Async XLA Ops:
  7.2 10.2 %copy-start.12 = (bf16[1024,640]{1,0:T(8,128)(2,1)S(1)}, bf16[1024,640]{1,0:T(8,128)(2,1)}, u32[]{:S(2)}) copy-start(bf16[1024,640]{1,0:T(8,128)(2,1)} %param.13) | copy-start | bytes 3932164
  7.2 73.2 %all-gather.9.cloned.1.call-start = ((), (), s32[]{:S(2)}) async-start(), calls=%async_computation.6 | async-start | bytes 1351680 | tf_op jit(solution)/shard_map/all_gather | solution.py:23
  7.9 171.8 %all-gather.5.cloned.1.call-start = ((), (), s32[]{:S(2)}) async-start(), calls=%async_computation.4 | async-start | bytes 13107200 | tf_op jit(solution)/shard_map/all_gather | solution.py:17
  8.7 10.2 %copy-start.15 = (s32[256]{0:T(256)S(1)}, s32[256]{0:T(256)}, u32[]{:S(2)}) copy-start(s32[256]{0:T(256)} %param.15) | copy-start | bytes 3076
  8.7 10.5 %copy-start.14 = (f32[1024,5]{0,1:T(8,128)S(1)}, f32[1024,5]{0,1:T(8,128)}, u32[]{:S(2)}) copy-start(f32[1024,5]{0,1:T(8,128)} %param.14) | copy-start | bytes 61444
  8.7 267.7 %all-gather.7.cloned.1.call-start = ((), (), s32[]{:S(2)}) async-start(), calls=%async_computation.5 | async-start | bytes 6758400 | tf_op jit(solution)/shard_map/all_gather | solution.py:22
  11.8 21.7 %all-to-all-start = ((bf16[256,4,640]{0,2,1:T(8,128)(2,1)}), bf16[256,4,640]{0,2,1:T(8,128)(2,1)S(1)}, u32[]{:S(2)}, u32[]{:S(2)}) async-start(bf16[256,4,640]{0,2,1:T(8,128)(2,1)} %bitcast.2), calls=%async_computation | async-start | bytes 2621440 | tf_op jit(solution)/shard_map/all_to_all | solution.py:32
  16.8 326.7 %all-gather.11.cloned.1.call-start = ((), (), s32[]{:S(2)}) async-start(), calls=%async_computation.7 | async-start | bytes 1351680 | tf_op jit(solution)/shard_map/all_gather | solution.py:24
  33.7 1.1 copy-start.4
  186.9 191.0 %collective-permute-start = (bf16[1024,128]{1,0:T(8,128)(2,1)S(1)}, bf16[1024,128]{1,0:T(8,128)(2,1)S(1)}, u32[]{:S(2)}, u32[]{:S(2)}) collective-permute-start(bf16[1024,128]{1,0:T(8,128)(2,1)S(1)} %convolution_convert_fusion.2), channel_id=1, source_target_pairs={{31,0},{0,1},{1,2},{2,3},{3,4},{4,5},{5,6},{6,7},{7,8},{8,9},{9,10... | collective-permute-start | bytes 786440 | tf_op jit(solution)/shard_map/ppermute | solution.py:13
  343.5 7.9 %copy-start.5 = (bf16[4,80,8,256]{3,2,0,1:T(8,128)(2,1)S(1)}, bf16[4,80,8,256]{3,2,0,1:T(8,128)(2,1)}, u32[]{:S(2)}) copy-start(bf16[4,80,8,256]{3,2,0,1:T(8,128)(2,1)} %copy-done.4) | copy-start | bytes 3932164
  343.5 7.9 %copy-start.10 = (f32[1024,1024]{1,0:T(8,128)S(1)}, f32[1024,1024]{1,0:T(8,128)}, u32[]{:S(2)}) copy-start(f32[1024,1024]{1,0:T(8,128)} %fusion.191) | copy-start | bytes 12582916
  350.8 31.5 %collective-permute-start.1 = (bf16[1024,128]{1,0:T(8,128)(2,1)S(1)}, bf16[1024,128]{1,0:T(8,128)(2,1)S(1)}, u32[]{:S(2)}, u32[]{:S(2)}) collective-permute-start(bf16[1024,128]{1,0:T(8,128)(2,1)S(1)} %convolution_convert_fusion.1), channel_id=1, source_target_pairs={{31,0},{0,1},{1,2},{2,3},{3,4},{4,5},{5,6},{6,7},{7,8},{8,9},{9,10... | collective-permute-start | bytes 786440 | tf_op jit(solution)/shard_map/ppermute | solution.py:13
  353.3 2.2 copy-start.8
  355.5 2.7 copy-start.9
  358.2 2.7 copy-start.11
  368.1 2.2 copy-start.7
  372.4 4.8 copy-start.2
  401.5 2.4 copy-start.6
  403.9 1.4 copy-start
  405.3 21.1 %collective-permute-start.3 = (bf16[1024,128]{1,0:T(8,128)(2,1)S(1)}, bf16[1024,128]{1,0:T(8,128)(2,1)S(1)}, u32[]{:S(2)}, u32[]{:S(2)}) collective-permute-start(bf16[1024,128]{1,0:T(8,128)(2,1)S(1)} %collective-permute-done.1), channel_id=1, source_target_pairs={{31,0},{0,1},{1,2},{2,3},{3,4},{4,5},{5,6},{6,7},{7,8},{8,9},{9,10... | collective-permute-start | bytes 786440 | tf_op jit(solution)/shard_map/ppermute | solution.py:13
  406.1 15.9 %collective-permute-start.2 = (bf16[1024,128]{1,0:T(8,128)(2,1)S(1)}, bf16[1024,128]{1,0:T(8,128)(2,1)S(1)}, u32[]{:S(2)}, u32[]{:S(2)}) collective-permute-start(bf16[1024,128]{1,0:T(8,128)(2,1)S(1)} %collective-permute-done), channel_id=1, source_target_pairs={{31,0},{0,1},{1,2},{2,3},{3,4},{4,5},{5,6},{6,7},{7,8},{8,9},{9,10... | collective-permute-start | bytes 786440 | tf_op jit(solution)/shard_map/ppermute | solution.py:13
  448.6 33.1 %collective-permute-start.4 = (f32[1024,128]{1,0:T(8,128)}, f32[1024,128]{1,0:T(8,128)S(1)}, u32[]{:S(2)}, u32[]{:S(2)}) collective-permute-start(f32[1024,128]{1,0:T(8,128)} %convolution_add_fusion.8), channel_id=1, source_target_pairs={{1,0},{2,1},{3,2},{4,3},{5,4},{6,5},{7,6},{8,7},{9,8},{10,9},{11,1... | collective-permute-start | bytes 1572872 | tf_op jit(solution)/shard_map/ppermute | solution.py:13
  449.8 20.4 %collective-permute-start.6 = (f32[1024,128]{1,0:T(8,128)}, f32[1024,128]{1,0:T(8,128)}, u32[]{:S(2)}, u32[]{:S(2)}) collective-permute-start(f32[1024,128]{1,0:T(8,128)} %fusion.97), channel_id=1, source_target_pairs={{1,0},{2,1},{3,2},{4,3},{5,4},{6,5},{7,6},{8,7},{9,8},{10,9},{11,1... | collective-permute-start | bytes 1572872 | tf_op jit(solution)/shard_map/ppermute | solution.py:13
  455.1 54.3 %all-to-all-start.1 = ((bf16[4,256,640]{2,1,0:T(8,128)(2,1)}), bf16[4,256,640]{2,1,0:T(8,128)(2,1)}, u32[]{:S(2)}, u32[]{:S(2)}) async-start(bf16[4,256,640]{2,1,0:T(8,128)(2,1)} %add_convert_fusion), calls=%async_computation.1 | async-start | bytes 2621440 | tf_op jit(solution)/shard_map/all_to_all | solution.py:107
  463.2 18.6 %copy-start.1 = (bf16[1024,1024]{1,0:T(8,128)(2,1)S(1)}, bf16[1024,1024]{1,0:T(8,128)(2,1)}, u32[]{:S(2)}) copy-start(bf16[1024,1024]{1,0:T(8,128)(2,1)} %copy-done) | copy-start | bytes 6291460
  474.9 8.4 %copy-start.3 = (bf16[1024,1024]{1,0:T(8,128)(2,1)S(1)}, bf16[1024,1024]{1,0:T(8,128)(2,1)}, u32[]{:S(2)}) copy-start(bf16[1024,1024]{1,0:T(8,128)(2,1)} %copy-done.2) | copy-start | bytes 6291460
  474.9 36.9 %collective-permute-start.7 = (f32[1024,128]{1,0:T(8,128)}, f32[1024,128]{1,0:T(8,128)}, u32[]{:S(2)}, u32[]{:S(2)}) collective-permute-start(f32[1024,128]{1,0:T(8,128)} %fusion.112), channel_id=1, source_target_pairs={{1,0},{2,1},{3,2},{4,3},{5,4},{6,5},{7,6},{8,7},{9,8},{10,9},{11,1... | collective-permute-start | bytes 1572872 | tf_op jit(solution)/shard_map/ppermute | solution.py:13
  483.3 28.5 %copy-start.13 = (f32[1024,128]{1,0:T(8,128)S(1)}, f32[1024,128]{1,0:T(8,128)}, u32[]{:S(2)}) copy-start(f32[1024,128]{1,0:T(8,128)} %fusion.109) | copy-start | bytes 1572868
  483.3 34.2 %collective-permute-start.5 = (f32[1024,128]{1,0:T(8,128)}, f32[1024,128]{1,0:T(8,128)S(1)}, u32[]{:S(2)}, u32[]{:S(2)}) collective-permute-start(f32[1024,128]{1,0:T(8,128)} %fusion.75), channel_id=1, source_target_pairs={{1,0},{2,1},{3,2},{4,3},{5,4},{6,5},{7,6},{8,7},{9,8},{10,9},{11,1... | collective-permute-start | bytes 1572872 | tf_op jit(solution)/shard_map/ppermute | solution.py:13
  513.6 9.0 %all-to-all-start.3 = ((bf16[4,256,128]{2,1,0:T(8,128)(2,1)}), bf16[4,256,128]{2,1,0:T(8,128)(2,1)S(1)}, u32[]{:S(2)}, u32[]{:S(2)}) async-start(bf16[4,256,128]{2,1,0:T(8,128)(2,1)} %bitcast.49), calls=%async_computation.3 | async-start | bytes 524288 | tf_op jit(solution)/shard_map/all_to_all | solution.py:113
  522.6 9.4 %all-to-all-start.2 = ((bf16[4,256,128]{2,1,0:T(8,128)(2,1)}), bf16[4,256,128]{2,1,0:T(8,128)(2,1)S(1)}, u32[]{:S(2)}, u32[]{:S(2)}) async-start(bf16[4,256,128]{2,1,0:T(8,128)(2,1)} %bitcast.47), calls=%async_computation.2 | async-start | bytes 524288 | tf_op jit(solution)/shard_map/all_to_all | solution.py:110
Sparse Core Ops, SparseCore 0:
  11.1 69.2 all-gather.8
  82.0 97.6 all-gather.4
  182.8 93.4 all-gather.6
  279.3 64.1 all-gather.10
where the time goes:
time: 549 us; the launch traced here: 540 us
  waiting for transfers between devices  344 us (63%)
  matrix products  130 us (24%)
  starting transfers between devices  32.6 us (6%)
  between operations  14.7 us (3%)
  local copies, waits for them, and re-layouts  11.7 us (2%)
  other arithmetic  6.32 us (1%)
    all_gather x1, waiting for transfers between devices, local(): x_group = lax.all_gather(x_ckpt, 'head', axis=0, tiled=True)  99.4 us
    all_gather x1, waiting for transfers between devices, local(): lax.all_gather(w_query, 'blk', axis=0, tiled=True)  88.1 us
    all_gather x1, waiting for transfers between devices, local(): lax.all_gather(w_key, 'blk', axis=0, tiled=True)  43.5 us
    all_gather x1, waiting for transfers between devices, local(): lax.all_gather(w_value, 'blk', axis=0, tiled=True)  40.5 us
    dot_general x15, matrix products, tile(): lax.dot_general(grad_head, value_block, contract_cols, preferred_element_...  30.4 us
    dot_general x15, matrix products, tile(): lax.dot_general(prob_half, grad_head, contract_rows, preferred_element_ty...  27.9 us
    dot_general x3, matrix products, local(): jnp.dot(x_group, piece, preferred_element_type=jnp.float32)  27.4 us
    all_to_all x1, waiting for transfers between devices, local(): lax.all_to_all(grad_q.astype(jnp.bfloat16), 'head', split_axis=0, concat_...  25.3 us
  transfers between devices with their start and end apart: 16, of which 10 were waited for; matrix products, arithmetic and copies ran while one was open for 18% of the time, Pallas kernels for 0%

commit v1 on v0

v1 whole, which is shorter than its diff:
```python
import jax
import jax.numpy as jnp
from jax import lax
from jax.experimental import pallas as pl
from jax.experimental.pallas import tpu as pltpu
from jax.sharding import Mesh, PartitionSpec as P

HD = 128
SPAN = 128
REACH = 2
HEAD = ("y_lo", "core")
BLK = ("x", "y_hi", "z")
FINE = (2, 2, 4, 2, 4)
SCALE = HD ** (-0.5)
LOG2E = 1.4426950408889634
BIG = 1e30
NN = (((1,), (0,)), ((), ()))
NT = (((1,), (1,)), ((), ()))


def dot(a, b, dims):
    return lax.dot_general(a, b, dims, preferred_element_type=jnp.float32)


def tile_grads(query, grad_out, lse2, delta, query_spans, key_spans, kvs, own, key_rows, query_rows):
    rows, cols = query.shape
    heads = cols // HD
    n = len(kvs)
    length = kvs[0].shape[0]
    query_rows = min(query_rows, rows)

    def body(qspan_ref, kspan_ref, q_ref, g_ref, lse_ref, delta_ref, *rest):
        kv_refs, dq_ref, dkv_refs, kt_ref = rest[:n], rest[n], rest[n + 1 : 2 * n + 1], rest[2 * n + 1]

        @pl.when(pl.program_id(0) == 0)
        def _():
            for i in range(n):
                dkv_refs[i][...] = jnp.zeros_like(dkv_refs[i])
                kt_ref[i] = kv_refs[i][:, :HD].T

        lane = lax.broadcasted_iota(jnp.int32, (1, query_rows), 1)
        spans = query_rows // SPAN
        for qb in range(rows // query_rows):
            qs = pl.ds(qb * query_rows, query_rows)
            q, g = q_ref[qs, :], g_ref[qs, :]
            lse, delt = lse_ref[0, :, qs], delta_ref[0, :, qs]
            qspan = jnp.full((1, query_rows), qspan_ref[qb * spans], jnp.int32)
            for s in range(1, spans):
                qspan = jnp.where(lane >= s * SPAN, qspan_ref[qb * spans + s], qspan)
            qpos = qspan * SPAN + lane % SPAN
            dq = None
            for i in range(n):
                for kb in range(length // key_rows):
                    ks = pl.ds(kb * key_rows, key_rows)
                    score = dot(kv_refs[i][ks, :HD], q, NT)
                    gprob = dot(kv_refs[i][ks, HD:], g, NT)
                    probs, scores = [], []
                    for s in range(key_rows // SPAN):
                        at = slice(s * SPAN, (s + 1) * SPAN)
                        kspan = kspan_ref[i, kb * (key_rows // SPAN) + s]
                        if i == own:
                            kpos = kspan * SPAN + lax.broadcasted_iota(jnp.int32, (SPAN, 1), 0)
                            prob = jnp.exp2(
                                jnp.where(kpos <= qpos, score[at] * (SCALE * LOG2E) - lse, -BIG)
                            )
                        else:
                            prob = jnp.exp2(
                                score[at] * (SCALE * LOG2E) - jnp.where(kspan < qspan, lse, BIG)
                            )
                        probs.append(prob.astype(jnp.bfloat16))
                        scores.append((prob * (gprob[at] - delt)).astype(jnp.bfloat16))
                    prob_half = jnp.concatenate(probs, 0)
                    score_half = jnp.concatenate(scores, 0)
                    dkv_refs[i][ks, HD:] += dot(prob_half, g, NN)
                    dkv_refs[i][ks, :HD] += dot(score_half, q, NN) * SCALE
                    part = dot(kt_ref[i, :, ks], score_half, NN)
                    dq = part if dq is None else dq + part
            dq_ref[qs, :] = dq.T * SCALE

    def whole(shape):
        return pl.BlockSpec(shape, lambda h: (0,) * len(shape))

    smem = pl.BlockSpec(memory_space=pltpu.SMEM)
    per_head = pl.BlockSpec((rows, HD), lambda h: (0, h))
    per_row = pl.BlockSpec((1, 1, rows), lambda h: (h, 0, 0))
    return pl.pallas_call(
        body,
        grid=(heads,),
        in_specs=[smem, smem, per_head, per_head, per_row, per_row] + [whole((length, 2 * HD))] * n,
        out_specs=[per_head] + [whole((length, 2 * HD))] * n,
        out_shape=[jax.ShapeDtypeStruct((rows, cols), jnp.float32)]
        + [jax.ShapeDtypeStruct((length, 2 * HD), jnp.float32)] * n,
        scratch_shapes=[pltpu.VMEM((n, HD, length), jnp.bfloat16)],
        compiler_params=pltpu.CompilerParams(
            vmem_limit_bytes=48 * 2**20, dimension_semantics=("arbitrary",)
        ),
        cost_estimate=pl.CostEstimate(
            flops=10 * rows * length * n * cols,
            bytes_accessed=n * length * HD * 12 + rows * cols * 8,
            transcendentals=rows * length * n * heads,
        ),
    )(query_spans, key_spans, query, grad_out, lse2, delta, *kvs)


def shift(block, axis, by):
    size = lax.axis_size(axis)
    return lax.ppermute(block, axis, [(i, (i + by) % size) for i in range(size)])


def to_peer(block, d):
    return lax.ppermute(block, HEAD, [(i, i ^ d) for i in range(4)]) if d else block


def local(x_ckpt, w_query, w_key, w_value, dout_seq, out_heads, lse_heads, span_order):
    rows = x_ckpt.shape[0]
    cols = w_query.shape[1]
    heads = cols // HD
    me = lax.axis_index(HEAD)
    group = lax.axis_index(BLK)
    groups = lax.axis_size(BLK)
    peers = range(4)
    mine = [me ^ d for d in peers]

    w_own = jnp.concatenate([w_key, w_value, w_query], axis=1)
    w_all = lax.all_gather(w_own, BLK, axis=0, tiled=True)

    x_pair = to_peer(x_ckpt, 2)
    x_rows = jnp.concatenate([x_ckpt, to_peer(x_ckpt, 1), x_pair, to_peer(x_pair, 1)], axis=0)

    grad_out = jnp.concatenate(
        [
            to_peer(lax.dynamic_slice_in_dim(dout_seq, mine[d] * cols, cols, 1), d)
            for d in peers
        ],
        axis=0,
    )

    def by_peer(array):
        return jnp.concatenate(
            [lax.dynamic_slice_in_dim(array, mine[d] * rows, rows, 0) for d in peers], axis=0
        )

    lse2 = (by_peer(lse_heads) * LOG2E).T[:, None, :]
    delta = jnp.sum(
        (grad_out.astype(jnp.float32) * by_peer(out_heads).astype(jnp.float32)).reshape(
            4 * rows, heads, HD
        ),
        axis=2,
    ).T[:, None, :]

    spans = rows // SPAN

    def spans_of(which):
        base = which * (4 * spans)
        return jnp.concatenate(
            [lax.dynamic_slice_in_dim(span_order, base + mine[d] * spans, spans) for d in peers]
        )

    span_ids = [spans_of((group - r) % groups) for r in range(REACH + 1)]

    kv = dot(x_rows, w_all[:, : 2 * HD], NN).astype(jnp.bfloat16)
    query = dot(x_rows, w_all[:, 2 * HD :], NN).astype(jnp.bfloat16)

    kv1, kv2 = shift(kv, BLK, 1), shift(kv, BLK, 2)
    far = slice(2 * rows, None)
    near = slice(0, 2 * rows)

    def part(at, kvs, ids, own):
        spans_at = slice(at.start // SPAN, None if at.stop is None else at.stop // SPAN)
        return tile_grads(
            query[at], grad_out[at], lse2[:, :, at], delta[:, :, at],
            span_ids[0][spans_at], jnp.stack(ids), kvs, own, 1024, 256,
        )

    dq_far0, dkv0_far = part(far, [kv], [span_ids[0]], 0)
    dq_far1, dkv1_far, dkv2_far = part(far, [kv1, kv2], span_ids[1:], -1)
    dq_far = (dq_far0 + dq_far1).astype(jnp.bfloat16)
    dq2, dq3 = to_peer(dq_far[:rows], 2), to_peer(dq_far[rows:], 3)
    dq_near1, dkv1_near, dkv2_near = part(near, [kv1, kv2], span_ids[1:], -1)
    back1 = shift((dkv1_far + dkv1_near).astype(jnp.bfloat16), BLK, -1)
    back2 = shift((dkv2_far + dkv2_near).astype(jnp.bfloat16), BLK, -2)
    dq_near0, dkv0_near = part(near, [kv], [span_ids[0]], 0)
    dq_near = (dq_near0 + dq_near1).astype(jnp.bfloat16)
    dq1 = to_peer(dq_near[rows:], 1)
    dkv = (
        dkv0_far + dkv0_near + back1.astype(jnp.float32) + back2.astype(jnp.float32)
    ).astype(jnp.bfloat16)
    dkvs = [to_peer(dkv[d * rows : (d + 1) * rows], d) for d in peers]
    dqs = [dq_near[:rows], dq1, dq2, dq3]

    def by_head(pieces):
        width = pieces[0].shape[1]
        out = jnp.zeros((rows, 4 * width), jnp.bfloat16)
        for d in peers:
            out = lax.dynamic_update_slice_in_dim(out, pieces[d], mine[d] * width, 1)
        return out

    return (
        by_head(dqs),
        by_head([piece[:, :HD] for piece in dkvs]),
        by_head([piece[:, HD:] for piece in dkvs]),
    )


def solution(mesh):
    fine = Mesh(mesh.devices.reshape(FINE), HEAD + BLK)
    rows = P(BLK + HEAD, None)
    both = P(BLK, HEAD)
    return jax.shard_map(
        local,
        mesh=fine,
        in_specs=(rows, both, both, both, rows, both, both, P()),
        out_specs=(rows, rows, rows),
        check_vma=False,
    )
```

time: 549 us -> 278 us (0.51)
  waiting for transfers between devices: 344 us -> 119 us
  matrix products: 130 us -> 16 us
  Pallas kernels: 0 us -> 48.2 us
  local copies, waits for them, and re-layouts: 11.7 us -> 35.9 us
    all_gather x4 -> x1, waiting for transfers between devices: 271 us -> 27.7 us  [local(): w_all = lax.all_gather(w_own, BLK, axis=0, tiled=True)]
    dot_general x78 -> x2, matrix products: 130 us -> 16 us  [dot(): return lax.dot_general(a, b, dims, preferred_element_type=jnp.float32)]
    ppermute x8 -> x16, waiting for transfers between devices: 21.6 us -> 91.4 us  [the longest x12 91.3 us: to_peer(): lax.ppermute(block, HEAD, [(i, i ^ d) for i in range(4)])]
    all_to_all x4 -> x0, waiting for transfers between devices: 48.5 us -> none  [the longest x1 25.3 us: local(): lax.all_to_all(grad_q.astype(jnp.bfloat16), 'head', split_axis=0, concat_...]
    pallas_call x0 -> x4, Pallas kernels: none -> 48.2 us  [tile_grads(): pl.pallas_call(body, grid=(heads,), in_specs=[smem, smem, per_head, per_h...]
    all_to_all x4 -> x0, starting transfers between devices: 21.1 us -> none  [the longest x1 8.07 us: local(): lax.all_to_all(grad_q.astype(jnp.bfloat16), 'head', split_axis=0, concat_...]
    ppermute x8 -> x16, starting transfers between devices: 11.4 us -> 30 us  [the longest x4 16.6 us: shift(): lax.ppermute(block, axis, [(i, (i + by) % size) for i in range(size)])]
    unnamed x46 -> x30, local copies, waits for them, and re-layouts: 7.48 us -> 17.9 us
  transfers between devices with their start and end apart: 16 -> 17, of which waited for: 10 -> 8; matrix products, arithmetic and copies ran while one was open for 18% -> 17% of each run, Pallas kernels for 0% -> 12%
where the time goes in v1:
time: 278 us; the launch traced here: 272 us
  waiting for transfers between devices  119 us (43%)
  Pallas kernels  48.2 us (17%)
  local copies, waits for them, and re-layouts  35.9 us (13%)
  starting transfers between devices  30.1 us (11%)
  matrix products  16 us (6%)
  between operations  14.4 us (5%)
  other arithmetic  8.76 us (3%)
    ppermute x12, waiting for transfers between devices, to_peer(): lax.ppermute(block, HEAD, [(i, i ^ d) for i in range(4)])  91.3 us
    pallas_call x4, Pallas kernels, tile_grads(): pl.pallas_call(body, grid=(heads,), in_specs=[smem, smem, per_head, per_h...  48.2 us
    all_gather x1, waiting for transfers between devices, local(): w_all = lax.all_gather(w_own, BLK, axis=0, tiled=True)  27.7 us
    unnamed x30, local copies, waits for them, and re-layouts  17.9 us
    ppermute x4, starting transfers between devices, shift(): lax.ppermute(block, axis, [(i, (i + by) % size) for i in range(size)])  16.6 us
    dot_general x2, matrix products, dot(): return lax.dot_general(a, b, dims, preferred_element_type=jnp.float32)  16 us
    ppermute x12, starting transfers between devices, to_peer(): lax.ppermute(block, HEAD, [(i, i ^ d) for i in range(4)])  13.4 us
  transfers between devices with their start and end apart: 17, of which 8 were waited for; matrix products, arithmetic and copies ran while one was open for 17% of the time, Pallas kernels for 12%

profile of v1, /device:TPU:1, one launch (start us, length us, event | category | flops | bytes accessed | tf_op | source)
XLA Modules:
  0.0 272.4 jit_solution(13661690843473859986)
XLA Ops:
  7.2 1.7 pad_maximum_fusion.1
  8.9 2.2 collective-permute-start.1
  11.1 1.0 collective-permute-start
  12.1 2.2 constant_dynamic-slice_fusion.5
  14.8 1.4 collective-permute-start.4
  16.3 0.9 copy.11
  17.2 2.6 constant_dynamic-slice_fusion.3
  19.7 1.9 copy.22
  21.6 1.9 copy.21
  23.5 1.9 copy.20
  25.4 1.9 copy.19
  27.5 1.6 constant_dynamic-update-slice_fusion.3
  29.2 48.7 %collective-permute-done.1 = bf16[256,5120]{1,0:T(8,128)(2,1)} collective-permute-done((bf16[256,5120]{1,0:T(8,128)(2,1)}, bf16[256,5120]{1,0:T(8,128)(2,1)}, u32[]{:S(2)}, u32[]{:S(2)}) %collective-permute-start.1) | collective-permute-done | bytes 2621472 | tf_op jit(solution)/shard_map/ppermute | solution.py:111
  77.9 2.9 %collective-permute-start.2 = (bf16[256,5120]{1,0:T(8,128)(2,1)}, bf16[256,5120]{1,0:T(8,128)(2,1)}, u32[]{:S(2)}, u32[]{:S(2)}) collective-permute-start(bf16[256,5120]{1,0:T(8,128)(2,1)} %collective-permute-done.1), channel_id=1, source_target_pairs={{0,32},{32,0},{64,96},{96,64},{1,33},{33,1},{65,97},{97,65},{2,34}... | collective-permute-start | bytes 7864328 | tf_op jit(solution)/shard_map/ppermute | solution.py:111
  81.0 7.0 %collective-permute-done.5 = bf16[256,640]{1,0:T(8,128)(2,1)} collective-permute-done((bf16[256,640]{1,0:T(8,128)(2,1)}, bf16[256,640]{1,0:T(8,128)(2,1)}, u32[]{:S(2)}, u32[]{:S(2)}) %collective-permute-start.5) | collective-permute-done | bytes 327712 | tf_op jit(solution)/shard_map/ppermute | solution.py:111
  88.0 1.1 copy.14
  89.2 8.8 %collective-permute-done.4 = bf16[256,640]{1,0:T(8,128)(2,1)} collective-permute-done((bf16[256,640]{1,0:T(8,128)(2,1)}, bf16[256,640]{1,0:T(8,128)(2,1)}, u32[]{:S(2)}, u32[]{:S(2)}) %collective-permute-start.4) | collective-permute-done | bytes 327712 | tf_op jit(solution)/shard_map/ppermute | solution.py:111
  98.0 1.1 copy.13
  99.3 1.7 multiply_reduce_fusion
  101.1 1.0 constant_dynamic-update-slice_fusion.5
  102.1 1.0 constant_dynamic-update-slice_fusion.4.g_ref
  103.1 1.0 pad_maximum_fusion.g_ref
  104.2 3.5 %constant_dynamic-update-slice_fusion.2 = bf16[1024,5120]{1,0:T(8,128)(2,1)} fusion(bf16[1024,5120]{1,0:T(8,128)(2,1)} %constant_dynamic-update-slice_fusion.3, bf16[256,5120]{1,0:T(8,128)(2,1)} %collective-permute-done), kind=kLoop, calls=%fused_computation.27 | loop fusion | bytes 5242880
  107.7 3.4 %constant_dynamic-update-slice_fusion.1 = bf16[1024,5120]{1,0:T(8,128)(2,1)} fusion(bf16[1024,5120]{1,0:T(8,128)(2,1)} %constant_dynamic-update-slice_fusion.2, bf16[256,5120]{1,0:T(8,128)(2,1)} %collective-permute-done.1), kind=kLoop, calls=%fused_computation.26 | loop fusion | bytes 5242880
  111.1 3.5 %constant_dynamic-update-slice_fusion = bf16[1024,5120]{1,0:T(8,128)(2,1)} fusion(bf16[1024,5120]{1,0:T(8,128)(2,1)} %constant_dynamic-update-slice_fusion.1, bf16[256,5120]{1,0:T(8,128)(2,1)} %collective-permute-done.2), kind=kLoop, calls=%fused_computation.25 | loop fusion | bytes 5242880 | tf_op jit(solution)/shard_map/concatenate | solution.py:128
  114.5 27.7 %all-gather.2.cloned.1.call-done = bf16[5120,896]{1,0:T(8,128)(2,1)} async-done(((bf16[160,896]{1,0:T(8,128)(2,1)}), bf16[5120,896]{1,0:T(8,128)(2,1)}) %all-gather.2.cloned.1.call-update) | async-done | bytes 9175056 | tf_op jit(solution)/shard_map/all_gather | solution.py:125
  142.3 7.7 %fusion.7.rest_0_ = bf16[1024,256]{1,0:T(8,128)(2,1)S(1)} fusion(bf16[1024,5120]{1,0:T(8,128)(2,1)} %constant_dynamic-update-slice_fusion, bf16[5120,896]{1,0:T(8,128)(2,1)} %all-gather.2.cloned.1.call-done), kind=kOutput, calls=%fused_computation.8 | convolution fusion | flops 2684616704 | bytes 13631488 | tf_op jit(solution)/shard_map/dot_general | solution.py:22
  150.4 3.3 %collective-permute-start.7 = (bf16[1024,256]{1,0:T(8,128)(2,1)S(1)}, bf16[1024,256]{1,0:T(8,128)(2,1)S(1)}, u32[]{:S(2)}, u32[]{:S(2)}) collective-permute-start(bf16[1024,256]{1,0:T(8,128)(2,1)S(1)} %fusion.7.rest_0_), channel_id=1, source_target_pairs={{0,2},{1,3},{2,4},{3,5},{4,6},{5,7},{6,8},{7,9},{8,10},{9,11},{10,... | collective-permute-start | bytes 1572872 | tf_op jit(solution)/shard_map/ppermute | solution.py:107
  153.7 8.3 %fusion.4 = bf16[1024,640]{1,0:T(8,128)(2,1)S(1)} fusion(bf16[1024,5120]{1,0:T(8,128)(2,1)S(1)} %copy-done.5, bf16[5120,896]{1,0:T(8,128)(2,1)S(1)} %copy-done.10), kind=kOutput, calls=%fused_computation.5 | convolution fusion | flops 6711541760 | bytes 18350080 | tf_op jit(solution)/shard_map/dot_general | solution.py:22
  162.1 8.9 %shard_map.103 = (f32[512,640]{1,0:T(8,128)S(1)}, f32[1024,256]{1,0:T(8,128)S(1)}) custom-call(s32[4]{0:T(128)S(1)} %pad_add_fusion.1.qspan_ref, s32[1,8]{1,0:T(1,128)S(1)} %add_bitcast_fusion.kspan_ref, bf16[512,640]{1,0:T(8,128)(2,1)S(1)} %get-tuple-element.24.q_ref, bf16[512,640]{1,0:T(8,128)(2,1)S(1)} %pad_maximum_fusion.g_ref, ...), custom_call_target="tpu_custom_call" | custom-call | flops 3355443200 | bytes 4194304 | tf_op jit(solution)/shard_map/pallas_call | solution.py:86
  171.0 8.7 %shard_map.105 = (f32[512,640]{1,0:T(8,128)S(1)}, f32[1024,256]{1,0:T(8,128)S(1)}) custom-call(s32[4]{0:T(128)S(1)} %pad_add_fusion.2.qspan_ref, s32[1,8]{1,0:T(1,128)S(1)} %add_bitcast_fusion.kspan_ref, bf16[512,640]{1,0:T(8,128)(2,1)S(1)} %get-tuple-element.23.q_ref, bf16[512,640]{1,0:T(8,128)(2,1)S(1)} %constant_dynamic-update-slice_fusion.4.g_ref, ...), custom_call_target="tpu_custom_call" | custom-call | flops 3355443200 | bytes 4194304 | tf_op jit(solution)/shard_map/pallas_call | solution.py:86
  179.7 15.3 %shard_map.104 = (f32[512,640]{1,0:T(8,128)S(1)}, f32[1024,256]{1,0:T(8,128)S(1)}, f32[1024,256]{1,0:T(8,128)S(1)}) custom-call(s32[4]{0:T(128)S(1)} %pad_add_fusion.1.qspan_ref, s32[2,8]{1,0:T(2,128)S(1)} %pad_add_fusion.kspan_ref, bf16[512,640]{1,0:T(8,128)(2,1)S(1)} %get-tuple-element.24.q_ref, bf16[512,640]{1,0:T(8,128)(2,1)S(1)} %pad_maximum_fusion.g_ref, ...), custom_call_target="tpu_custom_call" | custom-call | flops 6710886400 | bytes 5767168 | tf_op jit(solution)/shard_map/pallas_call | solution.py:86
  196.1 1.7 collective-permute-start.8
  197.7 15.3 %shard_map.106 = (f32[512,640]{1,0:T(8,128)S(1)}, f32[1024,256]{1,0:T(8,128)S(1)}, f32[1024,256]{1,0:T(8,128)S(1)}) custom-call(s32[4]{0:T(128)S(1)} %pad_add_fusion.2.qspan_ref, s32[2,8]{1,0:T(2,128)S(1)} %pad_add_fusion.kspan_ref, bf16[512,640]{1,0:T(8,128)(2,1)S(1)} %get-tuple-element.23.q_ref, ...), custom_call_target="tpu_custom_call" | custom-call | flops 6710886400 | bytes 5767168 | tf_op jit(solution)/shard_map/pallas_call | solution.py:86
  214.1 0.9 add_convert_fusion.3
  215.1 4.4 %collective-permute-start.12 = (bf16[1024,256]{1,0:T(8,128)(2,1)}, bf16[1024,256]{1,0:T(8,128)(2,1)}, u32[]{:S(2)}, u32[]{:S(2)}) collective-permute-start(bf16[1024,256]{1,0:T(8,128)(2,1)} %add_convert_fusion.3), channel_id=1, source_target_pairs={{0,30},{1,31},{2,0},{3,1},{4,2},{5,3},{6,4},{7,5},{8,6},{9,7},{10,... | collective-permute-start | bytes 1572872 | tf_op jit(solution)/shard_map/ppermute | solution.py:107
  219.4 0.9 add_convert_fusion.4
  220.3 8.6 %collective-permute-start.11 = (bf16[1024,256]{1,0:T(8,128)(2,1)}, bf16[1024,256]{1,0:T(8,128)(2,1)}, u32[]{:S(2)}, u32[]{:S(2)}) collective-permute-start(bf16[1024,256]{1,0:T(8,128)(2,1)} %add_convert_fusion.4), channel_id=1, source_target_pairs={{0,31},{1,0},{2,1},{3,2},{4,3},{5,4},{6,5},{7,6},{8,7},{9,8},{10,9... | collective-permute-start | bytes 1572872 | tf_op jit(solution)/shard_map/ppermute | solution.py:107
  228.9 1.6 collective-permute-start.10
  230.5 1.0 constant_dynamic-update-slice_fusion.8
  231.6 10.2 %collective-permute-done.9 = bf16[256,640]{1,0:T(8,128)(2,1)} collective-permute-done((bf16[256,640]{1,0:T(8,128)(2,1)}, bf16[256,640]{1,0:T(8,128)(2,1)}, u32[]{:S(2)}, u32[]{:S(2)}) %collective-permute-start.9) | collective-permute-done | bytes 327712 | tf_op jit(solution)/shard_map/ppermute | solution.py:111
  241.7 1.0 constant_dynamic-update-slice_fusion.7
  242.8 10.6 %collective-permute-done.10 = bf16[256,640]{1,0:T(8,128)(2,1)} collective-permute-done((bf16[256,640]{1,0:T(8,128)(2,1)}, bf16[256,640]{1,0:T(8,128)(2,1)}, u32[]{:S(2)}, u32[]{:S(2)}) %collective-permute-start.10) | collective-permute-done | bytes 327712 | tf_op jit(solution)/shard_map/ppermute | solution.py:111
  253.4 1.0 constant_dynamic-update-slice_fusion.6
  254.4 1.9 add_convert_fusion.2
  256.8 1.8 collective-permute-start.15
  258.7 2.8 %collective-permute-done.14 = bf16[256,256]{1,0:T(8,128)(2,1)S(1)} collective-permute-done((bf16[256,256]{1,0:T(8,128)(2,1)S(1)}, bf16[256,256]{1,0:T(8,128)(2,1)S(1)}, u32[]{:S(2)}, u32[]{:S(2)}) %collective-permute-start.14) | collective-permute-done | bytes 131104 | tf_op jit(solution)/shard_map/ppermute | solution.py:111
  261.6 3.1 %collective-permute-done.15 = bf16[256,256]{1,0:T(8,128)(2,1)S(1)} collective-permute-done((bf16[256,256]{1,0:T(8,128)(2,1)S(1)}, bf16[256,256]{1,0:T(8,128)(2,1)S(1)}, u32[]{:S(2)}, u32[]{:S(2)}) %collective-permute-start.15) | collective-permute-done | bytes 131104 | tf_op jit(solution)/shard_map/ppermute | solution.py:111
  (66 shorter events, 5.2 us)
Async XLA Ops:
  7.2 9.0 %copy-start.9 = (f32[1024,5]{0,1:T(8,128)S(1)}, f32[1024,5]{0,1:T(8,128)}, u32[]{:S(2)}) copy-start(f32[1024,5]{0,1:T(8,128)} %param.14) | copy-start | bytes 61444
  7.2 135.1 %all-gather.2.cloned.1.call-start = ((), (), s32[]{:S(2)}) async-start(), calls=%async_computation | async-start | bytes 9461760 | tf_op jit(solution)/shard_map/all_gather | solution.py:125
  8.9 69.0 %collective-permute-start.1 = (bf16[256,5120]{1,0:T(8,128)(2,1)}, bf16[256,5120]{1,0:T(8,128)(2,1)}, u32[]{:S(2)}, u32[]{:S(2)}) collective-permute-start(bf16[256,5120]{1,0:T(8,128)(2,1)} %param.8), channel_id=1, source_target_pairs={{0,64},{32,96},{64,0},{96,32},{1,65},{33,97},{65,1},{97,33},{2,66}... | collective-permute-start | bytes 7864328 | tf_op jit(solution)/shard_map/ppermute | solution.py:111
  11.1 93.0 %collective-permute-start = (bf16[256,5120]{1,0:T(8,128)(2,1)}, bf16[256,5120]{1,0:T(8,128)(2,1)}, u32[]{:S(2)}, u32[]{:S(2)}) collective-permute-start(bf16[256,5120]{1,0:T(8,128)(2,1)} %param.8), channel_id=1, source_target_pairs={{0,32},{32,0},{64,96},{96,64},{1,33},{33,1},{65,97},{97,65},{2,34}... | collective-permute-start | bytes 7864328 | tf_op jit(solution)/shard_map/ppermute | solution.py:111
  14.3 84.8 %collective-permute-start.3 = (bf16[256,640]{1,0:T(8,128)(2,1)}, bf16[256,640]{1,0:T(8,128)(2,1)S(1)}, u32[]{:S(2)}, u32[]{:S(2)}) collective-permute-start(bf16[256,640]{1,0:T(8,128)(2,1)} %get-tuple-element.30), channel_id=1, source_target_pairs={{0,32},{32,0},{64,96},{96,64},{1,33},{33,1},{65,97},{97,65},{2,34}... | collective-permute-start | bytes 983048 | tf_op jit(solution)/shard_map/ppermute | solution.py:111
  14.3 73.7 %collective-permute-start.5 = (bf16[256,640]{1,0:T(8,128)(2,1)}, bf16[256,640]{1,0:T(8,128)(2,1)}, u32[]{:S(2)}, u32[]{:S(2)}) collective-permute-start(bf16[256,640]{1,0:T(8,128)(2,1)} %get-tuple-element.32), channel_id=1, source_target_pairs={{0,96},{32,64},{64,32},{96,0},{1,97},{33,65},{65,33},{97,1},{2,98}... | collective-permute-start | bytes 983048 | tf_op jit(solution)/shard_map/ppermute | solution.py:111
  14.8 83.1 %collective-permute-start.4 = (bf16[256,640]{1,0:T(8,128)(2,1)}, bf16[256,640]{1,0:T(8,128)(2,1)}, u32[]{:S(2)}, u32[]{:S(2)}) collective-permute-start(bf16[256,640]{1,0:T(8,128)(2,1)} %get-tuple-element.29), channel_id=1, source_target_pairs={{0,64},{32,96},{64,0},{96,32},{1,65},{33,97},{65,1},{97,33},{2,66}... | collective-permute-start | bytes 983048 | tf_op jit(solution)/shard_map/ppermute | solution.py:111
  17.2 10.1 %copy-start.8 = (s32[256]{0:T(256)S(1)}, s32[256]{0:T(256)}, u32[]{:S(2)}) copy-start(s32[256]{0:T(256)} %param.15) | copy-start | bytes 3076
  17.2 10.4 %copy-start = (bf16[256,5120]{1,0:T(8,128)(2,1)S(1)}, bf16[256,5120]{1,0:T(8,128)(2,1)}, u32[]{:S(2)}) copy-start(bf16[256,5120]{1,0:T(8,128)(2,1)} %param.8) | copy-start | bytes 7864324
  77.9 33.1 %collective-permute-start.2 = (bf16[256,5120]{1,0:T(8,128)(2,1)}, bf16[256,5120]{1,0:T(8,128)(2,1)}, u32[]{:S(2)}, u32[]{:S(2)}) collective-permute-start(bf16[256,5120]{1,0:T(8,128)(2,1)} %collective-permute-done.1), channel_id=1, source_target_pairs={{0,32},{32,0},{64,96},{96,64},{1,33},{33,1},{65,97},{97,65},{2,34}... | collective-permute-start | bytes 7864328 | tf_op jit(solution)/shard_map/ppermute | solution.py:111
  99.1 1.9 copy-start.1
  142.3 11.4 %copy-start.5 = (bf16[1024,5120]{1,0:T(8,128)(2,1)S(1)}, bf16[1024,5120]{1,0:T(8,128)(2,1)}, u32[]{:S(2)}) copy-start(bf16[1024,5120]{1,0:T(8,128)(2,1)} %constant_dynamic-update-slice_fusion) | copy-start | bytes 31457284
  142.3 11.4 %copy-start.10 = (bf16[5120,896]{1,0:T(8,128)(2,1)S(1)}, bf16[5120,896]{1,0:T(8,128)(2,1)}, u32[]{:S(2)}) copy-start(bf16[5120,896]{1,0:T(8,128)(2,1)} %all-gather.2.cloned.1.call-done) | copy-start | bytes 27525124
  150.0 29.7 %collective-permute-start.6 = (bf16[1024,256]{1,0:T(8,128)(2,1)S(1)}, bf16[1024,256]{1,0:T(8,128)(2,1)S(1)}, u32[]{:S(2)}, u32[]{:S(2)}) collective-permute-start(bf16[1024,256]{1,0:T(8,128)(2,1)S(1)} %fusion.7.rest_0_), channel_id=1, source_target_pairs={{0,1},{1,2},{2,3},{3,4},{4,5},{5,6},{6,7},{7,8},{8,9},{9,10},{10,1... | collective-permute-start | bytes 1572872 | tf_op jit(solution)/shard_map/ppermute | solution.py:107
  150.4 29.3 %collective-permute-start.7 = (bf16[1024,256]{1,0:T(8,128)(2,1)S(1)}, bf16[1024,256]{1,0:T(8,128)(2,1)S(1)}, u32[]{:S(2)}, u32[]{:S(2)}) collective-permute-start(bf16[1024,256]{1,0:T(8,128)(2,1)S(1)} %fusion.7.rest_0_), channel_id=1, source_target_pairs={{0,2},{1,3},{2,4},{3,5},{4,6},{5,7},{6,8},{7,9},{8,10},{9,11},{10,... | collective-permute-start | bytes 1572872 | tf_op jit(solution)/shard_map/ppermute | solution.py:107
  196.1 17.0 %copy-start.2 = (bf16[256,2560]{1,0:T(8,128)(2,1)}, bf16[256,2560]{1,0:T(8,128)(2,1)S(1)}, u32[]{:S(2)}) copy-start(bf16[256,2560]{1,0:T(8,128)(2,1)S(1)} %get-tuple-element.36) | copy-start | bytes 3932164
  196.1 34.5 %collective-permute-start.8 = (bf16[256,640]{1,0:T(8,128)(2,1)}, bf16[256,640]{1,0:T(8,128)(2,1)}, u32[]{:S(2)}, u32[]{:S(2)}) collective-permute-start(bf16[256,640]{1,0:T(8,128)(2,1)} %get-tuple-element.35), channel_id=1, source_target_pairs={{0,32},{32,0},{64,96},{96,64},{1,33},{33,1},{65,97},{97,65},{2,34}... | collective-permute-start | bytes 983048 | tf_op jit(solution)/shard_map/ppermute | solution.py:111
  214.1 27.6 %collective-permute-start.9 = (bf16[256,640]{1,0:T(8,128)(2,1)}, bf16[256,640]{1,0:T(8,128)(2,1)}, u32[]{:S(2)}, u32[]{:S(2)}) collective-permute-start(bf16[256,640]{1,0:T(8,128)(2,1)} %get-tuple-element.34), channel_id=1, source_target_pairs={{0,64},{32,96},{64,0},{96,32},{1,65},{33,97},{65,1},{97,33},{2,66}... | collective-permute-start | bytes 983048 | tf_op jit(solution)/shard_map/ppermute | solution.py:111
  214.1 16.4 %copy-start.3 = (bf16[256,2560]{1,0:T(8,128)(2,1)S(1)}, bf16[256,2560]{1,0:T(8,128)(2,1)}, u32[]{:S(2)}) copy-start(bf16[256,2560]{1,0:T(8,128)(2,1)} %copy-done.2) | copy-start | bytes 3932164
  215.1 39.3 %collective-permute-start.12 = (bf16[1024,256]{1,0:T(8,128)(2,1)}, bf16[1024,256]{1,0:T(8,128)(2,1)}, u32[]{:S(2)}, u32[]{:S(2)}) collective-permute-start(bf16[1024,256]{1,0:T(8,128)(2,1)} %add_convert_fusion.3), channel_id=1, source_target_pairs={{0,30},{1,31},{2,0},{3,1},{4,2},{5,3},{6,4},{7,5},{8,6},{9,7},{10,... | collective-permute-start | bytes 1572872 | tf_op jit(solution)/shard_map/ppermute | solution.py:107
  220.3 34.1 %collective-permute-start.11 = (bf16[1024,256]{1,0:T(8,128)(2,1)}, bf16[1024,256]{1,0:T(8,128)(2,1)}, u32[]{:S(2)}, u32[]{:S(2)}) collective-permute-start(bf16[1024,256]{1,0:T(8,128)(2,1)} %add_convert_fusion.4), channel_id=1, source_target_pairs={{0,31},{1,0},{2,1},{3,2},{4,3},{5,4},{6,5},{7,6},{8,7},{9,8},{10,9... | collective-permute-start | bytes 1572872 | tf_op jit(solution)/shard_map/ppermute | solution.py:107
  228.9 24.4 %collective-permute-start.10 = (bf16[256,640]{1,0:T(8,128)(2,1)}, bf16[256,640]{1,0:T(8,128)(2,1)}, u32[]{:S(2)}, u32[]{:S(2)}) collective-permute-start(bf16[256,640]{1,0:T(8,128)(2,1)} %get-tuple-element.33), channel_id=1, source_target_pairs={{0,96},{32,64},{64,32},{96,0},{1,97},{33,65},{65,33},{97,1},{2,98}... | collective-permute-start | bytes 983048 | tf_op jit(solution)/shard_map/ppermute | solution.py:111
  254.4 4.3 %copy-start.4 = (bf16[256,2560]{1,0:T(8,128)(2,1)}, bf16[256,2560]{1,0:T(8,128)(2,1)S(1)}, u32[]{:S(2)}) copy-start(bf16[256,2560]{1,0:T(8,128)(2,1)S(1)} %constant_dynamic-update-slice_fusion.6) | copy-start | bytes 3932164
  256.3 2.4 collective-permute-start.13
  256.7 4.9 %collective-permute-start.14 = (bf16[256,256]{1,0:T(8,128)(2,1)S(1)}, bf16[256,256]{1,0:T(8,128)(2,1)S(1)}, u32[]{:S(2)}, u32[]{:S(2)}) collective-permute-start(bf16[256,256]{1,0:T(8,128)(2,1)S(1)} %get-tuple-element.38), channel_id=1, source_target_pairs={{0,64},{32,96},{64,0},{96,32},{1,65},{33,97},{65,1},{97,33},{2,66}... | collective-permute-start | bytes 393224 | tf_op jit(solution)/shard_map/ppermute | solution.py:111
  256.8 8.0 %collective-permute-start.15 = (bf16[256,256]{1,0:T(8,128)(2,1)S(1)}, bf16[256,256]{1,0:T(8,128)(2,1)S(1)}, u32[]{:S(2)}, u32[]{:S(2)}) collective-permute-start(bf16[256,256]{1,0:T(8,128)(2,1)S(1)} %get-tuple-element.37), channel_id=1, source_target_pairs={{0,96},{32,64},{64,32},{96,0},{1,97},{33,65},{65,33},{97,1},{2,98}... | collective-permute-start | bytes 393224 | tf_op jit(solution)/shard_map/ppermute | solution.py:111
  264.8 0.7 copy-start.6
  264.8 0.8 copy-start.7
Sparse Core Ops, SparseCore 0:
  11.1 131.1 all-gather.1

commit v2 on v1

v2 whole, which is shorter than its diff:
```python
import jax
import jax.numpy as jnp
from jax import lax
from jax.experimental import pallas as pl
from jax.experimental.pallas import tpu as pltpu
from jax.sharding import Mesh, PartitionSpec as P

HD = 128
SPAN = 128
REACH = 2
HEAD = ("y_lo", "core")
BLK = ("x", "y_hi", "z")
FINE = (2, 2, 4, 2, 4)
SCALE = HD ** (-0.5)
LOG2E = 1.4426950408889634
BIG = 1e30
NN = (((1,), (0,)), ((), ()))
NT = (((1,), (1,)), ((), ()))


def dot(a, b, dims):
    return lax.dot_general(a, b, dims, preferred_element_type=jnp.float32)


def tile_grads(query, grad_out, lse2, delta, query_spans, key_spans, kvs, own, dq_sum, dkv_sums, dq_type, dkv_type):
    rows, cols = query.shape
    heads = cols // HD
    n = len(kvs)
    length = kvs[0].shape[0]
    query_rows = min(256, rows)
    key_rows = length
    sums = ([] if dq_sum is None else [dq_sum]) + ([] if dkv_sums is None else list(dkv_sums))

    def body(qspan_ref, kspan_ref, q_ref, g_ref, lse_ref, delta_ref, *rest):
        kv_refs, rest = rest[:n], list(rest[n:])
        dq_sum_ref = rest.pop(0) if dq_sum is not None else None
        dkv_sum_refs = [rest.pop(0) for _ in range(n)] if dkv_sums is not None else None
        dq_ref, dkv_refs, kt_ref, total = rest[0], rest[1 : n + 1], rest[n + 1], rest[n + 2]

        @pl.when(pl.program_id(0) == 0)
        def _():
            for i in range(n):
                if dkv_sums is None:
                    total[i] = jnp.zeros((length, 2 * HD), jnp.float32)
                else:
                    total[i] = dkv_sum_refs[i][...]
                kt_ref[i] = kv_refs[i][:, :HD].T

        lane = lax.broadcasted_iota(jnp.int32, (1, query_rows), 1)
        spans = query_rows // SPAN
        for qb in range(rows // query_rows):
            qs = pl.ds(qb * query_rows, query_rows)
            q, g = q_ref[qs, :], g_ref[qs, :]
            lse, delt = lse_ref[0, :, qs], delta_ref[0, :, qs]
            qspan = jnp.full((1, query_rows), qspan_ref[qb * spans], jnp.int32)
            for s in range(1, spans):
                qspan = jnp.where(lane >= s * SPAN, qspan_ref[qb * spans + s], qspan)
            qpos = qspan * SPAN + lane % SPAN
            dq = None
            for i in range(n):
                for kb in range(length // key_rows):
                    ks = pl.ds(kb * key_rows, key_rows)
                    score = dot(kv_refs[i][ks, :HD], q, NT)
                    gprob = dot(kv_refs[i][ks, HD:], g, NT)
                    probs, scores = [], []
                    for s in range(key_rows // SPAN):
                        at = slice(s * SPAN, (s + 1) * SPAN)
                        kspan = kspan_ref[i, kb * (key_rows // SPAN) + s]
                        if i == own:
                            kpos = kspan * SPAN + lax.broadcasted_iota(jnp.int32, (SPAN, 1), 0)
                            prob = jnp.exp2(
                                jnp.where(kpos <= qpos, score[at] * (SCALE * LOG2E) - lse, -BIG)
                            )
                        else:
                            prob = jnp.exp2(
                                score[at] * (SCALE * LOG2E) - jnp.where(kspan < qspan, lse, BIG)
                            )
                        probs.append(prob.astype(jnp.bfloat16))
                        scores.append((prob * (gprob[at] - delt)).astype(jnp.bfloat16))
                    prob_half = jnp.concatenate(probs, 0)
                    score_half = jnp.concatenate(scores, 0)
                    total[i, ks, HD:] += dot(prob_half, g, NN)
                    total[i, ks, :HD] += dot(score_half, q, NN) * SCALE
                    part = dot(kt_ref[i, :, ks], score_half, NN)
                    dq = part if dq is None else dq + part
            dq = dq.T * SCALE
            if dq_sum is not None:
                dq = dq + dq_sum_ref[qs, :]
            dq_ref[qs, :] = dq.astype(dq_type)

        @pl.when(pl.program_id(0) == heads - 1)
        def _():
            for i in range(n):
                dkv_refs[i][...] = total[i].astype(dkv_type)

    def whole(shape):
        return pl.BlockSpec(shape, lambda h: (0,) * len(shape))

    smem = pl.BlockSpec(memory_space=pltpu.SMEM)
    per_head = pl.BlockSpec((rows, HD), lambda h: (0, h))
    per_row = pl.BlockSpec((1, 1, rows), lambda h: (h, 0, 0))
    sum_specs = ([] if dq_sum is None else [per_head]) + (
        [] if dkv_sums is None else [whole((length, 2 * HD))] * n
    )
    return pl.pallas_call(
        body,
        grid=(heads,),
        in_specs=[smem, smem, per_head, per_head, per_row, per_row]
        + [whole((length, 2 * HD))] * n
        + sum_specs,
        out_specs=[per_head] + [whole((length, 2 * HD))] * n,
        out_shape=[jax.ShapeDtypeStruct((rows, cols), dq_type)]
        + [jax.ShapeDtypeStruct((length, 2 * HD), dkv_type)] * n,
        scratch_shapes=[
            pltpu.VMEM((n, HD, length), jnp.bfloat16),
            pltpu.VMEM((n, length, 2 * HD), jnp.float32),
        ],
        compiler_params=pltpu.CompilerParams(
            vmem_limit_bytes=32 * 2**20, dimension_semantics=("arbitrary",)
        ),
        cost_estimate=pl.CostEstimate(
            flops=10 * rows * length * n * cols,
            bytes_accessed=n * length * HD * 12 + rows * cols * 8,
            transcendentals=rows * length * n * heads,
        ),
    )(query_spans, key_spans, query, grad_out, lse2, delta, *kvs, *sums)


def prepare(pieces, out_heads, mine):
    rows, cols = pieces[0].shape
    heads = cols // HD

    def body(mine_ref, *refs):
        out_ref, grad_ref, delta_ref = refs[4:]
        for d in range(4):
            at = pl.ds(d * rows, rows)
            there = pl.ds(pl.multiple_of(mine_ref[d] * rows, rows), rows)
            grad_ref[at, :] = refs[d][...]
            for h in range(heads):
                cs = slice(h * HD, (h + 1) * HD)
                product = refs[d][:, cs].astype(jnp.float32) * out_ref[there, cs].astype(jnp.float32)
                delta_ref[h, :, at] = jnp.sum(product.T, axis=0, keepdims=True)

    vmem = pl.BlockSpec(memory_space=pltpu.VMEM)
    return pl.pallas_call(
        body,
        in_specs=[pl.BlockSpec(memory_space=pltpu.SMEM)] + [vmem] * 5,
        out_specs=[vmem, vmem],
        out_shape=[
            jax.ShapeDtypeStruct((4 * rows, cols), jnp.bfloat16),
            jax.ShapeDtypeStruct((heads, 1, 4 * rows), jnp.float32),
        ],
        compiler_params=pltpu.CompilerParams(vmem_limit_bytes=24 * 2**20),
        cost_estimate=pl.CostEstimate(
            flops=8 * rows * cols, bytes_accessed=24 * rows * cols, transcendentals=0
        ),
    )(mine, *pieces, out_heads)


def by_head(pieces, mine, widths):
    rows = pieces[0].shape[0]
    n = len(widths)

    def body(mine_ref, *refs):
        for d in range(4):
            at = 0
            for out_ref, width in zip(refs[4:], widths):
                to = pl.ds(pl.multiple_of(mine_ref[d] * width, HD), width)
                out_ref[:, to] = refs[d][:, at : at + width]
                at += width

    vmem = pl.BlockSpec(memory_space=pltpu.VMEM)
    return pl.pallas_call(
        body,
        in_specs=[pl.BlockSpec(memory_space=pltpu.SMEM)] + [vmem] * 4,
        out_specs=[vmem] * n,
        out_shape=[jax.ShapeDtypeStruct((rows, 4 * width), jnp.bfloat16) for width in widths],
        cost_estimate=pl.CostEstimate(
            flops=0, bytes_accessed=16 * rows * sum(widths), transcendentals=0
        ),
    )(mine, *pieces)


def shift(block, axis, by):
    size = lax.axis_size(axis)
    return lax.ppermute(block, axis, [(i, (i + by) % size) for i in range(size)])


def to_peer(block, d):
    return lax.ppermute(block, HEAD, [(i, i ^ d) for i in range(4)]) if d else block


def fence(*arrays):
    return lax.optimization_barrier(arrays)


def gather(blocks):
    half = blocks[0].shape[0] // 2
    axes = (("z", "x"), ("x", "z"))

    def step(sends):
        got = fence(*(shift(array, axis, by) for array, axis, by in sends))
        return list(zip(got[0::2], got[1::2]))

    block = [
        jnp.concatenate([b[s * half : (s + 1) * half] for b in blocks], axis=0) for s in range(2)
    ]
    near = step([(block[s], axes[s][0], by) for s in range(2) for by in (1, 3)])
    far = step(
        [
            (piece, axes[s][0], by)
            for s in range(2)
            for by, piece in ((1, near[s][0][:half]), (3, near[s][1][half:]))
        ]
    )
    line = [
        jnp.concatenate([block[s], near[s][0], far[s][0], far[s][1], near[s][1]], axis=0)
        for s in range(2)
    ]
    near = step([(line[s], axes[s][1], by) for s in range(2) for by in (1, 3)])
    far = step(
        [
            (piece, axes[s][1], by)
            for s in range(2)
            for by, piece in ((1, near[s][0][: 4 * half]), (3, near[s][1][4 * half :]))
        ]
    )
    return [[line[s], near[s][0], far[s][0], far[s][1], near[s][1]] for s in range(2)]


def lines_place(half):
    def copies(px, py, pz):
        for dx in range(4):
            for other in range(2):
                for dz in range(4):
                    for side, (first, second) in enumerate(((dz, dx), (dx, dz))):
                        src = (first * 2 + other) * half
                        kind = (0, 1, 2, 4)[second]
                        if second == 2 and first >= 2:
                            kind, src = 3, src - 4 * half
                        row = ((((px + 4 - dx) % 4) * 2 + (py + other) % 2) * 4 + (pz + 4 - dz) % 4)
                        yield dx, side * 5 + kind, src, row * (2 * half) + side * half, half

    return copies


def planes_place(length):
    def copies(px, py, pz):
        for dx in range(4):
            ax = (px + 4 - dx) % 4
            for z in range(4):
                for other in range(2):
                    src = ((ax * 4 + z) * 2 + other) * length
                    yield dx, 0, src, ((ax * 2 + (py + other) % 2) * 4 + z) * length, length

    return copies


def project(x_pieces, w_place, w_pieces, where):
    depth = x_pieces[0].shape[1]
    width = w_pieces[0].shape[1]
    chunk = depth // 4
    rows = sum(piece.shape[0] for piece in x_pieces)
    n_x, n_w = len(x_pieces), len(w_pieces)
    at_once = 512

    def body(where_ref, *refs):
        x_refs, w_refs = refs[:n_x], refs[n_x : n_x + n_w]
        out_ref, x_mem, w_mem, total, x_sems, w_sems = refs[n_x + n_w :]
        px, py, pz = where_ref[0], where_ref[1], where_ref[2]

        def columns(dx):
            return pl.ds(pl.multiple_of(((px + 4 - dx) % 4) * chunk, 128), chunk)

        moves = list(w_place(px, py, pz))
        for dx in range(4):
            for which, src, dst, size in [m[1:] for m in moves if m[0] == dx]:
                src = src if isinstance(src, int) else pl.multiple_of(src, 16)
                pltpu.make_async_copy(
                    w_refs[which].at[pl.ds(src, size), :],
                    w_mem.at[pl.ds(pl.multiple_of(dst, 16), size), :],
                    w_sems.at[dx],
                ).start()
            at = 0
            for ref in x_refs:
                pltpu.make_async_copy(
                    ref.at[:, columns(dx)],
                    x_mem.at[pl.ds(at, ref.shape[0]), columns(dx)],
                    x_sems.at[dx],
                ).start()
                at += ref.shape[0]
        for dx in range(4):
            here = columns(dx)
            pltpu.make_async_copy(w_mem.at[here, :], w_mem.at[here, :], w_sems.at[dx]).wait()
            pltpu.make_async_copy(x_mem.at[:, here], x_mem.at[:, here], x_sems.at[dx]).wait()
            for start in range(0, rows, at_once):
                at = pl.ds(start, at_once)
                part = dot(x_mem[at, here], w_mem[here, :], NN)
                if dx == 0:
                    total[at, :] = part
                elif dx == 3:
                    out_ref[at, :] = (total[at, :] + part).astype(jnp.bfloat16)
                else:
                    total[at, :] += part

    hbm = pl.BlockSpec(memory_space=pl.ANY)
    return pl.pallas_call(
        body,
        in_specs=[pl.BlockSpec(memory_space=pltpu.SMEM)] + [hbm] * (n_x + n_w),
        out_specs=pl.BlockSpec(memory_space=pltpu.VMEM),
        out_shape=jax.ShapeDtypeStruct((rows, width), jnp.bfloat16),
        scratch_shapes=[
            pltpu.VMEM((rows, depth), jnp.bfloat16),
            pltpu.VMEM((depth, width), jnp.bfloat16),
            pltpu.VMEM((rows, width), jnp.float32),
            pltpu.SemaphoreType.DMA((4,)),
            pltpu.SemaphoreType.DMA((4,)),
        ],
        compiler_params=pltpu.CompilerParams(vmem_limit_bytes=32 * 2**20),
        cost_estimate=pl.CostEstimate(
            flops=2 * rows * depth * width,
            bytes_accessed=2 * (rows * depth + depth * width + rows * width),
            transcendentals=0,
        ),
    )(where, *x_pieces, *w_pieces)


def local(x_ckpt, w_query, w_key, w_value, dout_seq, out_heads, lse_heads, span_order):
    rows = x_ckpt.shape[0]
    cols = w_query.shape[1]
    me = lax.axis_index(HEAD)
    group = lax.axis_index(BLK)
    groups = lax.axis_size(BLK)
    peers = range(4)
    mine = [me ^ d for d in peers]
    mine_all = jnp.stack(mine)
    where = jnp.stack([lax.axis_index(axis) for axis in ("x", "y_hi", "z")])

    w_own = jnp.concatenate([w_key, w_value, w_query], axis=1)
    w_pair = shift(w_own, "y_hi", 1)
    q_rows = jnp.concatenate([w_query, w_pair[:, 2 * HD :]], axis=0)
    q_weights = lax.all_gather(q_rows, ("x", "z"), axis=0, tiled=True)
    kv_lines = gather([w_own[:, : 2 * HD], w_pair[:, : 2 * HD]])

    x_sent, _ = fence(x_ckpt, w_pair)
    x_far = to_peer(x_sent, 2)
    x_core = to_peer(x_sent, 1)
    x_far, *flat = fence(x_far, *kv_lines[0], *kv_lines[1])
    kv_lines = [flat[:5], flat[5:]]
    x_pieces = [x_ckpt, x_core, x_far, to_peer(x_far, 1)]

    lse_rows = lse_heads.T * LOG2E
    lse2 = jnp.concatenate(
        [lax.dynamic_slice_in_dim(lse_rows, mine[d] * rows, rows, 1) for d in peers], axis=1
    )[:, None, :]
    spans = rows // SPAN

    def spans_of(which):
        base = which * (4 * spans)
        return jnp.concatenate(
            [lax.dynamic_slice_in_dim(span_order, base + mine[d] * spans, spans) for d in peers]
        )

    span_ids = [spans_of((group - r) % groups) for r in range(REACH + 1)]

    kv = project(x_pieces, lines_place(w_own.shape[0] // 2), kv_lines[0] + kv_lines[1], where)
    kv1, kv2 = shift(kv, BLK, 1), shift(kv, BLK, 2)
    grads = [lax.dynamic_slice_in_dim(dout_seq, mine[d] * cols, cols, 1) for d in peers]
    *grads, _ = fence(*grads, x_far)
    grads = [to_peer(grads[d], d) for d in peers]
    query = project(x_pieces, planes_place(w_query.shape[0]), [q_weights], where)
    *grads, query = fence(*grads, query)
    grad_out, delta = prepare(grads, out_heads, mine_all)

    far = slice(2 * rows, 4 * rows)
    near = slice(0, 2 * rows)

    def part(at, kvs, ids, own, dq_sum, dkv_sums, dq_type, dkv_type):
        return tile_grads(
            query[at], grad_out[at], lse2[:, :, at], delta[:, :, at],
            span_ids[0][at.start // SPAN : at.stop // SPAN], jnp.stack(ids), kvs, own,
            dq_sum, dkv_sums, dq_type, dkv_type,
        )

    f32, bf16 = jnp.float32, jnp.bfloat16
    dq_far, dkv0 = part(far, [kv], span_ids[:1], 0, None, None, f32, f32)
    dq_far, dkv1, dkv2 = part(far, [kv1, kv2], span_ids[1:], -1, dq_far, None, bf16, f32)
    dq_near, dkv1, dkv2 = part(near, [kv1, kv2], span_ids[1:], -1, None, [dkv1, dkv2], f32, bf16)
    dq2, dq3 = to_peer(dq_far[:rows], 2), to_peer(dq_far[rows:], 3)
    back1, back2 = shift(dkv1, BLK, -1), shift(dkv2, BLK, -2)
    dq_near, dkv0 = part(near, [kv], span_ids[:1], 0, dq_near, [dkv0], bf16, f32)
    dq1 = to_peer(dq_near[rows:], 1)
    dkv = (dkv0 + back1.astype(f32) + back2.astype(f32)).astype(bf16)
    dkvs = [to_peer(dkv[d * rows : (d + 1) * rows], d) for d in peers]
    (grad_query,) = by_head([dq_near[:rows], dq1, dq2, dq3], mine_all, [cols])
    grad_key, grad_value = by_head(dkvs, mine_all, [HD, HD])
    return grad_query, grad_key, grad_value


def solution(mesh):
    fine = Mesh(mesh.devices.reshape(FINE), HEAD + BLK)
    rows = P(BLK + HEAD, None)
    both = P(BLK, HEAD)
    return jax.shard_map(
        local,
        mesh=fine,
        in_specs=(rows, both, both, both, rows, both, both, P()),
        out_specs=(rows, rows, rows),
        check_vma=False,
    )
```

time: 278 us -> 231 us (0.83); the launches traced: 272 us -> 230 us
  waiting for transfers between devices: 119 us -> 56.9 us
  Pallas kernels: 48.2 us -> 84.6 us
  starting transfers between devices: 30.1 us -> 59.9 us
  local copies, waits for them, and re-layouts: 35.9 us -> 10.9 us
  matrix products: 16 us -> 0 us
  other arithmetic: 8.76 us -> 3.31 us
    ppermute x12, waiting for transfers between devices: 91.3 us -> 26.3 us  [to_peer(): lax.ppermute(block, HEAD, [(i, i ^ d) for i in range(4)])]
    pallas_call x0 -> x5, Pallas kernels: none -> 33.3 us  [the longest x2 26.9 us: project(): pl.pallas_call(body, in_specs=[pl.BlockSpec(memory_space=pltpu.SMEM)] + [...]
    ppermute x4 -> x21, waiting for transfers between devices: 0.01 us -> 30.6 us  [shift(): lax.ppermute(block, axis, [(i, (i + by) % size) for i in range(size)])]
    all_gather x1, waiting for transfers between devices: 27.7 us -> 0.01 us  [local(): q_weights = lax.all_gather(q_rows, ('x', 'z'), axis=0, tiled=True)]
    ppermute x4 -> x21, starting transfers between devices: 16.6 us -> 42.6 us  [shift(): lax.ppermute(block, axis, [(i, (i + by) % size) for i in range(size)])]
    dot_general x2 -> x0, matrix products: 16 us -> none  [dot(): return lax.dot_general(a, b, dims, preferred_element_type=jnp.float32)]
    unnamed x30 -> x69, local copies, waits for them, and re-layouts: 17.9 us -> 6.38 us
    concatenate x2 -> x3, local copies, waits for them, and re-layouts: 4.48 us -> 0.03 us  [the longest x2 0.02 us: gather(): jnp.concatenate([block[s], near[s][0], far[s][0], far[s][1], near[s][1]],...]
  transfers between devices with their start and end apart: 17 -> 34, of which waited for: 8 -> 11; matrix products, arithmetic and copies ran while one was open for 17% -> 2% of each run, Pallas kernels for 12% -> 22%
where the time goes in v2:
time: 231 us; the launch traced here: 230 us
  Pallas kernels  84.6 us (37%)
  starting transfers between devices  59.9 us (26%)
  waiting for transfers between devices  56.9 us (25%)
  between operations  14.7 us (6%)
  local copies, waits for them, and re-layouts  10.9 us (5%)
  other arithmetic  3.31 us (1%)
    pallas_call x4, Pallas kernels, tile_grads(): pl.pallas_call(body, grid=(heads,), in_specs=[smem, smem, per_head, per_h...  51.3 us
    ppermute x21, starting transfers between devices, shift(): lax.ppermute(block, axis, [(i, (i + by) % size) for i in range(size)])  42.6 us
    ppermute x21, waiting for transfers between devices, shift(): lax.ppermute(block, axis, [(i, (i + by) % size) for i in range(size)])  30.6 us
    pallas_call x2, Pallas kernels, project(): pl.pallas_call(body, in_specs=[pl.BlockSpec(memory_space=pltpu.SMEM)] + [...  26.9 us
    ppermute x12, waiting for transfers between devices, to_peer(): lax.ppermute(block, HEAD, [(i, i ^ d) for i in range(4)])  26.3 us
    ppermute x12, starting transfers between devices, to_peer(): lax.ppermute(block, HEAD, [(i, i ^ d) for i in range(4)])  17.2 us
    unnamed x69, local copies, waits for them, and re-layouts  6.38 us
  transfers between devices with their start and end apart: 34, of which 11 were waited for; matrix products, arithmetic and copies ran while one was open for 2% of the time, Pallas kernels for 22%

profile of v2, /device:TPU:1, one launch (start us, length us, event | category | flops | bytes accessed | tf_op | source)
XLA Modules:
  0.0 230.2 jit_solution(8457449142539697584)
XLA Ops:
  7.2 1.0 pad_maximum_fusion.1
  8.2 3.8 %collective-permute-start = (bf16[160,896]{1,0:T(8,128)(2,1)S(1)}, bf16[160,896]{1,0:T(8,128)(2,1)S(1)}, u32[]{:S(2)}, u32[]{:S(2)}) collective-permute-start(bf16[160,896]{1,0:T(8,128)(2,1)S(1)} %pad_maximum_fusion.1), channel_id=1, source_target_pairs={{0,4},{4,0},{1,5},{5,1},{2,6},{6,2},{3,7},{7,3},{8,12},{12,8},{9,1... | collective-permute-start | bytes 860168 | tf_op jit(solution)/shard_map/ppermute | solution.py:186
  12.0 6.3 %collective-permute-done = bf16[160,896]{1,0:T(8,128)(2,1)S(1)} collective-permute-done((bf16[160,896]{1,0:T(8,128)(2,1)S(1)}, bf16[160,896]{1,0:T(8,128)(2,1)S(1)}, u32[]{:S(2)}, u32[]{:S(2)}) %collective-permute-start) | collective-permute-done | bytes 286752 | tf_op jit(solution)/shard_map/ppermute | solution.py:186
  18.3 1.7 pad_maximum_fusion
  20.1 1.4 collective-permute-start.1
  21.6 1.7 collective-permute-start.2
  23.3 2.2 collective-permute-start.3
  25.5 1.3 collective-permute-start.4
  26.8 1.5 collective-permute-start.5
  28.3 1.8 collective-permute-done.4
  30.5 2.7 %collective-permute-start.7 = (bf16[80,256]{1,0:T(8,128)(2,1)S(1)}, bf16[80,256]{1,0:T(8,128)(2,1)S(1)}, u32[]{:S(2)}, u32[]{:S(2)}) collective-permute-start(bf16[80,256]{1,0:T(8,128)(2,1)S(1)} %slice.112), channel_id=1, source_target_pairs={{0,3},{1,0},{2,1},{3,2},{4,7},{5,4},{6,5},{7,6},{8,11},{9,8},{10,9... | collective-permute-start | bytes 122888 | tf_op jit(solution)/shard_map/ppermute | solution.py:186
  33.2 1.2 collective-permute-start.8
  34.4 1.5 collective-permute-start.9
  35.9 1.3 collective-permute-done.8
  37.3 1.0 collective-permute-done.9
  38.3 2.7 %collective-permute-start.13 = (bf16[640,256]{1,0:T(8,128)(2,1)S(1)}, bf16[640,256]{1,0:T(8,128)(2,1)S(1)}, u32[]{:S(2)}, u32[]{:S(2)}) collective-permute-start(bf16[640,256]{1,0:T(8,128)(2,1)S(1)} %constant_dynamic-update-slice_fusion.8.refs_9_), channel_id=1, source_target_pairs={{0,3},{1,0},{2,1},{3,2},{4,7},{5,4},{6,5},{7,6},{8,11},{9,8},{10,9... | collective-permute-start | bytes 983048 | tf_op jit(solution)/shard_map/ppermute | solution.py:186
  41.0 1.1 collective-permute-start.10
  42.1 1.7 collective-permute-start.11
  43.8 7.5 %collective-permute-done.12.refs_10_ = bf16[640,256]{1,0:T(8,128)(2,1)S(1)} collective-permute-done((bf16[640,256]{1,0:T(8,128)(2,1)S(1)}, bf16[640,256]{1,0:T(8,128)(2,1)S(1)}, u32[]{:S(2)}, u32[]{:S(2)}) %collective-permute-start.12) | collective-permute-done | bytes 327712 | tf_op jit(solution)/shard_map/ppermute | solution.py:186
  52.3 1.9 collective-permute-start.15
  54.5 2.5 %collective-permute-start.17 = (bf16[320,256]{1,0:T(8,128)(2,1)S(1)}, bf16[320,256]{1,0:T(8,128)(2,1)S(1)}, u32[]{:S(2)}, u32[]{:S(2)}) collective-permute-start(bf16[320,256]{1,0:T(8,128)(2,1)S(1)} %slice.118), channel_id=1, source_target_pairs={{0,3},{1,0},{2,1},{3,2},{4,7},{5,4},{6,5},{7,6},{8,11},{9,8},{10,9... | collective-permute-start | bytes 491528 | tf_op jit(solution)/shard_map/ppermute | solution.py:186
  57.1 4.6 %collective-permute-start.21 = (bf16[256,5120]{1,0:T(8,128)(2,1)S(1)}, bf16[256,5120]{1,0:T(8,128)(2,1)}, u32[]{:S(2)}, u32[]{:S(2)}) collective-permute-start(bf16[256,5120]{1,0:T(8,128)(2,1)S(1)} %copy-done), channel_id=1, source_target_pairs={{0,32},{32,0},{64,96},{96,64},{1,33},{33,1},{65,97},{97,65},{2,34}... | collective-permute-start | bytes 7864328 | tf_op jit(solution)/shard_map/ppermute | solution.py:190
  63.7 13.6 %collective-permute-done.1.refs_2_ = bf16[256,5120]{1,0:T(8,128)(2,1)} collective-permute-done((bf16[256,5120]{1,0:T(8,128)(2,1)}, bf16[256,5120]{1,0:T(8,128)(2,1)}, u32[]{:S(2)}, u32[]{:S(2)}) %collective-permute-start.1) | collective-permute-done | bytes 2621472 | tf_op jit(solution)/shard_map/ppermute | solution.py:190
  77.4 2.4 %collective-permute-start.22 = (bf16[256,5120]{1,0:T(8,128)(2,1)}, bf16[256,5120]{1,0:T(8,128)(2,1)}, u32[]{:S(2)}, u32[]{:S(2)}) collective-permute-start(bf16[256,5120]{1,0:T(8,128)(2,1)} %collective-permute-done.1.refs_2_), channel_id=1, source_target_pairs={{0,32},{32,0},{64,96},{96,64},{1,33},{33,1},{65,97},{97,65},{2,34}... | collective-permute-start | bytes 7864328 | tf_op jit(solution)/shard_map/ppermute | solution.py:190
  80.6 2.5 %constant_dynamic-slice_fusion = (bf16[256,640]{1,0:T(8,128)(2,1)}, bf16[256,640]{1,0:T(8,128)(2,1)}, bf16[256,640]{1,0:T(8,128)(2,1)S(1)}, bf16[256,640]{1,0:T(8,128)(2,1)}) fusion(bf16[256,2560]{1,0:T(8,128)(2,1)} %param.12, s32[]{:T(128)S(6)} %select_n.83, s32[]{:T(128)S(6)} %select_n.81, s32[]{:T(128)S(6)} %select_n.80, s32[]{:T(128)S(6)} %select_n.82), kind=kLoop, calls=%fused_computation.25 | loop fusion | bytes 2621456 | tf_op jit(solution)/shard_map/dynamic_slice | solution.py:368
  83.1 1.4 collective-permute-start.19
  85.3 8.8 %shard_map.105.rest_0_ = bf16[1024,256]{1,0:T(8,128)(2,1)} custom-call(s32[3]{0:T(128)S(1)} %pad_add_fusion.3.where_ref, bf16[256,5120]{1,0:T(8,128)(2,1)S(1)} %copy-done, bf16[256,5120]{1,0:T(8,128)(2,1)} %collective-permute-done.21.refs_1_, bf16[256,5120]{1,0:T(8,128)(2,1)} %collective-permute-done.1.refs_2_, ...), custom_call_target="tpu_custom_call" | custom-call | flops 2684354560 | bytes 13631488 | tf_op jit(solution)/shard_map/pallas_call | solution.py:307
  94.1 1.7 collective-permute-start.23
  95.7 3.3 %collective-permute-start.24 = (bf16[1024,256]{1,0:T(8,128)(2,1)}, bf16[1024,256]{1,0:T(8,128)(2,1)}, u32[]{:S(2)}, u32[]{:S(2)}) collective-permute-start(bf16[1024,256]{1,0:T(8,128)(2,1)} %shard_map.105.rest_0_), channel_id=1, source_target_pairs={{0,2},{1,3},{2,4},{3,5},{4,6},{5,7},{6,8},{7,9},{8,10},{9,11},{10,... | collective-permute-start | bytes 1572872 | tf_op jit(solution)/shard_map/ppermute | solution.py:186
  99.0 2.9 %copy-done.19 = bf16[5120,640]{1,0:T(8,128)(2,1)S(1)} copy-done((bf16[5120,640]{1,0:T(8,128)(2,1)S(1)}, bf16[5120,640]{1,0:T(8,128)(2,1)}, u32[]{:S(2)}) %copy-start.19) | copy-done | bytes 6553624
  101.9 18.1 %shard_map.103 = bf16[1024,640]{1,0:T(8,128)(2,1)S(1)} custom-call(s32[3]{0:T(128)S(1)} %pad_add_fusion.3.where_ref, bf16[256,5120]{1,0:T(8,128)(2,1)S(1)} %copy-done, bf16[256,5120]{1,0:T(8,128)(2,1)} %collective-permute-done.21.refs_1_, bf16[256,5120]{1,0:T(8,128)(2,1)} %collective-permute-done.1.refs_2_, ...), custom_call_target="tpu_custom_call" | custom-call | flops 6710886400 | bytes 18350080 | tf_op jit(solution)/shard_map/pallas_call | solution.py:307
  120.1 2.0 shard_map.104
  122.3 9.3 %shard_map.106 = (f32[512,640]{1,0:T(8,128)S(1)}, f32[1024,256]{1,0:T(8,128)S(1)}) custom-call(s32[4]{0:T(128)S(1)} %get-tuple-element.150.qspan_ref, s32[1,8]{1,0:T(1,128)S(1)} %get-tuple-element.151.kspan_ref, bf16[512,640]{1,0:T(8,128)(2,1)S(1)} %get-tuple-element.154.q_ref, bf16[512,640]{1,0:T(8,128)(2,1)S(1)} %get-tuple-element.105.g_ref, ...), custom_call_target="tpu_custom_call" | custom-call | flops 3355443200 | bytes 4194304 | tf_op jit(solution)/shard_map/pallas_call | solution.py:105
  131.6 16.3 %shard_map.107 = (bf16[512,640]{1,0:T(8,128)(2,1)S(1)}, f32[1024,256]{1,0:T(8,128)S(1)}, f32[1024,256]{1,0:T(8,128)S(1)}) custom-call(s32[4]{0:T(128)S(1)} %get-tuple-element.150.qspan_ref, s32[2,8]{1,0:T(2,128)S(1)} %pad_add_fusion.kspan_ref, bf16[512,640]{1,0:T(8,128)(2,1)S(1)} %get-tuple-element.154.q_ref, bf16[512,640]{1,0:T(8,128)(2,1)S(1)} %get-tuple-element.105.g_ref, ...), custom_call_target="tpu_custom_call" | custom-call | flops 6710886400 | bytes 5767168 | tf_op jit(solution)/shard_map/pallas_call | solution.py:105
  147.9 16.4 %shard_map.108 = (f32[512,640]{1,0:T(8,128)S(1)}, bf16[1024,256]{1,0:T(8,128)(2,1)S(1)}, bf16[1024,256]{1,0:T(8,128)(2,1)S(1)}) custom-call(s32[4]{0:T(128)S(1)} %get-tuple-element.149.qspan_ref, s32[2,8]{1,0:T(2,128)S(1)} %pad_add_fusion.kspan_ref, bf16[512,640]{1,0:T(8,128)(2,1)S(1)} %get-tuple-element.153.q_ref, ...), custom_call_target="tpu_custom_call" | custom-call | flops 6710886400 | bytes 5767168 | tf_op jit(solution)/shard_map/pallas_call | solution.py:105
  164.3 5.3 %collective-permute-start.28 = (bf16[1024,256]{1,0:T(8,128)(2,1)S(1)}, bf16[1024,256]{1,0:T(8,128)(2,1)S(1)}, u32[]{:S(2)}, u32[]{:S(2)}) collective-permute-start(bf16[1024,256]{1,0:T(8,128)(2,1)S(1)} %get-tuple-element.101), channel_id=1, source_target_pairs={{0,31},{1,0},{2,1},{3,2},{4,3},{5,4},{6,5},{7,6},{8,7},{9,8},{10,9... | collective-permute-start | bytes 1572872 | tf_op jit(solution)/shard_map/ppermute | solution.py:186
  169.6 5.4 %collective-permute-start.29 = (bf16[1024,256]{1,0:T(8,128)(2,1)S(1)}, bf16[1024,256]{1,0:T(8,128)(2,1)S(1)}, u32[]{:S(2)}, u32[]{:S(2)}) collective-permute-start(bf16[1024,256]{1,0:T(8,128)(2,1)S(1)} %get-tuple-element.102), channel_id=1, source_target_pairs={{0,30},{1,31},{2,0},{3,1},{4,2},{5,3},{6,4},{7,5},{8,6},{9,7},{10,... | collective-permute-start | bytes 1572872 | tf_op jit(solution)/shard_map/ppermute | solution.py:186
  175.0 9.4 %shard_map.109 = (bf16[512,640]{1,0:T(8,128)(2,1)S(1)}, f32[1024,256]{1,0:T(8,128)S(1)}) custom-call(s32[4]{0:T(128)S(1)} %get-tuple-element.149.qspan_ref, s32[1,8]{1,0:T(1,128)S(1)} %get-tuple-element.151.kspan_ref, bf16[512,640]{1,0:T(8,128)(2,1)S(1)} %get-tuple-element.153.q_ref, bf16[512,640]{1,0:T(8,128)(2,1)S(1)} %get-tuple-element.106.g_ref, ...), custom_call_target="tpu_custom_call" | custom-call | flops 3355443200 | bytes 4194304 | tf_op jit(solution)/shard_map/pallas_call | solution.py:105
  185.1 1.9 collective-permute-start.25
  187.2 1.6 collective-permute-start.27
  188.8 12.2 %collective-permute-done.29 = bf16[1024,256]{1,0:T(8,128)(2,1)S(1)} collective-permute-done((bf16[1024,256]{1,0:T(8,128)(2,1)S(1)}, bf16[1024,256]{1,0:T(8,128)(2,1)S(1)}, u32[]{:S(2)}, u32[]{:S(2)}) %collective-permute-start.29) | collective-permute-done | bytes 524320 | tf_op jit(solution)/shard_map/ppermute | solution.py:186
  201.9 1.4 collective-permute-start.30
  203.3 1.6 collective-permute-start.32
  204.9 3.2 %collective-permute-done.26.refs_2_ = bf16[256,640]{1,0:T(8,128)(2,1)S(1)} collective-permute-done((bf16[256,640]{1,0:T(8,128)(2,1)S(1)}, bf16[256,640]{1,0:T(8,128)(2,1)S(1)}, u32[]{:S(2)}, u32[]{:S(2)}) %collective-permute-start.26) | collective-permute-done | bytes 327712 | tf_op jit(solution)/shard_map/ppermute | solution.py:190
  208.1 7.2 %collective-permute-done.27.refs_3_ = bf16[256,640]{1,0:T(8,128)(2,1)S(1)} collective-permute-done((bf16[256,640]{1,0:T(8,128)(2,1)S(1)}, bf16[256,640]{1,0:T(8,128)(2,1)S(1)}, u32[]{:S(2)}, u32[]{:S(2)}) %collective-permute-start.27) | collective-permute-done | bytes 327712 | tf_op jit(solution)/shard_map/ppermute | solution.py:190
  216.0 2.4 %shard_map.110 = bf16[256,2560]{1,0:T(8,128)(2,1)} custom-call(s32[4]{0:T(128)} %copy-done.18, bf16[256,640]{1,0:T(8,128)(2,1)} %get-tuple-element.116.refs_0_, bf16[256,640]{1,0:T(8,128)(2,1)} %copy-done.20, bf16[256,640]{1,0:T(8,128)(2,1)} %copy-done.21, bf16[256,640]{1,0:T(8,128)(2,1)} %copy-done.22), custom_call_target="tpu_custom_call" | custom-call | bytes 2621440 | tf_op jit(solution)/shard_map/pallas_call | solution.py:173
  218.4 2.3 collective-permute-done.32.refs_3_
  221.4 2.0 shard_map.111
  (134 shorter events, 8.8 us)
Async XLA Ops:
  7.2 14.3 %copy-start.23 = (bf16[160,128]{1,0:T(8,128)(2,1)S(1)}, bf16[160,128]{1,0:T(8,128)(2,1)}, u32[]{:S(2)}) copy-start(bf16[160,128]{1,0:T(8,128)(2,1)} %param.10) | copy-start | bytes 122884
  7.2 14.3 %copy-start.24 = (bf16[160,128]{1,0:T(8,128)(2,1)S(1)}, bf16[160,128]{1,0:T(8,128)(2,1)}, u32[]{:S(2)}) copy-start(bf16[160,128]{1,0:T(8,128)(2,1)} %param.11) | copy-start | bytes 122884
  7.2 91.8 %all-gather.2.cloned.1.call-start = ((), (), s32[]{:S(2)}) async-start(), calls=%async_computation | async-start | bytes 6963200 | tf_op jit(solution)/shard_map/all_gather | solution.py:342
  8.2 10.1 %collective-permute-start = (bf16[160,896]{1,0:T(8,128)(2,1)S(1)}, bf16[160,896]{1,0:T(8,128)(2,1)S(1)}, u32[]{:S(2)}, u32[]{:S(2)}) collective-permute-start(bf16[160,896]{1,0:T(8,128)(2,1)S(1)} %pad_maximum_fusion.1), channel_id=1, source_target_pairs={{0,4},{4,0},{1,5},{5,1},{2,6},{6,2},{3,7},{7,3},{8,12},{12,8},{9,1... | collective-permute-start | bytes 860168 | tf_op jit(solution)/shard_map/ppermute | solution.py:186
  20.1 57.2 %collective-permute-start.1 = (bf16[256,5120]{1,0:T(8,128)(2,1)}, bf16[256,5120]{1,0:T(8,128)(2,1)}, u32[]{:S(2)}, u32[]{:S(2)}) collective-permute-start(bf16[256,5120]{1,0:T(8,128)(2,1)} %refs_0_.3), channel_id=1, source_target_pairs={{0,64},{32,96},{64,0},{96,32},{1,65},{33,97},{65,1},{97,33},{2,66}... | collective-permute-start | bytes 7864328 | tf_op jit(solution)/shard_map/ppermute | solution.py:190
  21.6 6.7 %collective-permute-start.2 = (bf16[160,256]{1,0:T(8,128)(2,1)S(1)}, bf16[160,256]{1,0:T(8,128)(2,1)S(1)}, u32[]{:S(2)}, u32[]{:S(2)}) collective-permute-start(bf16[160,256]{1,0:T(8,128)(2,1)S(1)} %pad_maximum_fusion.2), channel_id=1, source_target_pairs={{0,1},{1,2},{2,3},{3,0},{4,5},{5,6},{6,7},{7,4},{8,9},{9,10},{10,1... | collective-permute-start | bytes 245768 | tf_op jit(solution)/shard_map/ppermute | solution.py:186
  23.3 5.0 %collective-permute-start.3 = (bf16[160,256]{1,0:T(8,128)(2,1)S(1)}, bf16[160,256]{1,0:T(8,128)(2,1)S(1)}, u32[]{:S(2)}, u32[]{:S(2)}) collective-permute-start(bf16[160,256]{1,0:T(8,128)(2,1)S(1)} %pad_maximum_fusion.2), channel_id=1, source_target_pairs={{0,3},{1,0},{2,1},{3,2},{4,7},{5,4},{6,5},{7,6},{8,11},{9,8},{10,9... | collective-permute-start | bytes 245768 | tf_op jit(solution)/shard_map/ppermute | solution.py:186
  25.5 31.5 %copy-start = (bf16[256,5120]{1,0:T(8,128)(2,1)S(1)}, bf16[256,5120]{1,0:T(8,128)(2,1)}, u32[]{:S(2)}) copy-start(bf16[256,5120]{1,0:T(8,128)(2,1)} %refs_0_.3) | copy-start | bytes 7864324
  25.5 4.6 %collective-permute-start.4 = (bf16[160,256]{1,0:T(8,128)(2,1)S(1)}, bf16[160,256]{1,0:T(8,128)(2,1)S(1)}, u32[]{:S(2)}, u32[]{:S(2)}) collective-permute-start(bf16[160,256]{1,0:T(8,128)(2,1)S(1)} %pad_maximum_fusion.3), channel_id=1, source_target_pairs={{0,8},{8,16},{16,24},{24,0},{1,9},{9,17},{17,25},{25,1},{2,10},{10... | collective-permute-start | bytes 245768 | tf_op jit(solution)/shard_map/ppermute | solution.py:186
  26.8 3.7 %collective-permute-start.5 = (bf16[160,256]{1,0:T(8,128)(2,1)S(1)}, bf16[160,256]{1,0:T(8,128)(2,1)S(1)}, u32[]{:S(2)}, u32[]{:S(2)}) collective-permute-start(bf16[160,256]{1,0:T(8,128)(2,1)S(1)} %pad_maximum_fusion.3), channel_id=1, source_target_pairs={{0,24},{8,0},{16,8},{24,16},{1,25},{9,1},{17,9},{25,17},{2,26},{10... | collective-permute-start | bytes 245768 | tf_op jit(solution)/shard_map/ppermute | solution.py:186
  30.5 5.4 %collective-permute-start.6 = (bf16[80,256]{1,0:T(8,128)(2,1)S(1)}, bf16[80,256]{1,0:T(8,128)(2,1)S(1)}, u32[]{:S(2)}, u32[]{:S(2)}) collective-permute-start(bf16[80,256]{1,0:T(8,128)(2,1)S(1)} %slice.111), channel_id=1, source_target_pairs={{0,1},{1,2},{2,3},{3,0},{4,5},{5,6},{6,7},{7,4},{8,9},{9,10},{10,1... | collective-permute-start | bytes 122888 | tf_op jit(solution)/shard_map/ppermute | solution.py:186
  30.5 5.4 %collective-permute-start.7 = (bf16[80,256]{1,0:T(8,128)(2,1)S(1)}, bf16[80,256]{1,0:T(8,128)(2,1)S(1)}, u32[]{:S(2)}, u32[]{:S(2)}) collective-permute-start(bf16[80,256]{1,0:T(8,128)(2,1)S(1)} %slice.112), channel_id=1, source_target_pairs={{0,3},{1,0},{2,1},{3,2},{4,7},{5,4},{6,5},{7,6},{8,11},{9,8},{10,9... | collective-permute-start | bytes 122888 | tf_op jit(solution)/shard_map/ppermute | solution.py:186
  33.2 46.6 %copy-start.29 = (f32[1024,5]{0,1:T(8,128)S(1)}, f32[1024,5]{0,1:T(8,128)}, u32[]{:S(2)}) copy-start(f32[1024,5]{0,1:T(8,128)} %param.14) | copy-start | bytes 61444
  33.2 4.1 %collective-permute-start.8 = (bf16[80,256]{1,0:T(8,128)(2,1)S(1)}, bf16[80,256]{1,0:T(8,128)(2,1)S(1)}, u32[]{:S(2)}, u32[]{:S(2)}) collective-permute-start(bf16[80,256]{1,0:T(8,128)(2,1)S(1)} %slice.113), channel_id=1, source_target_pairs={{0,8},{8,16},{16,24},{24,0},{1,9},{9,17},{17,25},{25,1},{2,10},{10... | collective-permute-start | bytes 122888 | tf_op jit(solution)/shard_map/ppermute | solution.py:186
  34.4 3.8 %collective-permute-start.9 = (bf16[80,256]{1,0:T(8,128)(2,1)S(1)}, bf16[80,256]{1,0:T(8,128)(2,1)S(1)}, u32[]{:S(2)}, u32[]{:S(2)}) collective-permute-start(bf16[80,256]{1,0:T(8,128)(2,1)S(1)} %slice.114), channel_id=1, source_target_pairs={{0,24},{8,0},{16,8},{24,16},{1,25},{9,1},{17,9},{25,17},{2,26},{10... | collective-permute-start | bytes 122888 | tf_op jit(solution)/shard_map/ppermute | solution.py:186
  35.9 44.2 %copy-start.28 = (s32[256]{0:T(256)S(1)}, s32[256]{0:T(256)}, u32[]{:S(2)}) copy-start(s32[256]{0:T(256)} %param.15) | copy-start | bytes 3076
  38.3 23.5 %copy-start.8 = (bf16[640,256]{1,0:T(8,128)(2,1)}, bf16[640,256]{1,0:T(8,128)(2,1)S(1)}, u32[]{:S(2)}) copy-start(bf16[640,256]{1,0:T(8,128)(2,1)S(1)} %constant_dynamic-update-slice_fusion.8.refs_9_) | copy-start | bytes 983044
  38.3 13.0 %collective-permute-start.12 = (bf16[640,256]{1,0:T(8,128)(2,1)S(1)}, bf16[640,256]{1,0:T(8,128)(2,1)S(1)}, u32[]{:S(2)}, u32[]{:S(2)}) collective-permute-start(bf16[640,256]{1,0:T(8,128)(2,1)S(1)} %constant_dynamic-update-slice_fusion.8.refs_9_), channel_id=1, source_target_pairs={{0,1},{1,2},{2,3},{3,0},{4,5},{5,6},{6,7},{7,4},{8,9},{9,10},{10,1... | collective-permute-start | bytes 983048 | tf_op jit(solution)/shard_map/ppermute | solution.py:186
  38.3 13.0 %collective-permute-start.13 = (bf16[640,256]{1,0:T(8,128)(2,1)S(1)}, bf16[640,256]{1,0:T(8,128)(2,1)S(1)}, u32[]{:S(2)}, u32[]{:S(2)}) collective-permute-start(bf16[640,256]{1,0:T(8,128)(2,1)S(1)} %constant_dynamic-update-slice_fusion.8.refs_9_), channel_id=1, source_target_pairs={{0,3},{1,0},{2,1},{3,2},{4,7},{5,4},{6,5},{7,6},{8,11},{9,8},{10,9... | collective-permute-start | bytes 983048 | tf_op jit(solution)/shard_map/ppermute | solution.py:186
  41.0 20.7 %copy-start.10 = (bf16[640,256]{1,0:T(8,128)(2,1)}, bf16[640,256]{1,0:T(8,128)(2,1)S(1)}, u32[]{:S(2)}) copy-start(bf16[640,256]{1,0:T(8,128)(2,1)S(1)} %constant_dynamic-update-slice_fusion.2.refs_4_) | copy-start | bytes 983044
  41.0 10.3 %collective-permute-start.10 = (bf16[640,256]{1,0:T(8,128)(2,1)S(1)}, bf16[640,256]{1,0:T(8,128)(2,1)S(1)}, u32[]{:S(2)}, u32[]{:S(2)}) collective-permute-start(bf16[640,256]{1,0:T(8,128)(2,1)S(1)} %constant_dynamic-update-slice_fusion.2.refs_4_), channel_id=1, source_target_pairs={{0,8},{8,16},{16,24},{24,0},{1,9},{9,17},{17,25},{25,1},{2,10},{10... | collective-permute-start | bytes 983048 | tf_op jit(solution)/shard_map/ppermute | solution.py:186
  42.1 9.2 %collective-permute-start.11 = (bf16[640,256]{1,0:T(8,128)(2,1)S(1)}, bf16[640,256]{1,0:T(8,128)(2,1)S(1)}, u32[]{:S(2)}, u32[]{:S(2)}) collective-permute-start(bf16[640,256]{1,0:T(8,128)(2,1)S(1)} %constant_dynamic-update-slice_fusion.2.refs_4_), channel_id=1, source_target_pairs={{0,24},{8,0},{16,8},{24,16},{1,25},{9,1},{17,9},{25,17},{2,26},{10... | collective-permute-start | bytes 983048 | tf_op jit(solution)/shard_map/ppermute | solution.py:186
  51.3 29.1 %copy-start.2 = (bf16[640,256]{1,0:T(8,128)(2,1)}, bf16[640,256]{1,0:T(8,128)(2,1)S(1)}, u32[]{:S(2)}) copy-start(bf16[640,256]{1,0:T(8,128)(2,1)S(1)} %collective-permute-done.13.refs_13_) | copy-start | bytes 983044
  51.3 5.7 %copy-start.4 = (bf16[640,256]{1,0:T(8,128)(2,1)}, bf16[640,256]{1,0:T(8,128)(2,1)S(1)}, u32[]{:S(2)}) copy-start(bf16[640,256]{1,0:T(8,128)(2,1)S(1)} %collective-permute-done.10.refs_5_) | copy-start | bytes 983044
  51.3 5.7 %copy-start.6 = (bf16[640,256]{1,0:T(8,128)(2,1)}, bf16[640,256]{1,0:T(8,128)(2,1)S(1)}, u32[]{:S(2)}) copy-start(bf16[640,256]{1,0:T(8,128)(2,1)S(1)} %collective-permute-done.11.refs_8_) | copy-start | bytes 983044
  51.4 5.7 %collective-permute-start.14 = (bf16[320,256]{1,0:T(8,128)(2,1)S(1)}, bf16[320,256]{1,0:T(8,128)(2,1)S(1)}, u32[]{:S(2)}, u32[]{:S(2)}) collective-permute-start(bf16[320,256]{1,0:T(8,128)(2,1)S(1)} %slice.115), channel_id=1, source_target_pairs={{0,8},{8,16},{16,24},{24,0},{1,9},{9,17},{17,25},{25,1},{2,10},{10... | collective-permute-start | bytes 491528 | tf_op jit(solution)/shard_map/ppermute | solution.py:186
  52.3 9.4 %collective-permute-start.15 = (bf16[320,256]{1,0:T(8,128)(2,1)S(1)}, bf16[320,256]{1,0:T(8,128)(2,1)S(1)}, u32[]{:S(2)}, u32[]{:S(2)}) collective-permute-start(bf16[320,256]{1,0:T(8,128)(2,1)S(1)} %slice.116), channel_id=1, source_target_pairs={{0,24},{8,0},{16,8},{24,16},{1,25},{9,1},{17,9},{25,17},{2,26},{10... | collective-permute-start | bytes 491528 | tf_op jit(solution)/shard_map/ppermute | solution.py:186
  54.2 8.2 %collective-permute-start.16 = (bf16[320,256]{1,0:T(8,128)(2,1)S(1)}, bf16[320,256]{1,0:T(8,128)(2,1)S(1)}, u32[]{:S(2)}, u32[]{:S(2)}) collective-permute-start(bf16[320,256]{1,0:T(8,128)(2,1)S(1)} %slice.117), channel_id=1, source_target_pairs={{0,1},{1,2},{2,3},{3,0},{4,5},{5,6},{6,7},{7,4},{8,9},{9,10},{10,1... | collective-permute-start | bytes 491528 | tf_op jit(solution)/shard_map/ppermute | solution.py:186
  54.5 8.5 %collective-permute-start.17 = (bf16[320,256]{1,0:T(8,128)(2,1)S(1)}, bf16[320,256]{1,0:T(8,128)(2,1)S(1)}, u32[]{:S(2)}, u32[]{:S(2)}) collective-permute-start(bf16[320,256]{1,0:T(8,128)(2,1)S(1)} %slice.118), channel_id=1, source_target_pairs={{0,3},{1,0},{2,1},{3,2},{4,7},{5,4},{6,5},{7,6},{8,11},{9,8},{10,9... | collective-permute-start | bytes 491528 | tf_op jit(solution)/shard_map/ppermute | solution.py:186
  57.1 28.1 %collective-permute-start.21 = (bf16[256,5120]{1,0:T(8,128)(2,1)S(1)}, bf16[256,5120]{1,0:T(8,128)(2,1)}, u32[]{:S(2)}, u32[]{:S(2)}) collective-permute-start(bf16[256,5120]{1,0:T(8,128)(2,1)S(1)} %copy-done), channel_id=1, source_target_pairs={{0,32},{32,0},{64,96},{96,64},{1,33},{33,1},{65,97},{97,65},{2,34}... | collective-permute-start | bytes 7864328 | tf_op jit(solution)/shard_map/ppermute | solution.py:190
  77.4 7.8 %collective-permute-start.22 = (bf16[256,5120]{1,0:T(8,128)(2,1)}, bf16[256,5120]{1,0:T(8,128)(2,1)}, u32[]{:S(2)}, u32[]{:S(2)}) collective-permute-start(bf16[256,5120]{1,0:T(8,128)(2,1)} %collective-permute-done.1.refs_2_), channel_id=1, source_target_pairs={{0,32},{32,0},{64,96},{96,64},{1,33},{33,1},{65,97},{97,65},{2,34}... | collective-permute-start | bytes 7864328 | tf_op jit(solution)/shard_map/ppermute | solution.py:190
  80.1 39.9 %copy-start.18 = (s32[4]{0:T(128)}, s32[4]{0:T(128)S(1)}, u32[]{:S(2)}) copy-start(s32[4]{0:T(128)S(1)} %pad_add_fusion.1.mine_ref) | copy-start | bytes 52
  83.0 37.0 %collective-permute-start.18 = (bf16[256,640]{1,0:T(8,128)(2,1)}, bf16[256,640]{1,0:T(8,128)(2,1)}, u32[]{:S(2)}, u32[]{:S(2)}) collective-permute-start(bf16[256,640]{1,0:T(8,128)(2,1)} %get-tuple-element.73), channel_id=1, source_target_pairs={{0,32},{32,0},{64,96},{96,64},{1,33},{33,1},{65,97},{97,65},{2,34}... | collective-permute-start | bytes 983048 | tf_op jit(solution)/shard_map/ppermute | solution.py:190
  83.1 37.0 %collective-permute-start.19 = (bf16[256,640]{1,0:T(8,128)(2,1)}, bf16[256,640]{1,0:T(8,128)(2,1)}, u32[]{:S(2)}, u32[]{:S(2)}) collective-permute-start(bf16[256,640]{1,0:T(8,128)(2,1)} %get-tuple-element.74), channel_id=1, source_target_pairs={{0,64},{32,96},{64,0},{96,32},{1,65},{33,97},{65,1},{97,33},{2,66}... | collective-permute-start | bytes 983048 | tf_op jit(solution)/shard_map/ppermute | solution.py:190
  84.5 35.6 %collective-permute-start.20 = (bf16[256,640]{1,0:T(8,128)(2,1)}, bf16[256,640]{1,0:T(8,128)(2,1)}, u32[]{:S(2)}, u32[]{:S(2)}) collective-permute-start(bf16[256,640]{1,0:T(8,128)(2,1)} %get-tuple-element.75), channel_id=1, source_target_pairs={{0,96},{32,64},{64,32},{96,0},{1,97},{33,65},{65,33},{97,1},{2,98}... | collective-permute-start | bytes 983048 | tf_op jit(solution)/shard_map/ppermute | solution.py:190
  94.1 37.5 %collective-permute-start.23 = (bf16[1024,256]{1,0:T(8,128)(2,1)}, bf16[1024,256]{1,0:T(8,128)(2,1)}, u32[]{:S(2)}, u32[]{:S(2)}) collective-permute-start(bf16[1024,256]{1,0:T(8,128)(2,1)} %shard_map.105.rest_0_), channel_id=1, source_target_pairs={{0,1},{1,2},{2,3},{3,4},{4,5},{5,6},{6,7},{7,8},{8,9},{9,10},{10,1... | collective-permute-start | bytes 1572872 | tf_op jit(solution)/shard_map/ppermute | solution.py:186
  95.7 35.8 %collective-permute-start.24 = (bf16[1024,256]{1,0:T(8,128)(2,1)}, bf16[1024,256]{1,0:T(8,128)(2,1)}, u32[]{:S(2)}, u32[]{:S(2)}) collective-permute-start(bf16[1024,256]{1,0:T(8,128)(2,1)} %shard_map.105.rest_0_), channel_id=1, source_target_pairs={{0,2},{1,3},{2,4},{3,5},{4,6},{5,7},{6,8},{7,9},{8,10},{9,11},{10,... | collective-permute-start | bytes 1572872 | tf_op jit(solution)/shard_map/ppermute | solution.py:186
  101.9 18.2 %copy-start.1 = (bf16[1024,640]{1,0:T(8,128)(2,1)S(1)}, bf16[1024,640]{1,0:T(8,128)(2,1)}, u32[]{:S(2)}) copy-start(bf16[1024,640]{1,0:T(8,128)(2,1)} %refs_4_.1) | copy-start | bytes 3932164
  164.3 24.5 %collective-permute-start.28 = (bf16[1024,256]{1,0:T(8,128)(2,1)S(1)}, bf16[1024,256]{1,0:T(8,128)(2,1)S(1)}, u32[]{:S(2)}, u32[]{:S(2)}) collective-permute-start(bf16[1024,256]{1,0:T(8,128)(2,1)S(1)} %get-tuple-element.101), channel_id=1, source_target_pairs={{0,31},{1,0},{2,1},{3,2},{4,3},{5,4},{6,5},{7,6},{8,7},{9,8},{10,9... | collective-permute-start | bytes 1572872 | tf_op jit(solution)/shard_map/ppermute | solution.py:186
  169.6 31.4 %collective-permute-start.29 = (bf16[1024,256]{1,0:T(8,128)(2,1)S(1)}, bf16[1024,256]{1,0:T(8,128)(2,1)S(1)}, u32[]{:S(2)}, u32[]{:S(2)}) collective-permute-start(bf16[1024,256]{1,0:T(8,128)(2,1)S(1)} %get-tuple-element.102), channel_id=1, source_target_pairs={{0,30},{1,31},{2,0},{3,1},{4,2},{5,3},{6,4},{7,5},{8,6},{9,7},{10,... | collective-permute-start | bytes 1572872 | tf_op jit(solution)/shard_map/ppermute | solution.py:186
  185.1 18.1 %collective-permute-start.25 = (bf16[256,640]{1,0:T(8,128)(2,1)S(1)}, bf16[256,640]{1,0:T(8,128)(2,1)S(1)}, u32[]{:S(2)}, u32[]{:S(2)}) collective-permute-start(bf16[256,640]{1,0:T(8,128)(2,1)S(1)} %get-tuple-element.115), channel_id=1, source_target_pairs={{0,32},{32,0},{64,96},{96,64},{1,33},{33,1},{65,97},{97,65},{2,34}... | collective-permute-start | bytes 983048 | tf_op jit(solution)/shard_map/ppermute | solution.py:190
  187.1 21.0 %collective-permute-start.26 = (bf16[256,640]{1,0:T(8,128)(2,1)S(1)}, bf16[256,640]{1,0:T(8,128)(2,1)S(1)}, u32[]{:S(2)}, u32[]{:S(2)}) collective-permute-start(bf16[256,640]{1,0:T(8,128)(2,1)S(1)} %get-tuple-element.114), channel_id=1, source_target_pairs={{0,64},{32,96},{64,0},{96,32},{1,65},{33,97},{65,1},{97,33},{2,66}... | collective-permute-start | bytes 983048 | tf_op jit(solution)/shard_map/ppermute | solution.py:190
  187.2 28.1 %collective-permute-start.27 = (bf16[256,640]{1,0:T(8,128)(2,1)S(1)}, bf16[256,640]{1,0:T(8,128)(2,1)S(1)}, u32[]{:S(2)}, u32[]{:S(2)}) collective-permute-start(bf16[256,640]{1,0:T(8,128)(2,1)S(1)} %get-tuple-element.113), channel_id=1, source_target_pairs={{0,96},{32,64},{64,32},{96,0},{1,97},{33,65},{65,33},{97,1},{2,98}... | collective-permute-start | bytes 983048 | tf_op jit(solution)/shard_map/ppermute | solution.py:190
  201.9 16.5 %collective-permute-start.30 = (bf16[256,256]{1,0:T(8,128)(2,1)S(1)}, bf16[256,256]{1,0:T(8,128)(2,1)S(1)}, u32[]{:S(2)}, u32[]{:S(2)}) collective-permute-start(bf16[256,256]{1,0:T(8,128)(2,1)S(1)} %get-tuple-element.119), channel_id=1, source_target_pairs={{0,32},{32,0},{64,96},{96,64},{1,33},{33,1},{65,97},{97,65},{2,34}... | collective-permute-start | bytes 393224 | tf_op jit(solution)/shard_map/ppermute | solution.py:190
  203.2 15.2 %collective-permute-start.31 = (bf16[256,256]{1,0:T(8,128)(2,1)S(1)}, bf16[256,256]{1,0:T(8,128)(2,1)S(1)}, u32[]{:S(2)}, u32[]{:S(2)}) collective-permute-start(bf16[256,256]{1,0:T(8,128)(2,1)S(1)} %get-tuple-element.118), channel_id=1, source_target_pairs={{0,64},{32,96},{64,0},{96,32},{1,65},{33,97},{65,1},{97,33},{2,66}... | collective-permute-start | bytes 393224 | tf_op jit(solution)/shard_map/ppermute | solution.py:190
  203.3 12.0 %copy-start.20 = (bf16[256,640]{1,0:T(8,128)(2,1)}, bf16[256,640]{1,0:T(8,128)(2,1)S(1)}, u32[]{:S(2)}) copy-start(bf16[256,640]{1,0:T(8,128)(2,1)S(1)} %collective-permute-done.25.refs_1_) | copy-start | bytes 983044
  203.3 17.5 %collective-permute-start.32 = (bf16[256,256]{1,0:T(8,128)(2,1)S(1)}, bf16[256,256]{1,0:T(8,128)(2,1)S(1)}, u32[]{:S(2)}, u32[]{:S(2)}) collective-permute-start(bf16[256,256]{1,0:T(8,128)(2,1)S(1)} %get-tuple-element.117), channel_id=1, source_target_pairs={{0,96},{32,64},{64,32},{96,0},{1,97},{33,65},{65,33},{97,1},{2,98}... | collective-permute-start | bytes 393224 | tf_op jit(solution)/shard_map/ppermute | solution.py:190
  208.1 7.2 %copy-start.21 = (bf16[256,640]{1,0:T(8,128)(2,1)}, bf16[256,640]{1,0:T(8,128)(2,1)S(1)}, u32[]{:S(2)}) copy-start(bf16[256,640]{1,0:T(8,128)(2,1)S(1)} %collective-permute-done.26.refs_2_) | copy-start | bytes 983044
  (16 other events, 48.7 us)
Sparse Core Ops, SparseCore 0:
  20.2 69.3 all-gather.1

commit v3 on v2

--- a/solution.py
+++ b/solution.py
@@ -22,12 +22,13 @@
     return lax.dot_general(a, b, dims, preferred_element_type=jnp.float32)
 
 
-def tile_grads(query, grad_out, lse2, delta, query_spans, key_spans, kvs, own, dq_sum, dkv_sums, dq_type, dkv_type):
-    rows, cols = query.shape
+def tile_grads(start, rows, query, grad_out, lse2, delta, query_spans, key_spans, kvs, own, dq_sum, dkv_sums, dq_type, dkv_type):
+    cols = query.shape[1]
     heads = cols // HD
     n = len(kvs)
     length = kvs[0].shape[0]
     query_rows = min(256, rows)
+    block = start // rows
     key_rows = length
     sums = ([] if dq_sum is None else [dq_sum]) + ([] if dkv_sums is None else list(dkv_sums))
 
@@ -52,9 +53,9 @@
             qs = pl.ds(qb * query_rows, query_rows)
             q, g = q_ref[qs, :], g_ref[qs, :]
             lse, delt = lse_ref[0, :, qs], delta_ref[0, :, qs]
-            qspan = jnp.full((1, query_rows), qspan_ref[qb * spans], jnp.int32)
+            qspan = jnp.full((1, query_rows), qspan_ref[start // SPAN + qb * spans], jnp.int32)
             for s in range(1, spans):
-                qspan = jnp.where(lane >= s * SPAN, qspan_ref[qb * spans + s], qspan)
+                qspan = jnp.where(lane >= s * SPAN, qspan_ref[start // SPAN + qb * spans + s], qspan)
             qpos = qspan * SPAN + lane % SPAN
             dq = None
             for i in range(n):
@@ -97,9 +98,11 @@
         return pl.BlockSpec(shape, lambda h: (0,) * len(shape))
 
     smem = pl.BlockSpec(memory_space=pltpu.SMEM)
-    per_head = pl.BlockSpec((rows, HD), lambda h: (0, h))
-    per_row = pl.BlockSpec((1, 1, rows), lambda h: (h, 0, 0))
-    sum_specs = ([] if dq_sum is None else [per_head]) + (
+    per_head = pl.BlockSpec((rows, HD), lambda h: (block, h))
+    per_row = pl.BlockSpec((1, 1, rows), lambda h: (h, 0, block))
+    out_head = pl.BlockSpec((rows, HD), lambda h: (0, h))
+    sum_head = out_head if dq_sum is not None and dq_sum.shape[0] == rows else per_head
+    sum_specs = ([] if dq_sum is None else [sum_head]) + (
         [] if dkv_sums is None else [whole((length, 2 * HD))] * n
     )
     return pl.pallas_call(
@@ -108,7 +111,7 @@
         in_specs=[smem, smem, per_head, per_head, per_row, per_row]
         + [whole((length, 2 * HD))] * n
         + sum_specs,
-        out_specs=[per_head] + [whole((length, 2 * HD))] * n,
+        out_specs=[out_head] + [whole((length, 2 * HD))] * n,
         out_shape=[jax.ShapeDtypeStruct((rows, cols), dq_type)]
         + [jax.ShapeDtypeStruct((length, 2 * HD), dkv_type)] * n,
         scratch_shapes=[
@@ -303,7 +306,7 @@
                 else:
                     total[at, :] += part
 
-    hbm = pl.BlockSpec(memory_space=pl.ANY)
+    hbm = pl.BlockSpec(memory_space=pltpu.HBM)
     return pl.pallas_call(
         body,
         in_specs=[pl.BlockSpec(memory_space=pltpu.SMEM)] + [hbm] * (n_x + n_w),
@@ -316,7 +319,7 @@
             pltpu.SemaphoreType.DMA((4,)),
             pltpu.SemaphoreType.DMA((4,)),
         ],
-        compiler_params=pltpu.CompilerParams(vmem_limit_bytes=32 * 2**20),
+        compiler_params=pltpu.CompilerParams(vmem_limit_bytes=56 * 2**20),
         cost_estimate=pl.CostEstimate(
             flops=2 * rows * depth * width,
             bytes_accessed=2 * (rows * depth + depth * width + rows * width),
@@ -364,33 +367,33 @@
     span_ids = [spans_of((group - r) % groups) for r in range(REACH + 1)]
 
     kv = project(x_pieces, lines_place(w_own.shape[0] // 2), kv_lines[0] + kv_lines[1], where)
-    kv1, kv2 = shift(kv, BLK, 1), shift(kv, BLK, 2)
+    kv1 = shift(kv, BLK, 1)
     grads = [lax.dynamic_slice_in_dim(dout_seq, mine[d] * cols, cols, 1) for d in peers]
     *grads, _ = fence(*grads, x_far)
     grads = [to_peer(grads[d], d) for d in peers]
     query = project(x_pieces, planes_place(w_query.shape[0]), [q_weights], where)
-    *grads, query = fence(*grads, query)
+    *grads, kv1, query = fence(*grads, kv1, query)
+    kv2 = shift(kv1, BLK, 1)
     grad_out, delta = prepare(grads, out_heads, mine_all)
 
-    far = slice(2 * rows, 4 * rows)
-    near = slice(0, 2 * rows)
-
-    def part(at, kvs, ids, own, dq_sum, dkv_sums, dq_type, dkv_type):
+    def part(start, count, keys, ids, own, dq_sum, dkv_sum, dq_type, dkv_type):
         return tile_grads(
-            query[at], grad_out[at], lse2[:, :, at], delta[:, :, at],
-            span_ids[0][at.start // SPAN : at.stop // SPAN], jnp.stack(ids), kvs, own,
-            dq_sum, dkv_sums, dq_type, dkv_type,
+            start, count, query, grad_out, lse2, delta, span_ids[0], ids[None], [keys], own,
+            dq_sum, None if dkv_sum is None else [dkv_sum], dq_type, dkv_type,
         )
 
     f32, bf16 = jnp.float32, jnp.bfloat16
-    dq_far, dkv0 = part(far, [kv], span_ids[:1], 0, None, None, f32, f32)
-    dq_far, dkv1, dkv2 = part(far, [kv1, kv2], span_ids[1:], -1, dq_far, None, bf16, f32)
-    dq_near, dkv1, dkv2 = part(near, [kv1, kv2], span_ids[1:], -1, None, [dkv1, dkv2], f32, bf16)
+    half = 2 * rows
+    dq, dkv1 = part(0, 4 * rows, kv1, span_ids[1], -1, None, None, f32, bf16)
+    back1 = shift(dkv1, BLK, -1)
+    dq, dkv2 = part(0, 4 * rows, kv2, span_ids[2], -1, dq, None, f32, bf16)
+    back2 = shift(dkv2, BLK, -2)
+    dq_far, dkv0 = part(half, half, kv, span_ids[0], 0, dq, None, bf16, f32)
     dq2, dq3 = to_peer(dq_far[:rows], 2), to_peer(dq_far[rows:], 3)
-    back1, back2 = shift(dkv1, BLK, -1), shift(dkv2, BLK, -2)
-    dq_near, dkv0 = part(near, [kv], span_ids[:1], 0, dq_near, [dkv0], bf16, f32)
+    dq_near, dkv0 = part(0, half, kv, span_ids[0], 0, dq, dkv0, bf16, f32)
     dq1 = to_peer(dq_near[rows:], 1)
     dkv = (dkv0 + back1.astype(f32) + back2.astype(f32)).astype(bf16)
+    dkv, dq2, dq3 = fence(dkv, dq2, dq3)
     dkvs = [to_peer(dkv[d * rows : (d + 1) * rows], d) for d in peers]
     (grad_query,) = by_head([dq_near[:rows], dq1, dq2, dq3], mine_all, [cols])
     grad_key, grad_value = by_head(dkvs, mine_all, [HD, HD])

time: 231 us -> 197 us (0.85)
  waiting for transfers between devices: 56.9 us -> 39.6 us
  Pallas kernels: 84.6 us -> 74.1 us
  local copies, waits for them, and re-layouts: 10.9 us -> 6.64 us
  starting transfers between devices: 59.9 us -> 56.9 us
    ppermute x12, waiting for transfers between devices: 26.3 us -> 16.7 us  [to_peer(): lax.ppermute(block, HEAD, [(i, i ^ d) for i in range(4)])]
    ppermute x21, waiting for transfers between devices: 30.6 us -> 22.9 us  [shift(): lax.ppermute(block, axis, [(i, (i + by) % size) for i in range(size)])]
    ppermute x21, starting transfers between devices: 42.6 us -> 36.3 us  [shift(): lax.ppermute(block, axis, [(i, (i + by) % size) for i in range(size)])]
    pallas_call x2, Pallas kernels: 26.9 us -> 20.7 us  [project(): pl.pallas_call(body, in_specs=[pl.BlockSpec(memory_space=pltpu.SMEM)] + [...]
    pallas_call x4, Pallas kernels: 51.3 us -> 47.7 us  [tile_grads(): pl.pallas_call(body, grid=(heads,), in_specs=[smem, smem, per_head, per_h...]
    unnamed x69 -> x55, local copies, waits for them, and re-layouts: 6.38 us -> 2.94 us
    ppermute x12, starting transfers between devices: 17.2 us -> 20.6 us  [to_peer(): lax.ppermute(block, HEAD, [(i, i ^ d) for i in range(4)])]
  transfers between devices with their start and end apart: 34 -> 34, of which waited for: 11 -> 11; matrix products, arithmetic and copies ran while one was open for 2% -> 3% of each run, Pallas kernels for 22% -> 37%
where the time goes in v3:
time: 197 us; the launch traced here: 196 us
  Pallas kernels  74.1 us (38%)
  starting transfers between devices  56.9 us (29%)
  waiting for transfers between devices  39.6 us (20%)
  between operations  14.6 us (7%)
  local copies, waits for them, and re-layouts  6.64 us (3%)
  other arithmetic  3.95 us (2%)
    pallas_call x4, Pallas kernels, tile_grads(): pl.pallas_call(body, grid=(heads,), in_specs=[smem, smem, per_head, per_h...  47.7 us
    ppermute x21, starting transfers between devices, shift(): lax.ppermute(block, axis, [(i, (i + by) % size) for i in range(size)])  36.3 us
    ppermute x21, waiting for transfers between devices, shift(): lax.ppermute(block, axis, [(i, (i + by) % size) for i in range(size)])  22.9 us
    pallas_call x2, Pallas kernels, project(): pl.pallas_call(body, in_specs=[pl.BlockSpec(memory_space=pltpu.SMEM)] + [...  20.7 us
    ppermute x12, starting transfers between devices, to_peer(): lax.ppermute(block, HEAD, [(i, i ^ d) for i in range(4)])  20.6 us
    ppermute x12, waiting for transfers between devices, to_peer(): lax.ppermute(block, HEAD, [(i, i ^ d) for i in range(4)])  16.7 us
    pallas_call x2, Pallas kernels, by_head(): pl.pallas_call(body, in_specs=[pl.BlockSpec(memory_space=pltpu.SMEM)] + [...  4.43 us
  transfers between devices with their start and end apart: 34, of which 11 were waited for; matrix products, arithmetic and copies ran while one was open for 3% of the time, Pallas kernels for 37%

profile of v3, /device:TPU:1, one launch (start us, length us, event | category | flops | bytes accessed | tf_op | source)
XLA Modules:
  0.0 195.9 jit_solution(15358787596492492147)
XLA Ops:
  7.2 1.0 pad_maximum_fusion.1
  8.2 3.8 %collective-permute-start = (bf16[160,896]{1,0:T(8,128)(2,1)S(1)}, bf16[160,896]{1,0:T(8,128)(2,1)S(1)}, u32[]{:S(2)}, u32[]{:S(2)}) collective-permute-start(bf16[160,896]{1,0:T(8,128)(2,1)S(1)} %pad_maximum_fusion.1), channel_id=1, source_target_pairs={{0,4},{4,0},{1,5},{5,1},{2,6},{6,2},{3,7},{7,3},{8,12},{12,8},{9,1... | collective-permute-start | bytes 860168 | tf_op jit(solution)/shard_map/ppermute | solution.py:189
  12.0 6.3 %collective-permute-done = bf16[160,896]{1,0:T(8,128)(2,1)S(1)} collective-permute-done((bf16[160,896]{1,0:T(8,128)(2,1)S(1)}, bf16[160,896]{1,0:T(8,128)(2,1)S(1)}, u32[]{:S(2)}, u32[]{:S(2)}) %collective-permute-start) | collective-permute-done | bytes 286752 | tf_op jit(solution)/shard_map/ppermute | solution.py:189
  18.4 1.8 pad_maximum_fusion
  20.2 1.4 collective-permute-start.1
  21.6 0.8 constant_dynamic-update-slice_fusion.1
  22.4 0.8 constant_dynamic-update-slice_fusion
  23.2 1.7 collective-permute-start.2
  24.9 2.2 %collective-permute-start.3 = (bf16[160,256]{1,0:T(8,128)(2,1)S(1)}, bf16[160,256]{1,0:T(8,128)(2,1)S(1)}, u32[]{:S(2)}, u32[]{:S(2)}) collective-permute-start(bf16[160,256]{1,0:T(8,128)(2,1)S(1)} %pad_maximum_fusion.2), channel_id=1, source_target_pairs={{0,3},{1,0},{2,1},{3,2},{4,7},{5,4},{6,5},{7,6},{8,11},{9,8},{10,9... | collective-permute-start | bytes 245768 | tf_op jit(solution)/shard_map/ppermute | solution.py:189
  27.1 1.2 collective-permute-start.4
  28.4 1.5 collective-permute-start.5
  29.8 1.8 collective-permute-done.4
  32.1 2.7 %collective-permute-start.7 = (bf16[80,256]{1,0:T(8,128)(2,1)S(1)}, bf16[80,256]{1,0:T(8,128)(2,1)S(1)}, u32[]{:S(2)}, u32[]{:S(2)}) collective-permute-start(bf16[80,256]{1,0:T(8,128)(2,1)S(1)} %slice.74), channel_id=1, source_target_pairs={{0,3},{1,0},{2,1},{3,2},{4,7},{5,4},{6,5},{7,6},{8,11},{9,8},{10,9... | collective-permute-start | bytes 122888 | tf_op jit(solution)/shard_map/ppermute | solution.py:189
  34.7 1.2 collective-permute-start.8
  36.0 1.5 collective-permute-start.9
  37.5 2.3 %collective-permute-done.8 = bf16[80,256]{1,0:T(8,128)(2,1)S(1)} collective-permute-done((bf16[80,256]{1,0:T(8,128)(2,1)S(1)}, bf16[80,256]{1,0:T(8,128)(2,1)S(1)}, u32[]{:S(2)}, u32[]{:S(2)}) %collective-permute-start.8) | collective-permute-done | bytes 40992 | tf_op jit(solution)/shard_map/ppermute | solution.py:189
  39.8 1.0 collective-permute-start.10
  40.7 1.8 collective-permute-start.11
  42.6 2.7 %collective-permute-start.13 = (bf16[640,256]{1,0:T(8,128)(2,1)S(1)}, bf16[640,256]{1,0:T(8,128)(2,1)S(1)}, u32[]{:S(2)}, u32[]{:S(2)}) collective-permute-start(bf16[640,256]{1,0:T(8,128)(2,1)S(1)} %constant_dynamic-update-slice_fusion.8.refs_9_), channel_id=1, source_target_pairs={{0,3},{1,0},{2,1},{3,2},{4,7},{5,4},{6,5},{7,6},{8,11},{9,8},{10,9... | collective-permute-start | bytes 983048 | tf_op jit(solution)/shard_map/ppermute | solution.py:189
  45.3 6.1 %collective-permute-done.10.refs_5_ = bf16[640,256]{1,0:T(8,128)(2,1)S(1)} collective-permute-done((bf16[640,256]{1,0:T(8,128)(2,1)S(1)}, bf16[640,256]{1,0:T(8,128)(2,1)S(1)}, u32[]{:S(2)}, u32[]{:S(2)}) %collective-permute-start.10) | collective-permute-done | bytes 327712 | tf_op jit(solution)/shard_map/ppermute | solution.py:189
  51.8 2.7 %collective-permute-start.15 = (bf16[320,256]{1,0:T(8,128)(2,1)S(1)}, bf16[320,256]{1,0:T(8,128)(2,1)S(1)}, u32[]{:S(2)}, u32[]{:S(2)}) collective-permute-start(bf16[320,256]{1,0:T(8,128)(2,1)S(1)} %slice.78), channel_id=1, source_target_pairs={{0,24},{8,0},{16,8},{24,16},{1,25},{9,1},{17,9},{25,17},{2,26},{10... | collective-permute-start | bytes 491528 | tf_op jit(solution)/shard_map/ppermute | solution.py:189
  54.7 2.7 %collective-permute-start.17 = (bf16[320,256]{1,0:T(8,128)(2,1)S(1)}, bf16[320,256]{1,0:T(8,128)(2,1)S(1)}, u32[]{:S(2)}, u32[]{:S(2)}) collective-permute-start(bf16[320,256]{1,0:T(8,128)(2,1)S(1)} %slice.80), channel_id=1, source_target_pairs={{0,3},{1,0},{2,1},{3,2},{4,7},{5,4},{6,5},{7,6},{8,11},{9,8},{10,9... | collective-permute-start | bytes 491528 | tf_op jit(solution)/shard_map/ppermute | solution.py:189
  57.4 9.3 %collective-permute-start.21 = (bf16[256,5120]{1,0:T(8,128)(2,1)}, bf16[256,5120]{1,0:T(8,128)(2,1)}, u32[]{:S(2)}, u32[]{:S(2)}) collective-permute-start(bf16[256,5120]{1,0:T(8,128)(2,1)} %refs_0_.3), channel_id=1, source_target_pairs={{0,32},{32,0},{64,96},{96,64},{1,33},{33,1},{65,97},{97,65},{2,34}... | collective-permute-start | bytes 7864328 | tf_op jit(solution)/shard_map/ppermute | solution.py:193
  67.3 10.1 %collective-permute-done.1.refs_2_ = bf16[256,5120]{1,0:T(8,128)(2,1)} collective-permute-done((bf16[256,5120]{1,0:T(8,128)(2,1)}, bf16[256,5120]{1,0:T(8,128)(2,1)}, u32[]{:S(2)}, u32[]{:S(2)}) %collective-permute-start.1) | collective-permute-done | bytes 2621472 | tf_op jit(solution)/shard_map/ppermute | solution.py:193
  77.5 2.4 %collective-permute-start.22 = (bf16[256,5120]{1,0:T(8,128)(2,1)}, bf16[256,5120]{1,0:T(8,128)(2,1)}, u32[]{:S(2)}, u32[]{:S(2)}) collective-permute-start(bf16[256,5120]{1,0:T(8,128)(2,1)} %collective-permute-done.1.refs_2_), channel_id=1, source_target_pairs={{0,32},{32,0},{64,96},{96,64},{1,33},{33,1},{65,97},{97,65},{2,34}... | collective-permute-start | bytes 7864328 | tf_op jit(solution)/shard_map/ppermute | solution.py:193
  81.1 1.0 constant_dynamic-slice_fusion
  82.3 1.3 collective-permute-start.19
  83.6 0.7 collective-permute-start.20
  84.8 7.3 %shard_map.103.rest_0_ = bf16[1024,256]{1,0:T(8,128)(2,1)} custom-call(s32[3]{0:T(128)} %pad_add_fusion.2.where_ref, bf16[256,5120]{1,0:T(8,128)(2,1)} %refs_0_.3, bf16[256,5120]{1,0:T(8,128)(2,1)} %collective-permute-done.21.refs_1_, bf16[256,5120]{1,0:T(8,128)(2,1)} %collective-permute-done.1.refs_2_, bf16[256,5120]{1,0:T(8,128)(2,1)} %collective-permute-done.22.refs_3_, ...), custom_call_target="tpu_custom_call" | custom-call | flops 2684354560 | bytes 13631488 | tf_op jit(solution)/shard_map/pallas_call | solution.py:310
  92.1 1.9 collective-permute-start.23
  94.0 13.4 %shard_map.104.q_ref = bf16[1024,640]{1,0:T(8,128)(2,1)} custom-call(s32[3]{0:T(128)} %pad_add_fusion.2.where_ref, bf16[256,5120]{1,0:T(8,128)(2,1)} %refs_0_.3, bf16[256,5120]{1,0:T(8,128)(2,1)} %collective-permute-done.21.refs_1_, bf16[256,5120]{1,0:T(8,128)(2,1)} %collective-permute-done.1.refs_2_, bf16[256,5120]{1,0:T(8,128)(2,1)} %collective-permute-done.22.refs_3_, ...), custom_call_target="tpu_custom_call" | custom-call | flops 6710886400 | bytes 18350080 | tf_op jit(solution)/shard_map/pallas_call | solution.py:310
  107.5 5.7 %collective-permute-done.23.rest_0_ = bf16[1024,256]{1,0:T(8,128)(2,1)S(1)} collective-permute-done((bf16[1024,256]{1,0:T(8,128)(2,1)}, bf16[1024,256]{1,0:T(8,128)(2,1)S(1)}, u32[]{:S(2)}, u32[]{:S(2)}) %collective-permute-start.23) | collective-permute-done | bytes 524320 | tf_op jit(solution)/shard_map/ppermute | solution.py:189
  113.2 1.3 shard_map.105
  114.5 14.9 %shard_map.106 = (f32[1024,640]{1,0:T(8,128)S(1)}, bf16[1024,256]{1,0:T(8,128)(2,1)S(1)}) custom-call(s32[8]{0:T(128)S(1)} %pad_add_fusion.1.qspan_ref, s32[1,8]{1,0:T(1,128)S(1)} %add_bitcast_fusion.1.kspan_ref, bf16[1024,640]{1,0:T(8,128)(2,1)S(1)} %copy-done.3, bf16[1024,640]{1,0:T(8,128)(2,1)S(1)} %get-tuple-element.93.g_ref, ...), custom_call_target="tpu_custom_call" | custom-call | flops 6710886400 | bytes 6815744 | tf_op jit(solution)/shard_map/pallas_call | solution.py:108
  129.5 7.5 %collective-permute-start.26 = (bf16[1024,256]{1,0:T(8,128)(2,1)S(1)}, bf16[1024,256]{1,0:T(8,128)(2,1)S(1)}, u32[]{:S(2)}, u32[]{:S(2)}) collective-permute-start(bf16[1024,256]{1,0:T(8,128)(2,1)S(1)} %get-tuple-element.101), channel_id=1, source_target_pairs={{0,31},{1,0},{2,1},{3,2},{4,3},{5,4},{6,5},{7,6},{8,7},{9,8},{10,9... | collective-permute-start | bytes 1572872 | tf_op jit(solution)/shard_map/ppermute | solution.py:189
  136.9 15.0 %shard_map.107 = (f32[1024,640]{1,0:T(8,128)S(1)}, bf16[1024,256]{1,0:T(8,128)(2,1)S(1)}) custom-call(s32[8]{0:T(128)S(1)} %pad_add_fusion.1.qspan_ref, s32[1,8]{1,0:T(1,128)S(1)} %add_bitcast_fusion.kspan_ref, bf16[1024,640]{1,0:T(8,128)(2,1)S(1)} %copy-done.3, bf16[1024,640]{1,0:T(8,128)(2,1)S(1)} %get-tuple-element.93.g_ref, ...), custom_call_target="tpu_custom_call" | custom-call | flops 6710886400 | bytes 6815744 | tf_op jit(solution)/shard_map/pallas_call | solution.py:108
  152.1 8.9 %shard_map.108 = (bf16[512,640]{1,0:T(8,128)(2,1)S(1)}, f32[1024,256]{1,0:T(8,128)S(1)}) custom-call(s32[8]{0:T(128)S(1)} %pad_add_fusion.1.qspan_ref, s32[1,8]{1,0:T(1,128)S(1)} %bitcast.20, bf16[1024,640]{1,0:T(8,128)(2,1)S(1)} %copy-done.3, bf16[1024,640]{1,0:T(8,128)(2,1)S(1)} %get-tuple-element.93.g_ref, f32[5,1,1024]{2,1,0:T(1,128)S(1)} %broadcast_in_dim.14.lse_ref, ...), custom_call_target="tpu_custom_call" | custom-call | flops 3355443200 | bytes 4194304 | tf_op jit(solution)/shard_map/pallas_call | solution.py:108
  161.5 2.8 %collective-permute-start.29 = (bf16[256,640]{1,0:T(8,128)(2,1)S(1)}, bf16[256,640]{1,0:T(8,128)(2,1)S(1)}, u32[]{:S(2)}, u32[]{:S(2)}) collective-permute-start(bf16[256,640]{1,0:T(8,128)(2,1)S(1)} %get-tuple-element.113), channel_id=1, source_target_pairs={{0,96},{32,64},{64,32},{96,0},{1,97},{33,65},{65,33},{97,1},{2,98}... | collective-permute-start | bytes 983048 | tf_op jit(solution)/shard_map/ppermute | solution.py:193
  164.2 8.8 %shard_map.109 = (bf16[512,640]{1,0:T(8,128)(2,1)S(1)}, f32[1024,256]{1,0:T(8,128)S(1)}) custom-call(s32[8]{0:T(128)S(1)} %pad_add_fusion.1.qspan_ref, s32[1,8]{1,0:T(1,128)S(1)} %bitcast.21, bf16[1024,640]{1,0:T(8,128)(2,1)S(1)} %copy-done.3, bf16[1024,640]{1,0:T(8,128)(2,1)S(1)} %get-tuple-element.93.g_ref, f32[5,1,1024]{2,1,0:T(1,128)S(1)} %broadcast_in_dim.14.lse_ref, ...), custom_call_target="tpu_custom_call" | custom-call | flops 3355443200 | bytes 4194304 | tf_op jit(solution)/shard_map/pallas_call | solution.py:108
  173.1 0.8 fusion.1
  174.1 3.4 %collective-permute-done.29.refs_3_ = bf16[256,640]{1,0:T(8,128)(2,1)S(1)} collective-permute-done((bf16[256,640]{1,0:T(8,128)(2,1)S(1)}, bf16[256,640]{1,0:T(8,128)(2,1)S(1)}, u32[]{:S(2)}, u32[]{:S(2)}) %collective-permute-start.29) | collective-permute-done | bytes 327712 | tf_op jit(solution)/shard_map/ppermute | solution.py:193
  177.5 0.8 fusion.2
  178.9 1.5 collective-permute-start.32
  180.5 0.7 copy-done.13
  181.2 2.4 %shard_map.110 = bf16[256,2560]{1,0:T(8,128)(2,1)} custom-call(s32[4]{0:T(128)} %copy-done.2, bf16[256,640]{1,0:T(8,128)(2,1)} %get-tuple-element.116.refs_0_, bf16[256,640]{1,0:T(8,128)(2,1)} %copy-done.13, bf16[256,640]{1,0:T(8,128)(2,1)} %copy-done.11, bf16[256,640]{1,0:T(8,128)(2,1)} %copy-done.12), custom_call_target="tpu_custom_call" | custom-call | bytes 2621440 | tf_op jit(solution)/shard_map/pallas_call | solution.py:176
  183.7 2.7 %collective-permute-done.32.refs_3_ = bf16[256,256]{1,0:T(8,128)(2,1)S(1)} collective-permute-done((bf16[256,256]{1,0:T(8,128)(2,1)S(1)}, bf16[256,256]{1,0:T(8,128)(2,1)S(1)}, u32[]{:S(2)}, u32[]{:S(2)}) %collective-permute-start.32) | collective-permute-done | bytes 131104 | tf_op jit(solution)/shard_map/ppermute | solution.py:193
  186.4 0.7 copy-done.20
  187.0 2.0 %shard_map.111 = (bf16[256,512]{1,0:T(8,128)(2,1)}, bf16[256,512]{1,0:T(8,128)(2,1)}) custom-call(s32[4]{0:T(128)} %copy-done.2, bf16[256,256]{1,0:T(8,128)(2,1)} %get-tuple-element.120.refs_0_, bf16[256,256]{1,0:T(8,128)(2,1)} %copy-done.18, bf16[256,256]{1,0:T(8,128)(2,1)} %copy-done.19, bf16[256,256]{1,0:T(8,128)(2,1)} %copy-done.20), custom_call_target="tpu_custom_call" | custom-call | bytes 1048576 | tf_op jit(solution)/shard_map/pallas_call | solution.py:176
  (116 shorter events, 5.1 us)
Async XLA Ops:
  7.2 86.9 %all-gather.2.cloned.1.call-start = ((), (), s32[]{:S(2)}) async-start(), calls=%async_computation | async-start | bytes 6963200 | tf_op jit(solution)/shard_map/all_gather | solution.py:345
  8.2 10.1 %collective-permute-start = (bf16[160,896]{1,0:T(8,128)(2,1)S(1)}, bf16[160,896]{1,0:T(8,128)(2,1)S(1)}, u32[]{:S(2)}, u32[]{:S(2)}) collective-permute-start(bf16[160,896]{1,0:T(8,128)(2,1)S(1)} %pad_maximum_fusion.1), channel_id=1, source_target_pairs={{0,4},{4,0},{1,5},{5,1},{2,6},{6,2},{3,7},{7,3},{8,12},{12,8},{9,1... | collective-permute-start | bytes 860168 | tf_op jit(solution)/shard_map/ppermute | solution.py:189
  18.3 61.6 %copy-start.22 = (f32[1024,5]{0,1:T(8,128)S(1)}, f32[1024,5]{0,1:T(8,128)}, u32[]{:S(2)}) copy-start(f32[1024,5]{0,1:T(8,128)} %param.14) | copy-start | bytes 61444
  18.3 62.5 %copy-start.21 = (s32[256]{0:T(256)S(1)}, s32[256]{0:T(256)}, u32[]{:S(2)}) copy-start(s32[256]{0:T(256)} %param.15) | copy-start | bytes 3076
  18.3 62.8 %copy-start.4 = (bf16[256,2560]{1,0:T(8,128)(2,1)S(1)}, bf16[256,2560]{1,0:T(8,128)(2,1)}, u32[]{:S(2)}) copy-start(bf16[256,2560]{1,0:T(8,128)(2,1)} %param.12) | copy-start | bytes 3932164
  20.2 57.2 %collective-permute-start.1 = (bf16[256,5120]{1,0:T(8,128)(2,1)}, bf16[256,5120]{1,0:T(8,128)(2,1)}, u32[]{:S(2)}, u32[]{:S(2)}) collective-permute-start(bf16[256,5120]{1,0:T(8,128)(2,1)} %refs_0_.3), channel_id=1, source_target_pairs={{0,64},{32,96},{64,0},{96,32},{1,65},{33,97},{65,1},{97,33},{2,66}... | collective-permute-start | bytes 7864328 | tf_op jit(solution)/shard_map/ppermute | solution.py:193
  23.2 6.6 %collective-permute-start.2 = (bf16[160,256]{1,0:T(8,128)(2,1)S(1)}, bf16[160,256]{1,0:T(8,128)(2,1)S(1)}, u32[]{:S(2)}, u32[]{:S(2)}) collective-permute-start(bf16[160,256]{1,0:T(8,128)(2,1)S(1)} %pad_maximum_fusion.2), channel_id=1, source_target_pairs={{0,1},{1,2},{2,3},{3,0},{4,5},{5,6},{6,7},{7,4},{8,9},{9,10},{10,1... | collective-permute-start | bytes 245768 | tf_op jit(solution)/shard_map/ppermute | solution.py:189
  24.9 4.9 %collective-permute-start.3 = (bf16[160,256]{1,0:T(8,128)(2,1)S(1)}, bf16[160,256]{1,0:T(8,128)(2,1)S(1)}, u32[]{:S(2)}, u32[]{:S(2)}) collective-permute-start(bf16[160,256]{1,0:T(8,128)(2,1)S(1)} %pad_maximum_fusion.2), channel_id=1, source_target_pairs={{0,3},{1,0},{2,1},{3,2},{4,7},{5,4},{6,5},{7,6},{8,11},{9,8},{10,9... | collective-permute-start | bytes 245768 | tf_op jit(solution)/shard_map/ppermute | solution.py:189
  27.1 4.5 %collective-permute-start.4 = (bf16[160,256]{1,0:T(8,128)(2,1)S(1)}, bf16[160,256]{1,0:T(8,128)(2,1)S(1)}, u32[]{:S(2)}, u32[]{:S(2)}) collective-permute-start(bf16[160,256]{1,0:T(8,128)(2,1)S(1)} %pad_maximum_fusion.3), channel_id=1, source_target_pairs={{0,8},{8,16},{16,24},{24,0},{1,9},{9,17},{17,25},{25,1},{2,10},{10... | collective-permute-start | bytes 245768 | tf_op jit(solution)/shard_map/ppermute | solution.py:189
  28.4 3.7 %collective-permute-start.5 = (bf16[160,256]{1,0:T(8,128)(2,1)S(1)}, bf16[160,256]{1,0:T(8,128)(2,1)S(1)}, u32[]{:S(2)}, u32[]{:S(2)}) collective-permute-start(bf16[160,256]{1,0:T(8,128)(2,1)S(1)} %pad_maximum_fusion.3), channel_id=1, source_target_pairs={{0,24},{8,0},{16,8},{24,16},{1,25},{9,1},{17,9},{25,17},{2,26},{10... | collective-permute-start | bytes 245768 | tf_op jit(solution)/shard_map/ppermute | solution.py:189
  32.1 5.4 %collective-permute-start.6 = (bf16[80,256]{1,0:T(8,128)(2,1)S(1)}, bf16[80,256]{1,0:T(8,128)(2,1)S(1)}, u32[]{:S(2)}, u32[]{:S(2)}) collective-permute-start(bf16[80,256]{1,0:T(8,128)(2,1)S(1)} %slice.73), channel_id=1, source_target_pairs={{0,1},{1,2},{2,3},{3,0},{4,5},{5,6},{6,7},{7,4},{8,9},{9,10},{10,1... | collective-permute-start | bytes 122888 | tf_op jit(solution)/shard_map/ppermute | solution.py:189
  32.1 5.4 %collective-permute-start.7 = (bf16[80,256]{1,0:T(8,128)(2,1)S(1)}, bf16[80,256]{1,0:T(8,128)(2,1)S(1)}, u32[]{:S(2)}, u32[]{:S(2)}) collective-permute-start(bf16[80,256]{1,0:T(8,128)(2,1)S(1)} %slice.74), channel_id=1, source_target_pairs={{0,3},{1,0},{2,1},{3,2},{4,7},{5,4},{6,5},{7,6},{8,11},{9,8},{10,9... | collective-permute-start | bytes 122888 | tf_op jit(solution)/shard_map/ppermute | solution.py:189
  34.7 5.0 %collective-permute-start.8 = (bf16[80,256]{1,0:T(8,128)(2,1)S(1)}, bf16[80,256]{1,0:T(8,128)(2,1)S(1)}, u32[]{:S(2)}, u32[]{:S(2)}) collective-permute-start(bf16[80,256]{1,0:T(8,128)(2,1)S(1)} %slice.75), channel_id=1, source_target_pairs={{0,8},{8,16},{16,24},{24,0},{1,9},{9,17},{17,25},{25,1},{2,10},{10... | collective-permute-start | bytes 122888 | tf_op jit(solution)/shard_map/ppermute | solution.py:189
  36.0 3.8 %collective-permute-start.9 = (bf16[80,256]{1,0:T(8,128)(2,1)S(1)}, bf16[80,256]{1,0:T(8,128)(2,1)S(1)}, u32[]{:S(2)}, u32[]{:S(2)}) collective-permute-start(bf16[80,256]{1,0:T(8,128)(2,1)S(1)} %slice.76), channel_id=1, source_target_pairs={{0,24},{8,0},{16,8},{24,16},{1,25},{9,1},{17,9},{25,17},{2,26},{10... | collective-permute-start | bytes 122888 | tf_op jit(solution)/shard_map/ppermute | solution.py:189
  39.7 11.9 %copy-start.10 = (bf16[640,256]{1,0:T(8,128)(2,1)}, bf16[640,256]{1,0:T(8,128)(2,1)S(1)}, u32[]{:S(2)}) copy-start(bf16[640,256]{1,0:T(8,128)(2,1)S(1)} %constant_dynamic-update-slice_fusion.2.refs_4_) | copy-start | bytes 983044
  39.8 11.6 %collective-permute-start.10 = (bf16[640,256]{1,0:T(8,128)(2,1)S(1)}, bf16[640,256]{1,0:T(8,128)(2,1)S(1)}, u32[]{:S(2)}, u32[]{:S(2)}) collective-permute-start(bf16[640,256]{1,0:T(8,128)(2,1)S(1)} %constant_dynamic-update-slice_fusion.2.refs_4_), channel_id=1, source_target_pairs={{0,8},{8,16},{16,24},{24,0},{1,9},{9,17},{17,25},{25,1},{2,10},{10... | collective-permute-start | bytes 983048 | tf_op jit(solution)/shard_map/ppermute | solution.py:189
  40.7 10.7 %collective-permute-start.11 = (bf16[640,256]{1,0:T(8,128)(2,1)S(1)}, bf16[640,256]{1,0:T(8,128)(2,1)S(1)}, u32[]{:S(2)}, u32[]{:S(2)}) collective-permute-start(bf16[640,256]{1,0:T(8,128)(2,1)S(1)} %constant_dynamic-update-slice_fusion.2.refs_4_), channel_id=1, source_target_pairs={{0,24},{8,0},{16,8},{24,16},{1,25},{9,1},{17,9},{25,17},{2,26},{10... | collective-permute-start | bytes 983048 | tf_op jit(solution)/shard_map/ppermute | solution.py:189
  42.5 39.8 %copy-start.9 = (bf16[640,256]{1,0:T(8,128)(2,1)}, bf16[640,256]{1,0:T(8,128)(2,1)S(1)}, u32[]{:S(2)}) copy-start(bf16[640,256]{1,0:T(8,128)(2,1)S(1)} %constant_dynamic-update-slice_fusion.8.refs_9_) | copy-start | bytes 983044
  42.5 9.1 %collective-permute-start.12 = (bf16[640,256]{1,0:T(8,128)(2,1)S(1)}, bf16[640,256]{1,0:T(8,128)(2,1)S(1)}, u32[]{:S(2)}, u32[]{:S(2)}) collective-permute-start(bf16[640,256]{1,0:T(8,128)(2,1)S(1)} %constant_dynamic-update-slice_fusion.8.refs_9_), channel_id=1, source_target_pairs={{0,1},{1,2},{2,3},{3,0},{4,5},{5,6},{6,7},{7,4},{8,9},{9,10},{10,1... | collective-permute-start | bytes 983048 | tf_op jit(solution)/shard_map/ppermute | solution.py:189
  42.6 9.1 %collective-permute-start.13 = (bf16[640,256]{1,0:T(8,128)(2,1)S(1)}, bf16[640,256]{1,0:T(8,128)(2,1)S(1)}, u32[]{:S(2)}, u32[]{:S(2)}) collective-permute-start(bf16[640,256]{1,0:T(8,128)(2,1)S(1)} %constant_dynamic-update-slice_fusion.8.refs_9_), channel_id=1, source_target_pairs={{0,3},{1,0},{2,1},{3,2},{4,7},{5,4},{6,5},{7,6},{8,11},{9,8},{10,9... | collective-permute-start | bytes 983048 | tf_op jit(solution)/shard_map/ppermute | solution.py:189
  51.4 33.4 %copy-start.5 = (bf16[640,256]{1,0:T(8,128)(2,1)}, bf16[640,256]{1,0:T(8,128)(2,1)S(1)}, u32[]{:S(2)}) copy-start(bf16[640,256]{1,0:T(8,128)(2,1)S(1)} %collective-permute-done.10.refs_5_) | copy-start | bytes 983044
  51.4 33.4 %copy-start.6 = (bf16[640,256]{1,0:T(8,128)(2,1)}, bf16[640,256]{1,0:T(8,128)(2,1)S(1)}, u32[]{:S(2)}) copy-start(bf16[640,256]{1,0:T(8,128)(2,1)S(1)} %collective-permute-done.11.refs_8_) | copy-start | bytes 983044
  51.7 30.5 %copy-start.7 = (bf16[640,256]{1,0:T(8,128)(2,1)}, bf16[640,256]{1,0:T(8,128)(2,1)S(1)}, u32[]{:S(2)}) copy-start(bf16[640,256]{1,0:T(8,128)(2,1)S(1)} %collective-permute-done.12.refs_10_) | copy-start | bytes 983044
  51.7 30.5 %copy-start.8 = (bf16[640,256]{1,0:T(8,128)(2,1)}, bf16[640,256]{1,0:T(8,128)(2,1)S(1)}, u32[]{:S(2)}) copy-start(bf16[640,256]{1,0:T(8,128)(2,1)S(1)} %collective-permute-done.13.refs_13_) | copy-start | bytes 983044
  51.7 5.7 %collective-permute-start.14 = (bf16[320,256]{1,0:T(8,128)(2,1)S(1)}, bf16[320,256]{1,0:T(8,128)(2,1)S(1)}, u32[]{:S(2)}, u32[]{:S(2)}) collective-permute-start(bf16[320,256]{1,0:T(8,128)(2,1)S(1)} %slice.77), channel_id=1, source_target_pairs={{0,8},{8,16},{16,24},{24,0},{1,9},{9,17},{17,25},{25,1},{2,10},{10... | collective-permute-start | bytes 491528 | tf_op jit(solution)/shard_map/ppermute | solution.py:189
  51.8 14.8 %collective-permute-start.15 = (bf16[320,256]{1,0:T(8,128)(2,1)S(1)}, bf16[320,256]{1,0:T(8,128)(2,1)S(1)}, u32[]{:S(2)}, u32[]{:S(2)}) collective-permute-start(bf16[320,256]{1,0:T(8,128)(2,1)S(1)} %slice.78), channel_id=1, source_target_pairs={{0,24},{8,0},{16,8},{24,16},{1,25},{9,1},{17,9},{25,17},{2,26},{10... | collective-permute-start | bytes 491528 | tf_op jit(solution)/shard_map/ppermute | solution.py:189
  54.6 12.1 %collective-permute-start.16 = (bf16[320,256]{1,0:T(8,128)(2,1)S(1)}, bf16[320,256]{1,0:T(8,128)(2,1)S(1)}, u32[]{:S(2)}, u32[]{:S(2)}) collective-permute-start(bf16[320,256]{1,0:T(8,128)(2,1)S(1)} %slice.79), channel_id=1, source_target_pairs={{0,1},{1,2},{2,3},{3,0},{4,5},{5,6},{6,7},{7,4},{8,9},{9,10},{10,1... | collective-permute-start | bytes 491528 | tf_op jit(solution)/shard_map/ppermute | solution.py:189
  54.7 12.0 %collective-permute-start.17 = (bf16[320,256]{1,0:T(8,128)(2,1)S(1)}, bf16[320,256]{1,0:T(8,128)(2,1)S(1)}, u32[]{:S(2)}, u32[]{:S(2)}) collective-permute-start(bf16[320,256]{1,0:T(8,128)(2,1)S(1)} %slice.80), channel_id=1, source_target_pairs={{0,3},{1,0},{2,1},{3,2},{4,7},{5,4},{6,5},{7,6},{8,11},{9,8},{10,9... | collective-permute-start | bytes 491528 | tf_op jit(solution)/shard_map/ppermute | solution.py:189
  57.4 27.4 %copy-start.14 = (bf16[320,256]{1,0:T(8,128)(2,1)}, bf16[320,256]{1,0:T(8,128)(2,1)S(1)}, u32[]{:S(2)}) copy-start(bf16[320,256]{1,0:T(8,128)(2,1)S(1)} %collective-permute-done.14.refs_6_) | copy-start | bytes 491524
  57.4 26.9 %collective-permute-start.21 = (bf16[256,5120]{1,0:T(8,128)(2,1)}, bf16[256,5120]{1,0:T(8,128)(2,1)}, u32[]{:S(2)}, u32[]{:S(2)}) collective-permute-start(bf16[256,5120]{1,0:T(8,128)(2,1)} %refs_0_.3), channel_id=1, source_target_pairs={{0,32},{32,0},{64,96},{96,64},{1,33},{33,1},{65,97},{97,65},{2,34}... | collective-permute-start | bytes 7864328 | tf_op jit(solution)/shard_map/ppermute | solution.py:193
  67.3 12.5 %copy-start.17 = (bf16[320,256]{1,0:T(8,128)(2,1)}, bf16[320,256]{1,0:T(8,128)(2,1)S(1)}, u32[]{:S(2)}) copy-start(bf16[320,256]{1,0:T(8,128)(2,1)S(1)} %collective-permute-done.17.refs_12_) | copy-start | bytes 491524
  77.5 7.3 %collective-permute-start.22 = (bf16[256,5120]{1,0:T(8,128)(2,1)}, bf16[256,5120]{1,0:T(8,128)(2,1)}, u32[]{:S(2)}, u32[]{:S(2)}) collective-permute-start(bf16[256,5120]{1,0:T(8,128)(2,1)} %collective-permute-done.1.refs_2_), channel_id=1, source_target_pairs={{0,32},{32,0},{64,96},{96,64},{1,33},{33,1},{65,97},{97,65},{2,34}... | collective-permute-start | bytes 7864328 | tf_op jit(solution)/shard_map/ppermute | solution.py:193
  80.8 32.4 %copy-start.2 = (s32[4]{0:T(128)}, s32[4]{0:T(128)S(1)}, u32[]{:S(2)}) copy-start(s32[4]{0:T(128)S(1)} %pad_add_fusion.mine_ref) | copy-start | bytes 52
  82.2 25.3 %collective-permute-start.18 = (bf16[256,640]{1,0:T(8,128)(2,1)}, bf16[256,640]{1,0:T(8,128)(2,1)S(1)}, u32[]{:S(2)}, u32[]{:S(2)}) collective-permute-start(bf16[256,640]{1,0:T(8,128)(2,1)} %get-tuple-element.75), channel_id=1, source_target_pairs={{0,32},{32,0},{64,96},{96,64},{1,33},{33,1},{65,97},{97,65},{2,34}... | collective-permute-start | bytes 983048 | tf_op jit(solution)/shard_map/ppermute | solution.py:193
  82.3 25.1 %collective-permute-start.19 = (bf16[256,640]{1,0:T(8,128)(2,1)}, bf16[256,640]{1,0:T(8,128)(2,1)S(1)}, u32[]{:S(2)}, u32[]{:S(2)}) collective-permute-start(bf16[256,640]{1,0:T(8,128)(2,1)} %get-tuple-element.76), channel_id=1, source_target_pairs={{0,64},{32,96},{64,0},{96,32},{1,65},{33,97},{65,1},{97,33},{2,66}... | collective-permute-start | bytes 983048 | tf_op jit(solution)/shard_map/ppermute | solution.py:193
  83.6 23.8 %collective-permute-start.20 = (bf16[256,640]{1,0:T(8,128)(2,1)}, bf16[256,640]{1,0:T(8,128)(2,1)S(1)}, u32[]{:S(2)}, u32[]{:S(2)}) collective-permute-start(bf16[256,640]{1,0:T(8,128)(2,1)} %get-tuple-element.77), channel_id=1, source_target_pairs={{0,96},{32,64},{64,32},{96,0},{1,97},{33,65},{65,33},{97,1},{2,98}... | collective-permute-start | bytes 983048 | tf_op jit(solution)/shard_map/ppermute | solution.py:193
  92.1 21.1 %copy-start = (bf16[1024,640]{1,0:T(8,128)(2,1)S(1)}, bf16[1024,640]{1,0:T(8,128)(2,1)}, u32[]{:S(2)}) copy-start(bf16[1024,640]{1,0:T(8,128)(2,1)} %refs_4_.1) | copy-start | bytes 3932164
  92.1 21.1 %collective-permute-start.23 = (bf16[1024,256]{1,0:T(8,128)(2,1)}, bf16[1024,256]{1,0:T(8,128)(2,1)S(1)}, u32[]{:S(2)}, u32[]{:S(2)}) collective-permute-start(bf16[1024,256]{1,0:T(8,128)(2,1)} %shard_map.103.rest_0_), channel_id=1, source_target_pairs={{0,1},{1,2},{2,3},{3,4},{4,5},{5,6},{6,7},{7,8},{8,9},{9,10},{10,1... | collective-permute-start | bytes 1572872 | tf_op jit(solution)/shard_map/ppermute | solution.py:189
  113.2 23.7 %collective-permute-start.24 = (bf16[1024,256]{1,0:T(8,128)(2,1)S(1)}, bf16[1024,256]{1,0:T(8,128)(2,1)S(1)}, u32[]{:S(2)}, u32[]{:S(2)}) collective-permute-start(bf16[1024,256]{1,0:T(8,128)(2,1)S(1)} %collective-permute-done.23.rest_0_), channel_id=1, source_target_pairs={{0,1},{1,2},{2,3},{3,4},{4,5},{5,6},{6,7},{7,8},{8,9},{9,10},{10,1... | collective-permute-start | bytes 1572872 | tf_op jit(solution)/shard_map/ppermute | solution.py:189
  129.5 44.4 %collective-permute-start.26 = (bf16[1024,256]{1,0:T(8,128)(2,1)S(1)}, bf16[1024,256]{1,0:T(8,128)(2,1)S(1)}, u32[]{:S(2)}, u32[]{:S(2)}) collective-permute-start(bf16[1024,256]{1,0:T(8,128)(2,1)S(1)} %get-tuple-element.101), channel_id=1, source_target_pairs={{0,31},{1,0},{2,1},{3,2},{4,3},{5,4},{6,5},{7,6},{8,7},{9,8},{10,9... | collective-permute-start | bytes 1572872 | tf_op jit(solution)/shard_map/ppermute | solution.py:189
  136.9 15.1 %copy-start.1 = (bf16[1024,256]{1,0:T(8,128)(2,1)S(1)}, bf16[1024,256]{1,0:T(8,128)(2,1)}, u32[]{:S(2)}) copy-start(bf16[1024,256]{1,0:T(8,128)(2,1)} %shard_map.103.rest_0_) | copy-start | bytes 1572868
  152.0 21.9 %collective-permute-start.27 = (bf16[1024,256]{1,0:T(8,128)(2,1)S(1)}, bf16[1024,256]{1,0:T(8,128)(2,1)S(1)}, u32[]{:S(2)}, u32[]{:S(2)}) collective-permute-start(bf16[1024,256]{1,0:T(8,128)(2,1)S(1)} %get-tuple-element.102), channel_id=1, source_target_pairs={{0,30},{1,31},{2,0},{3,1},{4,2},{5,3},{6,4},{7,5},{8,6},{9,7},{10,... | collective-permute-start | bytes 1572872 | tf_op jit(solution)/shard_map/ppermute | solution.py:189
  161.0 13.1 %collective-permute-start.28 = (bf16[256,640]{1,0:T(8,128)(2,1)S(1)}, bf16[256,640]{1,0:T(8,128)(2,1)S(1)}, u32[]{:S(2)}, u32[]{:S(2)}) collective-permute-start(bf16[256,640]{1,0:T(8,128)(2,1)S(1)} %get-tuple-element.114), channel_id=1, source_target_pairs={{0,64},{32,96},{64,0},{96,32},{1,65},{33,97},{65,1},{97,33},{2,66}... | collective-permute-start | bytes 983048 | tf_op jit(solution)/shard_map/ppermute | solution.py:193
  161.5 16.1 %collective-permute-start.29 = (bf16[256,640]{1,0:T(8,128)(2,1)S(1)}, bf16[256,640]{1,0:T(8,128)(2,1)S(1)}, u32[]{:S(2)}, u32[]{:S(2)}) collective-permute-start(bf16[256,640]{1,0:T(8,128)(2,1)S(1)} %get-tuple-element.113), channel_id=1, source_target_pairs={{0,96},{32,64},{64,32},{96,0},{1,97},{33,65},{65,33},{97,1},{2,98}... | collective-permute-start | bytes 983048 | tf_op jit(solution)/shard_map/ppermute | solution.py:193
  173.9 6.6 %collective-permute-start.25 = (bf16[256,640]{1,0:T(8,128)(2,1)S(1)}, bf16[256,640]{1,0:T(8,128)(2,1)S(1)}, u32[]{:S(2)}, u32[]{:S(2)}) collective-permute-start(bf16[256,640]{1,0:T(8,128)(2,1)S(1)} %get-tuple-element.115), channel_id=1, source_target_pairs={{0,32},{32,0},{64,96},{96,64},{1,33},{33,1},{65,97},{97,65},{2,34}... | collective-permute-start | bytes 983048 | tf_op jit(solution)/shard_map/ppermute | solution.py:193
  178.3 5.3 %collective-permute-start.30 = (bf16[256,256]{1,0:T(8,128)(2,1)S(1)}, bf16[256,256]{1,0:T(8,128)(2,1)S(1)}, u32[]{:S(2)}, u32[]{:S(2)}) collective-permute-start(bf16[256,256]{1,0:T(8,128)(2,1)S(1)} %get-tuple-element.119), channel_id=1, source_target_pairs={{0,32},{32,0},{64,96},{96,64},{1,33},{33,1},{65,97},{97,65},{2,34}... | collective-permute-start | bytes 393224 | tf_op jit(solution)/shard_map/ppermute | solution.py:193
  178.3 5.3 %collective-permute-start.31 = (bf16[256,256]{1,0:T(8,128)(2,1)S(1)}, bf16[256,256]{1,0:T(8,128)(2,1)S(1)}, u32[]{:S(2)}, u32[]{:S(2)}) collective-permute-start(bf16[256,256]{1,0:T(8,128)(2,1)S(1)} %get-tuple-element.118), channel_id=1, source_target_pairs={{0,64},{32,96},{64,0},{96,32},{1,65},{33,97},{65,1},{97,33},{2,66}... | collective-permute-start | bytes 393224 | tf_op jit(solution)/shard_map/ppermute | solution.py:193
  178.9 7.4 %collective-permute-start.32 = (bf16[256,256]{1,0:T(8,128)(2,1)S(1)}, bf16[256,256]{1,0:T(8,128)(2,1)S(1)}, u32[]{:S(2)}, u32[]{:S(2)}) collective-permute-start(bf16[256,256]{1,0:T(8,128)(2,1)S(1)} %get-tuple-element.117), channel_id=1, source_target_pairs={{0,96},{32,64},{64,32},{96,0},{1,97},{33,65},{65,33},{97,1},{2,98}... | collective-permute-start | bytes 393224 | tf_op jit(solution)/shard_map/ppermute | solution.py:193
  (9 other events, 34.7 us)
Sparse Core Ops, SparseCore 0:
  20.3 69.2 all-gather.1

commit v4 on v3

--- a/solution.py
+++ b/solution.py
@@ -372,9 +372,10 @@
     *grads, _ = fence(*grads, x_far)
     grads = [to_peer(grads[d], d) for d in peers]
     query = project(x_pieces, planes_place(w_query.shape[0]), [q_weights], where)
-    *grads, kv1, query = fence(*grads, kv1, query)
+    *grads, query = fence(*grads, query)
+    grad_out, delta = prepare(grads, out_heads, mine_all)
+    kv1, delta = fence(kv1, delta)
     kv2 = shift(kv1, BLK, 1)
-    grad_out, delta = prepare(grads, out_heads, mine_all)
 
     def part(start, count, keys, ids, own, dq_sum, dkv_sum, dq_type, dkv_type):
         return tile_grads(

time: 197 us -> 197 us (level)
  transfers between devices with their start and end apart: 34 -> 34, of which waited for: 11 -> 10; matrix products, arithmetic and copies ran while one was open for 3% -> 3% of each run, Pallas kernels for 37% -> 37%
where the time goes in v4:
time: 197 us; the launch traced here: 196 us
  Pallas kernels  74.1 us (38%)
  starting transfers between devices  56.2 us (29%)
  waiting for transfers between devices  40.1 us (20%)
  between operations  14.6 us (7%)
  local copies, waits for them, and re-layouts  6.64 us (3%)
  other arithmetic  3.96 us (2%)
    pallas_call x4, Pallas kernels, tile_grads(): pl.pallas_call(body, grid=(heads,), in_specs=[smem, smem, per_head, per_h...  47.6 us
    ppermute x21, starting transfers between devices, shift(): lax.ppermute(block, axis, [(i, (i + by) % size) for i in range(size)])  37.4 us
    ppermute x21, waiting for transfers between devices, shift(): lax.ppermute(block, axis, [(i, (i + by) % size) for i in range(size)])  22.3 us
    pallas_call x2, Pallas kernels, project(): pl.pallas_call(body, in_specs=[pl.BlockSpec(memory_space=pltpu.SMEM)] + [...  20.7 us
    ppermute x12, starting transfers between devices, to_peer(): lax.ppermute(block, HEAD, [(i, i ^ d) for i in range(4)])  18.8 us
    ppermute x12, waiting for transfers between devices, to_peer(): lax.ppermute(block, HEAD, [(i, i ^ d) for i in range(4)])  17.8 us
    pallas_call x2, Pallas kernels, by_head(): pl.pallas_call(body, in_specs=[pl.BlockSpec(memory_space=pltpu.SMEM)] + [...  4.43 us
  transfers between devices with their start and end apart: 34, of which 10 were waited for; matrix products, arithmetic and copies ran while one was open for 3% of the time, Pallas kernels for 37%

profile of v4, /device:TPU:1, one launch (start us, length us, event | category | flops | bytes accessed | tf_op | source)
XLA Modules:
  0.0 195.6 jit_solution(6095252762686489880)
XLA Ops:
  7.2 1.0 pad_maximum_fusion.1
  8.2 3.8 %collective-permute-start = (bf16[160,896]{1,0:T(8,128)(2,1)S(1)}, bf16[160,896]{1,0:T(8,128)(2,1)S(1)}, u32[]{:S(2)}, u32[]{:S(2)}) collective-permute-start(bf16[160,896]{1,0:T(8,128)(2,1)S(1)} %pad_maximum_fusion.1), channel_id=1, source_target_pairs={{0,4},{4,0},{1,5},{5,1},{2,6},{6,2},{3,7},{7,3},{8,12},{12,8},{9,1... | collective-permute-start | bytes 860168 | tf_op jit(solution)/shard_map/ppermute | solution.py:189
  12.0 6.3 %collective-permute-done = bf16[160,896]{1,0:T(8,128)(2,1)S(1)} collective-permute-done((bf16[160,896]{1,0:T(8,128)(2,1)S(1)}, bf16[160,896]{1,0:T(8,128)(2,1)S(1)}, u32[]{:S(2)}, u32[]{:S(2)}) %collective-permute-start) | collective-permute-done | bytes 286752 | tf_op jit(solution)/shard_map/ppermute | solution.py:189
  18.4 1.8 pad_maximum_fusion
  20.2 1.4 collective-permute-start.1
  21.6 0.8 constant_dynamic-update-slice_fusion.1
  22.4 0.8 constant_dynamic-update-slice_fusion
  23.2 1.7 collective-permute-start.2
  24.9 2.2 %collective-permute-start.3 = (bf16[160,256]{1,0:T(8,128)(2,1)S(1)}, bf16[160,256]{1,0:T(8,128)(2,1)S(1)}, u32[]{:S(2)}, u32[]{:S(2)}) collective-permute-start(bf16[160,256]{1,0:T(8,128)(2,1)S(1)} %pad_maximum_fusion.2), channel_id=1, source_target_pairs={{0,3},{1,0},{2,1},{3,2},{4,7},{5,4},{6,5},{7,6},{8,11},{9,8},{10,9... | collective-permute-start | bytes 245768 | tf_op jit(solution)/shard_map/ppermute | solution.py:189
  27.1 1.2 collective-permute-start.4
  28.4 1.5 collective-permute-start.5
  29.8 1.8 collective-permute-done.4
  32.1 2.7 %collective-permute-start.7 = (bf16[80,256]{1,0:T(8,128)(2,1)S(1)}, bf16[80,256]{1,0:T(8,128)(2,1)S(1)}, u32[]{:S(2)}, u32[]{:S(2)}) collective-permute-start(bf16[80,256]{1,0:T(8,128)(2,1)S(1)} %slice.74), channel_id=1, source_target_pairs={{0,3},{1,0},{2,1},{3,2},{4,7},{5,4},{6,5},{7,6},{8,11},{9,8},{10,9... | collective-permute-start | bytes 122888 | tf_op jit(solution)/shard_map/ppermute | solution.py:189
  34.7 1.2 collective-permute-start.8
  36.0 1.5 collective-permute-start.9
  37.5 2.3 %collective-permute-done.8 = bf16[80,256]{1,0:T(8,128)(2,1)S(1)} collective-permute-done((bf16[80,256]{1,0:T(8,128)(2,1)S(1)}, bf16[80,256]{1,0:T(8,128)(2,1)S(1)}, u32[]{:S(2)}, u32[]{:S(2)}) %collective-permute-start.8) | collective-permute-done | bytes 40992 | tf_op jit(solution)/shard_map/ppermute | solution.py:189
  39.8 2.7 %collective-permute-start.13 = (bf16[640,256]{1,0:T(8,128)(2,1)S(1)}, bf16[640,256]{1,0:T(8,128)(2,1)S(1)}, u32[]{:S(2)}, u32[]{:S(2)}) collective-permute-start(bf16[640,256]{1,0:T(8,128)(2,1)S(1)} %constant_dynamic-update-slice_fusion.8.refs_9_), channel_id=1, source_target_pairs={{0,3},{1,0},{2,1},{3,2},{4,7},{5,4},{6,5},{7,6},{8,11},{9,8},{10,9... | collective-permute-start | bytes 983048 | tf_op jit(solution)/shard_map/ppermute | solution.py:189
  42.5 1.0 collective-permute-start.10
  43.5 1.8 collective-permute-start.11
  45.3 7.2 %collective-permute-done.12.refs_10_ = bf16[640,256]{1,0:T(8,128)(2,1)S(1)} collective-permute-done((bf16[640,256]{1,0:T(8,128)(2,1)S(1)}, bf16[640,256]{1,0:T(8,128)(2,1)S(1)}, u32[]{:S(2)}, u32[]{:S(2)}) %collective-permute-start.12) | collective-permute-done | bytes 327712 | tf_op jit(solution)/shard_map/ppermute | solution.py:189
  52.6 2.7 %collective-permute-start.15 = (bf16[320,256]{1,0:T(8,128)(2,1)S(1)}, bf16[320,256]{1,0:T(8,128)(2,1)S(1)}, u32[]{:S(2)}, u32[]{:S(2)}) collective-permute-start(bf16[320,256]{1,0:T(8,128)(2,1)S(1)} %slice.78), channel_id=1, source_target_pairs={{0,24},{8,0},{16,8},{24,16},{1,25},{9,1},{17,9},{25,17},{2,26},{10... | collective-permute-start | bytes 491528 | tf_op jit(solution)/shard_map/ppermute | solution.py:189
  55.5 2.7 %collective-permute-start.17 = (bf16[320,256]{1,0:T(8,128)(2,1)S(1)}, bf16[320,256]{1,0:T(8,128)(2,1)S(1)}, u32[]{:S(2)}, u32[]{:S(2)}) collective-permute-start(bf16[320,256]{1,0:T(8,128)(2,1)S(1)} %slice.80), channel_id=1, source_target_pairs={{0,3},{1,0},{2,1},{3,2},{4,7},{5,4},{6,5},{7,6},{8,11},{9,8},{10,9... | collective-permute-start | bytes 491528 | tf_op jit(solution)/shard_map/ppermute | solution.py:189
  58.2 8.5 %collective-permute-start.21 = (bf16[256,5120]{1,0:T(8,128)(2,1)}, bf16[256,5120]{1,0:T(8,128)(2,1)}, u32[]{:S(2)}, u32[]{:S(2)}) collective-permute-start(bf16[256,5120]{1,0:T(8,128)(2,1)} %refs_0_.3), channel_id=1, source_target_pairs={{0,32},{32,0},{64,96},{96,64},{1,33},{33,1},{65,97},{97,65},{2,34}... | collective-permute-start | bytes 7864328 | tf_op jit(solution)/shard_map/ppermute | solution.py:193
  67.4 10.1 %collective-permute-done.1.refs_2_ = bf16[256,5120]{1,0:T(8,128)(2,1)} collective-permute-done((bf16[256,5120]{1,0:T(8,128)(2,1)}, bf16[256,5120]{1,0:T(8,128)(2,1)}, u32[]{:S(2)}, u32[]{:S(2)}) %collective-permute-start.1) | collective-permute-done | bytes 2621472 | tf_op jit(solution)/shard_map/ppermute | solution.py:193
  77.5 2.4 %collective-permute-start.22 = (bf16[256,5120]{1,0:T(8,128)(2,1)}, bf16[256,5120]{1,0:T(8,128)(2,1)}, u32[]{:S(2)}, u32[]{:S(2)}) collective-permute-start(bf16[256,5120]{1,0:T(8,128)(2,1)} %collective-permute-done.1.refs_2_), channel_id=1, source_target_pairs={{0,32},{32,0},{64,96},{96,64},{1,33},{33,1},{65,97},{97,65},{2,34}... | collective-permute-start | bytes 7864328 | tf_op jit(solution)/shard_map/ppermute | solution.py:193
  81.1 1.0 constant_dynamic-slice_fusion
  82.4 1.3 collective-permute-start.19
  84.8 7.3 %shard_map.105.rest_0_ = bf16[1024,256]{1,0:T(8,128)(2,1)} custom-call(s32[3]{0:T(128)} %pad_add_fusion.2.where_ref, bf16[256,5120]{1,0:T(8,128)(2,1)} %refs_0_.3, bf16[256,5120]{1,0:T(8,128)(2,1)} %collective-permute-done.21.refs_1_, bf16[256,5120]{1,0:T(8,128)(2,1)} %collective-permute-done.1.refs_2_, bf16[256,5120]{1,0:T(8,128)(2,1)} %collective-permute-done.22.refs_3_, ...), custom_call_target="tpu_custom_call" | custom-call | flops 2684354560 | bytes 13631488 | tf_op jit(solution)/shard_map/pallas_call | solution.py:310
  92.1 1.9 collective-permute-start.23
  94.0 13.4 %shard_map.103.q_ref = bf16[1024,640]{1,0:T(8,128)(2,1)} custom-call(s32[3]{0:T(128)} %pad_add_fusion.2.where_ref, bf16[256,5120]{1,0:T(8,128)(2,1)} %refs_0_.3, bf16[256,5120]{1,0:T(8,128)(2,1)} %collective-permute-done.21.refs_1_, bf16[256,5120]{1,0:T(8,128)(2,1)} %collective-permute-done.1.refs_2_, bf16[256,5120]{1,0:T(8,128)(2,1)} %collective-permute-done.22.refs_3_, ...), custom_call_target="tpu_custom_call" | custom-call | flops 6710886400 | bytes 18350080 | tf_op jit(solution)/shard_map/pallas_call | solution.py:310
  107.5 1.3 shard_map.104
  108.8 4.4 %collective-permute-done.23.rest_0_ = bf16[1024,256]{1,0:T(8,128)(2,1)S(1)} collective-permute-done((bf16[1024,256]{1,0:T(8,128)(2,1)}, bf16[1024,256]{1,0:T(8,128)(2,1)S(1)}, u32[]{:S(2)}, u32[]{:S(2)}) %collective-permute-start.23) | collective-permute-done | bytes 524320 | tf_op jit(solution)/shard_map/ppermute | solution.py:189
  113.2 14.9 %shard_map.106 = (f32[1024,640]{1,0:T(8,128)S(1)}, bf16[1024,256]{1,0:T(8,128)(2,1)S(1)}) custom-call(s32[8]{0:T(128)S(1)} %pad_add_fusion.1.qspan_ref, s32[1,8]{1,0:T(1,128)S(1)} %add_bitcast_fusion.1.kspan_ref, bf16[1024,640]{1,0:T(8,128)(2,1)S(1)} %copy-done.3, bf16[1024,640]{1,0:T(8,128)(2,1)S(1)} %get-tuple-element.84.g_ref, ...), custom_call_target="tpu_custom_call" | custom-call | flops 6710886400 | bytes 6815744 | tf_op jit(solution)/shard_map/pallas_call | solution.py:108
  128.1 7.5 %collective-permute-start.26 = (bf16[1024,256]{1,0:T(8,128)(2,1)S(1)}, bf16[1024,256]{1,0:T(8,128)(2,1)S(1)}, u32[]{:S(2)}, u32[]{:S(2)}) collective-permute-start(bf16[1024,256]{1,0:T(8,128)(2,1)S(1)} %get-tuple-element.103), channel_id=1, source_target_pairs={{0,31},{1,0},{2,1},{3,2},{4,3},{5,4},{6,5},{7,6},{8,7},{9,8},{10,9... | collective-permute-start | bytes 1572872 | tf_op jit(solution)/shard_map/ppermute | solution.py:189
  135.6 15.0 %shard_map.107 = (f32[1024,640]{1,0:T(8,128)S(1)}, bf16[1024,256]{1,0:T(8,128)(2,1)S(1)}) custom-call(s32[8]{0:T(128)S(1)} %pad_add_fusion.1.qspan_ref, s32[1,8]{1,0:T(1,128)S(1)} %add_bitcast_fusion.kspan_ref, bf16[1024,640]{1,0:T(8,128)(2,1)S(1)} %copy-done.3, bf16[1024,640]{1,0:T(8,128)(2,1)S(1)} %get-tuple-element.84.g_ref, ...), custom_call_target="tpu_custom_call" | custom-call | flops 6710886400 | bytes 6815744 | tf_op jit(solution)/shard_map/pallas_call | solution.py:108
  150.6 1.2 collective-permute-start.27
  151.8 8.8 %shard_map.108 = (bf16[512,640]{1,0:T(8,128)(2,1)S(1)}, f32[1024,256]{1,0:T(8,128)S(1)}) custom-call(s32[8]{0:T(128)S(1)} %pad_add_fusion.1.qspan_ref, s32[1,8]{1,0:T(1,128)S(1)} %bitcast.20, bf16[1024,640]{1,0:T(8,128)(2,1)S(1)} %copy-done.3, bf16[1024,640]{1,0:T(8,128)(2,1)S(1)} %get-tuple-element.84.g_ref, f32[5,1,1024]{2,1,0:T(1,128)S(1)} %broadcast_in_dim.14.lse_ref, ...), custom_call_target="tpu_custom_call" | custom-call | flops 3355443200 | bytes 4194304 | tf_op jit(solution)/shard_map/pallas_call | solution.py:108
  161.2 1.7 collective-permute-start.29
  162.9 8.8 %shard_map.109 = (bf16[512,640]{1,0:T(8,128)(2,1)S(1)}, f32[1024,256]{1,0:T(8,128)S(1)}) custom-call(s32[8]{0:T(128)S(1)} %pad_add_fusion.1.qspan_ref, s32[1,8]{1,0:T(1,128)S(1)} %bitcast.21, bf16[1024,640]{1,0:T(8,128)(2,1)S(1)} %copy-done.3, bf16[1024,640]{1,0:T(8,128)(2,1)S(1)} %get-tuple-element.84.g_ref, f32[5,1,1024]{2,1,0:T(1,128)S(1)} %broadcast_in_dim.14.lse_ref, ...), custom_call_target="tpu_custom_call" | custom-call | flops 3355443200 | bytes 4194304 | tf_op jit(solution)/shard_map/pallas_call | solution.py:108
  171.8 0.8 fusion.1
  172.8 4.5 %collective-permute-done.29.refs_3_ = bf16[256,640]{1,0:T(8,128)(2,1)S(1)} collective-permute-done((bf16[256,640]{1,0:T(8,128)(2,1)S(1)}, bf16[256,640]{1,0:T(8,128)(2,1)S(1)}, u32[]{:S(2)}, u32[]{:S(2)}) %collective-permute-start.29) | collective-permute-done | bytes 327712 | tf_op jit(solution)/shard_map/ppermute | solution.py:193
  177.3 0.8 fusion.2
  178.0 1.2 collective-permute-start.31
  179.3 0.9 collective-permute-start.32
  180.2 0.7 copy-done.13
  180.9 2.4 %shard_map.110 = bf16[256,2560]{1,0:T(8,128)(2,1)} custom-call(s32[4]{0:T(128)} %copy-done.2, bf16[256,640]{1,0:T(8,128)(2,1)} %get-tuple-element.118.refs_0_, bf16[256,640]{1,0:T(8,128)(2,1)} %copy-done.13, bf16[256,640]{1,0:T(8,128)(2,1)} %copy-done.11, bf16[256,640]{1,0:T(8,128)(2,1)} %copy-done.12), custom_call_target="tpu_custom_call" | custom-call | bytes 2621440 | tf_op jit(solution)/shard_map/pallas_call | solution.py:176
  183.4 2.7 %collective-permute-done.32.refs_3_ = bf16[256,256]{1,0:T(8,128)(2,1)S(1)} collective-permute-done((bf16[256,256]{1,0:T(8,128)(2,1)S(1)}, bf16[256,256]{1,0:T(8,128)(2,1)S(1)}, u32[]{:S(2)}, u32[]{:S(2)}) %collective-permute-start.32) | collective-permute-done | bytes 131104 | tf_op jit(solution)/shard_map/ppermute | solution.py:193
  186.7 2.0 %shard_map.111 = (bf16[256,512]{1,0:T(8,128)(2,1)}, bf16[256,512]{1,0:T(8,128)(2,1)}) custom-call(s32[4]{0:T(128)} %copy-done.2, bf16[256,256]{1,0:T(8,128)(2,1)} %get-tuple-element.122.refs_0_, bf16[256,256]{1,0:T(8,128)(2,1)} %copy-done.18, bf16[256,256]{1,0:T(8,128)(2,1)} %copy-done.19, bf16[256,256]{1,0:T(8,128)(2,1)} %copy-done.20), custom_call_target="tpu_custom_call" | custom-call | bytes 1048576 | tf_op jit(solution)/shard_map/pallas_call | solution.py:176
  (116 shorter events, 5.4 us)
Async XLA Ops:
  7.2 86.9 %all-gather.2.cloned.1.call-start = ((), (), s32[]{:S(2)}) async-start(), calls=%async_computation | async-start | bytes 6963200 | tf_op jit(solution)/shard_map/all_gather | solution.py:345
  8.2 10.1 %collective-permute-start = (bf16[160,896]{1,0:T(8,128)(2,1)S(1)}, bf16[160,896]{1,0:T(8,128)(2,1)S(1)}, u32[]{:S(2)}, u32[]{:S(2)}) collective-permute-start(bf16[160,896]{1,0:T(8,128)(2,1)S(1)} %pad_maximum_fusion.1), channel_id=1, source_target_pairs={{0,4},{4,0},{1,5},{5,1},{2,6},{6,2},{3,7},{7,3},{8,12},{12,8},{9,1... | collective-permute-start | bytes 860168 | tf_op jit(solution)/shard_map/ppermute | solution.py:189
  18.3 61.6 %copy-start.22 = (f32[1024,5]{0,1:T(8,128)S(1)}, f32[1024,5]{0,1:T(8,128)}, u32[]{:S(2)}) copy-start(f32[1024,5]{0,1:T(8,128)} %param.14) | copy-start | bytes 61444
  18.3 62.5 %copy-start.21 = (s32[256]{0:T(256)S(1)}, s32[256]{0:T(256)}, u32[]{:S(2)}) copy-start(s32[256]{0:T(256)} %param.15) | copy-start | bytes 3076
  18.3 62.8 %copy-start.4 = (bf16[256,2560]{1,0:T(8,128)(2,1)S(1)}, bf16[256,2560]{1,0:T(8,128)(2,1)}, u32[]{:S(2)}) copy-start(bf16[256,2560]{1,0:T(8,128)(2,1)} %param.12) | copy-start | bytes 3932164
  20.2 57.2 %collective-permute-start.1 = (bf16[256,5120]{1,0:T(8,128)(2,1)}, bf16[256,5120]{1,0:T(8,128)(2,1)}, u32[]{:S(2)}, u32[]{:S(2)}) collective-permute-start(bf16[256,5120]{1,0:T(8,128)(2,1)} %refs_0_.3), channel_id=1, source_target_pairs={{0,64},{32,96},{64,0},{96,32},{1,65},{33,97},{65,1},{97,33},{2,66}... | collective-permute-start | bytes 7864328 | tf_op jit(solution)/shard_map/ppermute | solution.py:193
  23.2 6.6 %collective-permute-start.2 = (bf16[160,256]{1,0:T(8,128)(2,1)S(1)}, bf16[160,256]{1,0:T(8,128)(2,1)S(1)}, u32[]{:S(2)}, u32[]{:S(2)}) collective-permute-start(bf16[160,256]{1,0:T(8,128)(2,1)S(1)} %pad_maximum_fusion.2), channel_id=1, source_target_pairs={{0,1},{1,2},{2,3},{3,0},{4,5},{5,6},{6,7},{7,4},{8,9},{9,10},{10,1... | collective-permute-start | bytes 245768 | tf_op jit(solution)/shard_map/ppermute | solution.py:189
  24.9 4.9 %collective-permute-start.3 = (bf16[160,256]{1,0:T(8,128)(2,1)S(1)}, bf16[160,256]{1,0:T(8,128)(2,1)S(1)}, u32[]{:S(2)}, u32[]{:S(2)}) collective-permute-start(bf16[160,256]{1,0:T(8,128)(2,1)S(1)} %pad_maximum_fusion.2), channel_id=1, source_target_pairs={{0,3},{1,0},{2,1},{3,2},{4,7},{5,4},{6,5},{7,6},{8,11},{9,8},{10,9... | collective-permute-start | bytes 245768 | tf_op jit(solution)/shard_map/ppermute | solution.py:189
  27.1 4.5 %collective-permute-start.4 = (bf16[160,256]{1,0:T(8,128)(2,1)S(1)}, bf16[160,256]{1,0:T(8,128)(2,1)S(1)}, u32[]{:S(2)}, u32[]{:S(2)}) collective-permute-start(bf16[160,256]{1,0:T(8,128)(2,1)S(1)} %pad_maximum_fusion.3), channel_id=1, source_target_pairs={{0,8},{8,16},{16,24},{24,0},{1,9},{9,17},{17,25},{25,1},{2,10},{10... | collective-permute-start | bytes 245768 | tf_op jit(solution)/shard_map/ppermute | solution.py:189
  28.4 3.7 %collective-permute-start.5 = (bf16[160,256]{1,0:T(8,128)(2,1)S(1)}, bf16[160,256]{1,0:T(8,128)(2,1)S(1)}, u32[]{:S(2)}, u32[]{:S(2)}) collective-permute-start(bf16[160,256]{1,0:T(8,128)(2,1)S(1)} %pad_maximum_fusion.3), channel_id=1, source_target_pairs={{0,24},{8,0},{16,8},{24,16},{1,25},{9,1},{17,9},{25,17},{2,26},{10... | collective-permute-start | bytes 245768 | tf_op jit(solution)/shard_map/ppermute | solution.py:189
  32.1 5.4 %collective-permute-start.6 = (bf16[80,256]{1,0:T(8,128)(2,1)S(1)}, bf16[80,256]{1,0:T(8,128)(2,1)S(1)}, u32[]{:S(2)}, u32[]{:S(2)}) collective-permute-start(bf16[80,256]{1,0:T(8,128)(2,1)S(1)} %slice.73), channel_id=1, source_target_pairs={{0,1},{1,2},{2,3},{3,0},{4,5},{5,6},{6,7},{7,4},{8,9},{9,10},{10,1... | collective-permute-start | bytes 122888 | tf_op jit(solution)/shard_map/ppermute | solution.py:189
  32.1 5.4 %collective-permute-start.7 = (bf16[80,256]{1,0:T(8,128)(2,1)S(1)}, bf16[80,256]{1,0:T(8,128)(2,1)S(1)}, u32[]{:S(2)}, u32[]{:S(2)}) collective-permute-start(bf16[80,256]{1,0:T(8,128)(2,1)S(1)} %slice.74), channel_id=1, source_target_pairs={{0,3},{1,0},{2,1},{3,2},{4,7},{5,4},{6,5},{7,6},{8,11},{9,8},{10,9... | collective-permute-start | bytes 122888 | tf_op jit(solution)/shard_map/ppermute | solution.py:189
  34.7 5.0 %collective-permute-start.8 = (bf16[80,256]{1,0:T(8,128)(2,1)S(1)}, bf16[80,256]{1,0:T(8,128)(2,1)S(1)}, u32[]{:S(2)}, u32[]{:S(2)}) collective-permute-start(bf16[80,256]{1,0:T(8,128)(2,1)S(1)} %slice.75), channel_id=1, source_target_pairs={{0,8},{8,16},{16,24},{24,0},{1,9},{9,17},{17,25},{25,1},{2,10},{10... | collective-permute-start | bytes 122888 | tf_op jit(solution)/shard_map/ppermute | solution.py:189
  36.0 3.8 %collective-permute-start.9 = (bf16[80,256]{1,0:T(8,128)(2,1)S(1)}, bf16[80,256]{1,0:T(8,128)(2,1)S(1)}, u32[]{:S(2)}, u32[]{:S(2)}) collective-permute-start(bf16[80,256]{1,0:T(8,128)(2,1)S(1)} %slice.76), channel_id=1, source_target_pairs={{0,24},{8,0},{16,8},{24,16},{1,25},{9,1},{17,9},{25,17},{2,26},{10... | collective-permute-start | bytes 122888 | tf_op jit(solution)/shard_map/ppermute | solution.py:189
  39.7 42.6 %copy-start.9 = (bf16[640,256]{1,0:T(8,128)(2,1)}, bf16[640,256]{1,0:T(8,128)(2,1)S(1)}, u32[]{:S(2)}) copy-start(bf16[640,256]{1,0:T(8,128)(2,1)S(1)} %constant_dynamic-update-slice_fusion.8.refs_9_) | copy-start | bytes 983044
  39.8 12.7 %collective-permute-start.12 = (bf16[640,256]{1,0:T(8,128)(2,1)S(1)}, bf16[640,256]{1,0:T(8,128)(2,1)S(1)}, u32[]{:S(2)}, u32[]{:S(2)}) collective-permute-start(bf16[640,256]{1,0:T(8,128)(2,1)S(1)} %constant_dynamic-update-slice_fusion.8.refs_9_), channel_id=1, source_target_pairs={{0,1},{1,2},{2,3},{3,0},{4,5},{5,6},{6,7},{7,4},{8,9},{9,10},{10,1... | collective-permute-start | bytes 983048 | tf_op jit(solution)/shard_map/ppermute | solution.py:189
  39.8 12.6 %collective-permute-start.13 = (bf16[640,256]{1,0:T(8,128)(2,1)S(1)}, bf16[640,256]{1,0:T(8,128)(2,1)S(1)}, u32[]{:S(2)}, u32[]{:S(2)}) collective-permute-start(bf16[640,256]{1,0:T(8,128)(2,1)S(1)} %constant_dynamic-update-slice_fusion.8.refs_9_), channel_id=1, source_target_pairs={{0,3},{1,0},{2,1},{3,2},{4,7},{5,4},{6,5},{7,6},{8,11},{9,8},{10,9... | collective-permute-start | bytes 983048 | tf_op jit(solution)/shard_map/ppermute | solution.py:189
  42.5 9.9 %collective-permute-start.10 = (bf16[640,256]{1,0:T(8,128)(2,1)S(1)}, bf16[640,256]{1,0:T(8,128)(2,1)S(1)}, u32[]{:S(2)}, u32[]{:S(2)}) collective-permute-start(bf16[640,256]{1,0:T(8,128)(2,1)S(1)} %constant_dynamic-update-slice_fusion.2.refs_4_), channel_id=1, source_target_pairs={{0,8},{8,16},{16,24},{24,0},{1,9},{9,17},{17,25},{25,1},{2,10},{10... | collective-permute-start | bytes 983048 | tf_op jit(solution)/shard_map/ppermute | solution.py:189
  43.5 9.0 %collective-permute-start.11 = (bf16[640,256]{1,0:T(8,128)(2,1)S(1)}, bf16[640,256]{1,0:T(8,128)(2,1)S(1)}, u32[]{:S(2)}, u32[]{:S(2)}) collective-permute-start(bf16[640,256]{1,0:T(8,128)(2,1)S(1)} %constant_dynamic-update-slice_fusion.2.refs_4_), channel_id=1, source_target_pairs={{0,24},{8,0},{16,8},{24,16},{1,25},{9,1},{17,9},{25,17},{2,26},{10... | collective-permute-start | bytes 983048 | tf_op jit(solution)/shard_map/ppermute | solution.py:189
  52.4 32.3 %copy-start.5 = (bf16[640,256]{1,0:T(8,128)(2,1)}, bf16[640,256]{1,0:T(8,128)(2,1)S(1)}, u32[]{:S(2)}) copy-start(bf16[640,256]{1,0:T(8,128)(2,1)S(1)} %collective-permute-done.12.refs_10_) | copy-start | bytes 983044
  52.5 32.3 %copy-start.6 = (bf16[640,256]{1,0:T(8,128)(2,1)}, bf16[640,256]{1,0:T(8,128)(2,1)S(1)}, u32[]{:S(2)}) copy-start(bf16[640,256]{1,0:T(8,128)(2,1)S(1)} %collective-permute-done.13.refs_13_) | copy-start | bytes 983044
  52.5 29.7 %copy-start.7 = (bf16[640,256]{1,0:T(8,128)(2,1)}, bf16[640,256]{1,0:T(8,128)(2,1)S(1)}, u32[]{:S(2)}) copy-start(bf16[640,256]{1,0:T(8,128)(2,1)S(1)} %collective-permute-done.10.refs_5_) | copy-start | bytes 983044
  52.5 29.7 %copy-start.8 = (bf16[640,256]{1,0:T(8,128)(2,1)}, bf16[640,256]{1,0:T(8,128)(2,1)S(1)}, u32[]{:S(2)}) copy-start(bf16[640,256]{1,0:T(8,128)(2,1)S(1)} %collective-permute-done.11.refs_8_) | copy-start | bytes 983044
  52.5 5.7 %collective-permute-start.14 = (bf16[320,256]{1,0:T(8,128)(2,1)S(1)}, bf16[320,256]{1,0:T(8,128)(2,1)S(1)}, u32[]{:S(2)}, u32[]{:S(2)}) collective-permute-start(bf16[320,256]{1,0:T(8,128)(2,1)S(1)} %slice.77), channel_id=1, source_target_pairs={{0,8},{8,16},{16,24},{24,0},{1,9},{9,17},{17,25},{25,1},{2,10},{10... | collective-permute-start | bytes 491528 | tf_op jit(solution)/shard_map/ppermute | solution.py:189
  52.6 14.1 %collective-permute-start.15 = (bf16[320,256]{1,0:T(8,128)(2,1)S(1)}, bf16[320,256]{1,0:T(8,128)(2,1)S(1)}, u32[]{:S(2)}, u32[]{:S(2)}) collective-permute-start(bf16[320,256]{1,0:T(8,128)(2,1)S(1)} %slice.78), channel_id=1, source_target_pairs={{0,24},{8,0},{16,8},{24,16},{1,25},{9,1},{17,9},{25,17},{2,26},{10... | collective-permute-start | bytes 491528 | tf_op jit(solution)/shard_map/ppermute | solution.py:189
  55.4 11.3 %collective-permute-start.16 = (bf16[320,256]{1,0:T(8,128)(2,1)S(1)}, bf16[320,256]{1,0:T(8,128)(2,1)S(1)}, u32[]{:S(2)}, u32[]{:S(2)}) collective-permute-start(bf16[320,256]{1,0:T(8,128)(2,1)S(1)} %slice.79), channel_id=1, source_target_pairs={{0,1},{1,2},{2,3},{3,0},{4,5},{5,6},{6,7},{7,4},{8,9},{9,10},{10,1... | collective-permute-start | bytes 491528 | tf_op jit(solution)/shard_map/ppermute | solution.py:189
  55.5 11.2 %collective-permute-start.17 = (bf16[320,256]{1,0:T(8,128)(2,1)S(1)}, bf16[320,256]{1,0:T(8,128)(2,1)S(1)}, u32[]{:S(2)}, u32[]{:S(2)}) collective-permute-start(bf16[320,256]{1,0:T(8,128)(2,1)S(1)} %slice.80), channel_id=1, source_target_pairs={{0,3},{1,0},{2,1},{3,2},{4,7},{5,4},{6,5},{7,6},{8,11},{9,8},{10,9... | collective-permute-start | bytes 491528 | tf_op jit(solution)/shard_map/ppermute | solution.py:189
  58.2 26.6 %copy-start.14 = (bf16[320,256]{1,0:T(8,128)(2,1)}, bf16[320,256]{1,0:T(8,128)(2,1)S(1)}, u32[]{:S(2)}) copy-start(bf16[320,256]{1,0:T(8,128)(2,1)S(1)} %collective-permute-done.14.refs_6_) | copy-start | bytes 491524
  58.2 26.1 %collective-permute-start.21 = (bf16[256,5120]{1,0:T(8,128)(2,1)}, bf16[256,5120]{1,0:T(8,128)(2,1)}, u32[]{:S(2)}, u32[]{:S(2)}) collective-permute-start(bf16[256,5120]{1,0:T(8,128)(2,1)} %refs_0_.3), channel_id=1, source_target_pairs={{0,32},{32,0},{64,96},{96,64},{1,33},{33,1},{65,97},{97,65},{2,34}... | collective-permute-start | bytes 7864328 | tf_op jit(solution)/shard_map/ppermute | solution.py:193
  66.7 10.8 %copy-start.16 = (bf16[320,256]{1,0:T(8,128)(2,1)}, bf16[320,256]{1,0:T(8,128)(2,1)S(1)}, u32[]{:S(2)}) copy-start(bf16[320,256]{1,0:T(8,128)(2,1)S(1)} %collective-permute-done.16.refs_11_) | copy-start | bytes 491524
  67.3 12.5 %copy-start.17 = (bf16[320,256]{1,0:T(8,128)(2,1)}, bf16[320,256]{1,0:T(8,128)(2,1)S(1)}, u32[]{:S(2)}) copy-start(bf16[320,256]{1,0:T(8,128)(2,1)S(1)} %collective-permute-done.17.refs_12_) | copy-start | bytes 491524
  77.5 7.3 %collective-permute-start.22 = (bf16[256,5120]{1,0:T(8,128)(2,1)}, bf16[256,5120]{1,0:T(8,128)(2,1)}, u32[]{:S(2)}, u32[]{:S(2)}) collective-permute-start(bf16[256,5120]{1,0:T(8,128)(2,1)} %collective-permute-done.1.refs_2_), channel_id=1, source_target_pairs={{0,32},{32,0},{64,96},{96,64},{1,33},{33,1},{65,97},{97,65},{2,34}... | collective-permute-start | bytes 7864328 | tf_op jit(solution)/shard_map/ppermute | solution.py:193
  80.8 26.7 %copy-start.2 = (s32[4]{0:T(128)}, s32[4]{0:T(128)S(1)}, u32[]{:S(2)}) copy-start(s32[4]{0:T(128)S(1)} %pad_add_fusion.mine_ref) | copy-start | bytes 52
  82.2 25.3 %collective-permute-start.18 = (bf16[256,640]{1,0:T(8,128)(2,1)}, bf16[256,640]{1,0:T(8,128)(2,1)S(1)}, u32[]{:S(2)}, u32[]{:S(2)}) collective-permute-start(bf16[256,640]{1,0:T(8,128)(2,1)} %get-tuple-element.76), channel_id=1, source_target_pairs={{0,32},{32,0},{64,96},{96,64},{1,33},{33,1},{65,97},{97,65},{2,34}... | collective-permute-start | bytes 983048 | tf_op jit(solution)/shard_map/ppermute | solution.py:193
  82.4 25.1 %collective-permute-start.19 = (bf16[256,640]{1,0:T(8,128)(2,1)}, bf16[256,640]{1,0:T(8,128)(2,1)S(1)}, u32[]{:S(2)}, u32[]{:S(2)}) collective-permute-start(bf16[256,640]{1,0:T(8,128)(2,1)} %get-tuple-element.77), channel_id=1, source_target_pairs={{0,64},{32,96},{64,0},{96,32},{1,65},{33,97},{65,1},{97,33},{2,66}... | collective-permute-start | bytes 983048 | tf_op jit(solution)/shard_map/ppermute | solution.py:193
  83.7 23.8 %collective-permute-start.20 = (bf16[256,640]{1,0:T(8,128)(2,1)}, bf16[256,640]{1,0:T(8,128)(2,1)S(1)}, u32[]{:S(2)}, u32[]{:S(2)}) collective-permute-start(bf16[256,640]{1,0:T(8,128)(2,1)} %get-tuple-element.78), channel_id=1, source_target_pairs={{0,96},{32,64},{64,32},{96,0},{1,97},{33,65},{65,33},{97,1},{2,98}... | collective-permute-start | bytes 983048 | tf_op jit(solution)/shard_map/ppermute | solution.py:193
  92.1 15.4 %copy-start = (bf16[1024,640]{1,0:T(8,128)(2,1)S(1)}, bf16[1024,640]{1,0:T(8,128)(2,1)}, u32[]{:S(2)}) copy-start(bf16[1024,640]{1,0:T(8,128)(2,1)} %refs_4_.1) | copy-start | bytes 3932164
  92.1 21.1 %collective-permute-start.23 = (bf16[1024,256]{1,0:T(8,128)(2,1)}, bf16[1024,256]{1,0:T(8,128)(2,1)S(1)}, u32[]{:S(2)}, u32[]{:S(2)}) collective-permute-start(bf16[1024,256]{1,0:T(8,128)(2,1)} %shard_map.105.rest_0_), channel_id=1, source_target_pairs={{0,1},{1,2},{2,3},{3,4},{4,5},{5,6},{6,7},{7,8},{8,9},{9,10},{10,1... | collective-permute-start | bytes 1572872 | tf_op jit(solution)/shard_map/ppermute | solution.py:189
  113.2 22.4 %collective-permute-start.24 = (bf16[1024,256]{1,0:T(8,128)(2,1)S(1)}, bf16[1024,256]{1,0:T(8,128)(2,1)S(1)}, u32[]{:S(2)}, u32[]{:S(2)}) collective-permute-start(bf16[1024,256]{1,0:T(8,128)(2,1)S(1)} %collective-permute-done.23.rest_0_), channel_id=1, source_target_pairs={{0,1},{1,2},{2,3},{3,4},{4,5},{5,6},{6,7},{7,8},{8,9},{9,10},{10,1... | collective-permute-start | bytes 1572872 | tf_op jit(solution)/shard_map/ppermute | solution.py:189
  128.1 44.5 %collective-permute-start.26 = (bf16[1024,256]{1,0:T(8,128)(2,1)S(1)}, bf16[1024,256]{1,0:T(8,128)(2,1)S(1)}, u32[]{:S(2)}, u32[]{:S(2)}) collective-permute-start(bf16[1024,256]{1,0:T(8,128)(2,1)S(1)} %get-tuple-element.103), channel_id=1, source_target_pairs={{0,31},{1,0},{2,1},{3,2},{4,3},{5,4},{6,5},{7,6},{8,7},{9,8},{10,9... | collective-permute-start | bytes 1572872 | tf_op jit(solution)/shard_map/ppermute | solution.py:189
  135.6 16.2 %copy-start.1 = (bf16[1024,256]{1,0:T(8,128)(2,1)S(1)}, bf16[1024,256]{1,0:T(8,128)(2,1)}, u32[]{:S(2)}) copy-start(bf16[1024,256]{1,0:T(8,128)(2,1)} %shard_map.105.rest_0_) | copy-start | bytes 1572868
  150.6 22.0 %collective-permute-start.27 = (bf16[1024,256]{1,0:T(8,128)(2,1)S(1)}, bf16[1024,256]{1,0:T(8,128)(2,1)S(1)}, u32[]{:S(2)}, u32[]{:S(2)}) collective-permute-start(bf16[1024,256]{1,0:T(8,128)(2,1)S(1)} %get-tuple-element.104), channel_id=1, source_target_pairs={{0,30},{1,31},{2,0},{3,1},{4,2},{5,3},{6,4},{7,5},{8,6},{9,7},{10,... | collective-permute-start | bytes 1572872 | tf_op jit(solution)/shard_map/ppermute | solution.py:189
  160.7 12.1 %collective-permute-start.28 = (bf16[256,640]{1,0:T(8,128)(2,1)S(1)}, bf16[256,640]{1,0:T(8,128)(2,1)S(1)}, u32[]{:S(2)}, u32[]{:S(2)}) collective-permute-start(bf16[256,640]{1,0:T(8,128)(2,1)S(1)} %get-tuple-element.116), channel_id=1, source_target_pairs={{0,64},{32,96},{64,0},{96,32},{1,65},{33,97},{65,1},{97,33},{2,66}... | collective-permute-start | bytes 983048 | tf_op jit(solution)/shard_map/ppermute | solution.py:193
  161.2 16.1 %collective-permute-start.29 = (bf16[256,640]{1,0:T(8,128)(2,1)S(1)}, bf16[256,640]{1,0:T(8,128)(2,1)S(1)}, u32[]{:S(2)}, u32[]{:S(2)}) collective-permute-start(bf16[256,640]{1,0:T(8,128)(2,1)S(1)} %get-tuple-element.115), channel_id=1, source_target_pairs={{0,96},{32,64},{64,32},{96,0},{1,97},{33,65},{65,33},{97,1},{2,98}... | collective-permute-start | bytes 983048 | tf_op jit(solution)/shard_map/ppermute | solution.py:193
  172.6 7.6 %collective-permute-start.25 = (bf16[256,640]{1,0:T(8,128)(2,1)S(1)}, bf16[256,640]{1,0:T(8,128)(2,1)S(1)}, u32[]{:S(2)}, u32[]{:S(2)}) collective-permute-start(bf16[256,640]{1,0:T(8,128)(2,1)S(1)} %get-tuple-element.117), channel_id=1, source_target_pairs={{0,32},{32,0},{64,96},{96,64},{1,33},{33,1},{65,97},{97,65},{2,34}... | collective-permute-start | bytes 983048 | tf_op jit(solution)/shard_map/ppermute | solution.py:193
  178.0 5.3 %collective-permute-start.30 = (bf16[256,256]{1,0:T(8,128)(2,1)S(1)}, bf16[256,256]{1,0:T(8,128)(2,1)S(1)}, u32[]{:S(2)}, u32[]{:S(2)}) collective-permute-start(bf16[256,256]{1,0:T(8,128)(2,1)S(1)} %get-tuple-element.121), channel_id=1, source_target_pairs={{0,32},{32,0},{64,96},{96,64},{1,33},{33,1},{65,97},{97,65},{2,34}... | collective-permute-start | bytes 393224 | tf_op jit(solution)/shard_map/ppermute | solution.py:193
  178.0 5.3 %collective-permute-start.31 = (bf16[256,256]{1,0:T(8,128)(2,1)S(1)}, bf16[256,256]{1,0:T(8,128)(2,1)S(1)}, u32[]{:S(2)}, u32[]{:S(2)}) collective-permute-start(bf16[256,256]{1,0:T(8,128)(2,1)S(1)} %get-tuple-element.120), channel_id=1, source_target_pairs={{0,64},{32,96},{64,0},{96,32},{1,65},{33,97},{65,1},{97,33},{2,66}... | collective-permute-start | bytes 393224 | tf_op jit(solution)/shard_map/ppermute | solution.py:193
  179.3 6.8 %collective-permute-start.32 = (bf16[256,256]{1,0:T(8,128)(2,1)S(1)}, bf16[256,256]{1,0:T(8,128)(2,1)S(1)}, u32[]{:S(2)}, u32[]{:S(2)}) collective-permute-start(bf16[256,256]{1,0:T(8,128)(2,1)S(1)} %get-tuple-element.119), channel_id=1, source_target_pairs={{0,96},{32,64},{64,32},{96,0},{1,97},{33,65},{65,33},{97,1},{2,98}... | collective-permute-start | bytes 393224 | tf_op jit(solution)/shard_map/ppermute | solution.py:193
  (9 other events, 33.6 us)
Sparse Core Ops, SparseCore 0:
  20.3 69.1 all-gather.1

commit v5 on v4

--- a/solution.py
+++ b/solution.py
@@ -184,6 +184,30 @@
     )(mine, *pieces)
 
 
+def sum_pieces(total, *parts):
+    rows, cols = total.shape[0] // 4, total.shape[1]
+
+    def body(*refs):
+        for d in range(4):
+            at = pl.ds(d * rows, rows)
+            result = refs[0][at, :]
+            for ref in refs[1 : 1 + len(parts)]:
+                result = result + ref[at, :].astype(jnp.float32)
+            refs[1 + len(parts) + d][...] = result.astype(jnp.bfloat16)
+
+    vmem = pl.BlockSpec(memory_space=pltpu.VMEM)
+    return pl.pallas_call(
+        body,
+        in_specs=[vmem] * (1 + len(parts)),
+        out_specs=[vmem] * 4,
+        out_shape=[jax.ShapeDtypeStruct((rows, cols), jnp.bfloat16)] * 4,
+        compiler_params=pltpu.CompilerParams(vmem_limit_bytes=16 * 2**20),
+        cost_estimate=pl.CostEstimate(
+            flops=8 * rows * cols, bytes_accessed=40 * rows * cols, transcendentals=0
+        ),
+    )(total, *parts)
+
+
 def shift(block, axis, by):
     size = lax.axis_size(axis)
     return lax.ppermute(block, axis, [(i, (i + by) % size) for i in range(size)])
@@ -393,9 +417,9 @@
     dq2, dq3 = to_peer(dq_far[:rows], 2), to_peer(dq_far[rows:], 3)
     dq_near, dkv0 = part(0, half, kv, span_ids[0], 0, dq, dkv0, bf16, f32)
     dq1 = to_peer(dq_near[rows:], 1)
-    dkv = (dkv0 + back1.astype(f32) + back2.astype(f32)).astype(bf16)
-    dkv, dq2, dq3 = fence(dkv, dq2, dq3)
-    dkvs = [to_peer(dkv[d * rows : (d + 1) * rows], d) for d in peers]
+    dkvs = sum_pieces(dkv0, back1, back2)
+    *dkvs, dq2, dq3 = fence(*dkvs, dq2, dq3)
+    dkvs = [to_peer(dkvs[d], d) for d in peers]
     (grad_query,) = by_head([dq_near[:rows], dq1, dq2, dq3], mine_all, [cols])
     grad_key, grad_value = by_head(dkvs, mine_all, [HD, HD])
     return grad_query, grad_key, grad_value

time: 197 us -> 213 us (1.081)
  waiting for transfers between devices: 40.1 us -> 57.6 us
    ppermute x21, waiting for transfers between devices: 22.3 us -> 31.6 us  [shift(): lax.ppermute(block, axis, [(i, (i + by) % size) for i in range(size)])]
    ppermute x12, waiting for transfers between devices: 17.8 us -> 26.1 us  [to_peer(): lax.ppermute(block, HEAD, [(i, i ^ d) for i in range(4)])]
  transfers between devices with their start and end apart: 34 -> 34, of which waited for: 10 -> 12; matrix products, arithmetic and copies ran while one was open for 3% -> 2% of each run, Pallas kernels for 37% -> 34%
where the time goes in v5:
time: 213 us
  Pallas kernels  74.3 us (35%)
  waiting for transfers between devices  57.6 us (27%)
  starting transfers between devices  56.2 us (26%)
  between operations  14.6 us (7%)
  local copies, waits for them, and re-layouts  6.49 us (3%)
  other arithmetic  3.73 us (2%)
    pallas_call x4, Pallas kernels, tile_grads(): pl.pallas_call(body, grid=(heads,), in_specs=[smem, smem, per_head, per_h...  47.7 us
    ppermute x21, starting transfers between devices, shift(): lax.ppermute(block, axis, [(i, (i + by) % size) for i in range(size)])  37.3 us
    ppermute x21, waiting for transfers between devices, shift(): lax.ppermute(block, axis, [(i, (i + by) % size) for i in range(size)])  31.6 us
    ppermute x12, waiting for transfers between devices, to_peer(): lax.ppermute(block, HEAD, [(i, i ^ d) for i in range(4)])  26.1 us
    pallas_call x2, Pallas kernels, project(): pl.pallas_call(body, in_specs=[pl.BlockSpec(memory_space=pltpu.SMEM)] + [...  20.7 us
    ppermute x12, starting transfers between devices, to_peer(): lax.ppermute(block, HEAD, [(i, i ^ d) for i in range(4)])  18.9 us
    pallas_call x2, Pallas kernels, by_head(): pl.pallas_call(body, in_specs=[pl.BlockSpec(memory_space=pltpu.SMEM)] + [...  4.43 us
  transfers between devices with their start and end apart: 34, of which 12 were waited for; matrix products, arithmetic and copies ran while one was open for 2% of the time, Pallas kernels for 34%

profile of v5, /device:TPU:1, one launch (start us, length us, event | category | flops | bytes accessed | tf_op | source)
XLA Modules:
  0.0 213.0 jit_solution(6070999683953712173)
XLA Ops:
  7.2 1.0 pad_maximum_fusion.1
  8.2 3.8 %collective-permute-start = (bf16[160,896]{1,0:T(8,128)(2,1)S(1)}, bf16[160,896]{1,0:T(8,128)(2,1)S(1)}, u32[]{:S(2)}, u32[]{:S(2)}) collective-permute-start(bf16[160,896]{1,0:T(8,128)(2,1)S(1)} %pad_maximum_fusion.1), channel_id=1, source_target_pairs={{0,4},{4,0},{1,5},{5,1},{2,6},{6,2},{3,7},{7,3},{8,12},{12,8},{9,1... | collective-permute-start | bytes 860168 | tf_op jit(solution)/shard_map/ppermute | solution.py:213
  12.0 6.3 %collective-permute-done = bf16[160,896]{1,0:T(8,128)(2,1)S(1)} collective-permute-done((bf16[160,896]{1,0:T(8,128)(2,1)S(1)}, bf16[160,896]{1,0:T(8,128)(2,1)S(1)}, u32[]{:S(2)}, u32[]{:S(2)}) %collective-permute-start) | collective-permute-done | bytes 286752 | tf_op jit(solution)/shard_map/ppermute | solution.py:213
  18.4 1.8 pad_maximum_fusion
  20.2 1.4 collective-permute-start.1
  21.6 0.8 constant_dynamic-update-slice_fusion.1
  22.4 0.8 constant_dynamic-update-slice_fusion
  23.2 1.7 collective-permute-start.2
  24.9 2.2 %collective-permute-start.3 = (bf16[160,256]{1,0:T(8,128)(2,1)S(1)}, bf16[160,256]{1,0:T(8,128)(2,1)S(1)}, u32[]{:S(2)}, u32[]{:S(2)}) collective-permute-start(bf16[160,256]{1,0:T(8,128)(2,1)S(1)} %pad_maximum_fusion.2), channel_id=1, source_target_pairs={{0,3},{1,0},{2,1},{3,2},{4,7},{5,4},{6,5},{7,6},{8,11},{9,8},{10,9... | collective-permute-start | bytes 245768 | tf_op jit(solution)/shard_map/ppermute | solution.py:213
  27.1 1.2 collective-permute-start.4
  28.4 1.5 collective-permute-start.5
  29.8 1.8 collective-permute-done.4
  32.1 2.7 %collective-permute-start.7 = (bf16[80,256]{1,0:T(8,128)(2,1)S(1)}, bf16[80,256]{1,0:T(8,128)(2,1)S(1)}, u32[]{:S(2)}, u32[]{:S(2)}) collective-permute-start(bf16[80,256]{1,0:T(8,128)(2,1)S(1)} %slice.62), channel_id=1, source_target_pairs={{0,3},{1,0},{2,1},{3,2},{4,7},{5,4},{6,5},{7,6},{8,11},{9,8},{10,9... | collective-permute-start | bytes 122888 | tf_op jit(solution)/shard_map/ppermute | solution.py:213
  34.7 1.2 collective-permute-start.8
  36.0 1.5 collective-permute-start.9
  37.5 2.3 %collective-permute-done.8 = bf16[80,256]{1,0:T(8,128)(2,1)S(1)} collective-permute-done((bf16[80,256]{1,0:T(8,128)(2,1)S(1)}, bf16[80,256]{1,0:T(8,128)(2,1)S(1)}, u32[]{:S(2)}, u32[]{:S(2)}) %collective-permute-start.8) | collective-permute-done | bytes 40992 | tf_op jit(solution)/shard_map/ppermute | solution.py:213
  39.8 2.7 %collective-permute-start.13 = (bf16[640,256]{1,0:T(8,128)(2,1)S(1)}, bf16[640,256]{1,0:T(8,128)(2,1)S(1)}, u32[]{:S(2)}, u32[]{:S(2)}) collective-permute-start(bf16[640,256]{1,0:T(8,128)(2,1)S(1)} %constant_dynamic-update-slice_fusion.8.refs_9_), channel_id=1, source_target_pairs={{0,3},{1,0},{2,1},{3,2},{4,7},{5,4},{6,5},{7,6},{8,11},{9,8},{10,9... | collective-permute-start | bytes 983048 | tf_op jit(solution)/shard_map/ppermute | solution.py:213
  42.5 1.0 collective-permute-start.10
  43.5 1.8 collective-permute-start.11
  45.3 7.2 %collective-permute-done.12.refs_10_ = bf16[640,256]{1,0:T(8,128)(2,1)S(1)} collective-permute-done((bf16[640,256]{1,0:T(8,128)(2,1)S(1)}, bf16[640,256]{1,0:T(8,128)(2,1)S(1)}, u32[]{:S(2)}, u32[]{:S(2)}) %collective-permute-start.12) | collective-permute-done | bytes 327712 | tf_op jit(solution)/shard_map/ppermute | solution.py:213
  52.6 2.7 %collective-permute-start.15 = (bf16[320,256]{1,0:T(8,128)(2,1)S(1)}, bf16[320,256]{1,0:T(8,128)(2,1)S(1)}, u32[]{:S(2)}, u32[]{:S(2)}) collective-permute-start(bf16[320,256]{1,0:T(8,128)(2,1)S(1)} %slice.66), channel_id=1, source_target_pairs={{0,24},{8,0},{16,8},{24,16},{1,25},{9,1},{17,9},{25,17},{2,26},{10... | collective-permute-start | bytes 491528 | tf_op jit(solution)/shard_map/ppermute | solution.py:213
  55.5 2.7 %collective-permute-start.17 = (bf16[320,256]{1,0:T(8,128)(2,1)S(1)}, bf16[320,256]{1,0:T(8,128)(2,1)S(1)}, u32[]{:S(2)}, u32[]{:S(2)}) collective-permute-start(bf16[320,256]{1,0:T(8,128)(2,1)S(1)} %slice.68), channel_id=1, source_target_pairs={{0,3},{1,0},{2,1},{3,2},{4,7},{5,4},{6,5},{7,6},{8,11},{9,8},{10,9... | collective-permute-start | bytes 491528 | tf_op jit(solution)/shard_map/ppermute | solution.py:213
  58.2 8.5 %collective-permute-start.21 = (bf16[256,5120]{1,0:T(8,128)(2,1)}, bf16[256,5120]{1,0:T(8,128)(2,1)}, u32[]{:S(2)}, u32[]{:S(2)}) collective-permute-start(bf16[256,5120]{1,0:T(8,128)(2,1)} %refs_0_.3), channel_id=1, source_target_pairs={{0,32},{32,0},{64,96},{96,64},{1,33},{33,1},{65,97},{97,65},{2,34}... | collective-permute-start | bytes 7864328 | tf_op jit(solution)/shard_map/ppermute | solution.py:217
  67.4 10.1 %collective-permute-done.1.refs_2_ = bf16[256,5120]{1,0:T(8,128)(2,1)} collective-permute-done((bf16[256,5120]{1,0:T(8,128)(2,1)}, bf16[256,5120]{1,0:T(8,128)(2,1)}, u32[]{:S(2)}, u32[]{:S(2)}) %collective-permute-start.1) | collective-permute-done | bytes 2621472 | tf_op jit(solution)/shard_map/ppermute | solution.py:217
  77.5 2.4 %collective-permute-start.22 = (bf16[256,5120]{1,0:T(8,128)(2,1)}, bf16[256,5120]{1,0:T(8,128)(2,1)}, u32[]{:S(2)}, u32[]{:S(2)}) collective-permute-start(bf16[256,5120]{1,0:T(8,128)(2,1)} %collective-permute-done.1.refs_2_), channel_id=1, source_target_pairs={{0,32},{32,0},{64,96},{96,64},{1,33},{33,1},{65,97},{97,65},{2,34}... | collective-permute-start | bytes 7864328 | tf_op jit(solution)/shard_map/ppermute | solution.py:217
  81.1 1.0 constant_dynamic-slice_fusion
  82.3 1.3 collective-permute-start.19
  84.8 7.3 %shard_map.105.rest_0_ = bf16[1024,256]{1,0:T(8,128)(2,1)} custom-call(s32[3]{0:T(128)} %pad_add_fusion.2.where_ref, bf16[256,5120]{1,0:T(8,128)(2,1)} %refs_0_.3, bf16[256,5120]{1,0:T(8,128)(2,1)} %collective-permute-done.21.refs_1_, bf16[256,5120]{1,0:T(8,128)(2,1)} %collective-permute-done.1.refs_2_, bf16[256,5120]{1,0:T(8,128)(2,1)} %collective-permute-done.22.refs_3_, ...), custom_call_target="tpu_custom_call" | custom-call | flops 2684354560 | bytes 13631488 | tf_op jit(solution)/shard_map/pallas_call | solution.py:334
  92.1 1.9 collective-permute-start.23
  94.0 13.4 %shard_map.103.q_ref = bf16[1024,640]{1,0:T(8,128)(2,1)} custom-call(s32[3]{0:T(128)} %pad_add_fusion.2.where_ref, bf16[256,5120]{1,0:T(8,128)(2,1)} %refs_0_.3, bf16[256,5120]{1,0:T(8,128)(2,1)} %collective-permute-done.21.refs_1_, bf16[256,5120]{1,0:T(8,128)(2,1)} %collective-permute-done.1.refs_2_, bf16[256,5120]{1,0:T(8,128)(2,1)} %collective-permute-done.22.refs_3_, ...), custom_call_target="tpu_custom_call" | custom-call | flops 6710886400 | bytes 18350080 | tf_op jit(solution)/shard_map/pallas_call | solution.py:334
  107.5 1.3 shard_map.104
  108.8 4.4 %collective-permute-done.23.rest_0_ = bf16[1024,256]{1,0:T(8,128)(2,1)S(1)} collective-permute-done((bf16[1024,256]{1,0:T(8,128)(2,1)}, bf16[1024,256]{1,0:T(8,128)(2,1)S(1)}, u32[]{:S(2)}, u32[]{:S(2)}) %collective-permute-start.23) | collective-permute-done | bytes 524320 | tf_op jit(solution)/shard_map/ppermute | solution.py:213
  113.2 14.9 %shard_map.106 = (f32[1024,640]{1,0:T(8,128)S(1)}, bf16[1024,256]{1,0:T(8,128)(2,1)S(1)}) custom-call(s32[8]{0:T(128)S(1)} %pad_add_fusion.1.qspan_ref, s32[1,8]{1,0:T(1,128)S(1)} %add_bitcast_fusion.1.kspan_ref, bf16[1024,640]{1,0:T(8,128)(2,1)S(1)} %copy-done.4, bf16[1024,640]{1,0:T(8,128)(2,1)S(1)} %get-tuple-element.91.g_ref, ...), custom_call_target="tpu_custom_call" | custom-call | flops 6710886400 | bytes 6815744 | tf_op jit(solution)/shard_map/pallas_call | solution.py:108
  128.1 7.5 %collective-permute-start.26 = (bf16[1024,256]{1,0:T(8,128)(2,1)S(1)}, bf16[1024,256]{1,0:T(8,128)(2,1)S(1)}, u32[]{:S(2)}, u32[]{:S(2)}) collective-permute-start(bf16[1024,256]{1,0:T(8,128)(2,1)S(1)} %get-tuple-element.110), channel_id=1, source_target_pairs={{0,31},{1,0},{2,1},{3,2},{4,3},{5,4},{6,5},{7,6},{8,7},{9,8},{10,9... | collective-permute-start | bytes 1572872 | tf_op jit(solution)/shard_map/ppermute | solution.py:213
  135.6 15.0 %shard_map.107 = (f32[1024,640]{1,0:T(8,128)S(1)}, bf16[1024,256]{1,0:T(8,128)(2,1)S(1)}) custom-call(s32[8]{0:T(128)S(1)} %pad_add_fusion.1.qspan_ref, s32[1,8]{1,0:T(1,128)S(1)} %add_bitcast_fusion.kspan_ref, bf16[1024,640]{1,0:T(8,128)(2,1)S(1)} %copy-done.4, bf16[1024,640]{1,0:T(8,128)(2,1)S(1)} %get-tuple-element.91.g_ref, ...), custom_call_target="tpu_custom_call" | custom-call | flops 6710886400 | bytes 6815744 | tf_op jit(solution)/shard_map/pallas_call | solution.py:108
  150.6 8.9 %shard_map.108 = (bf16[512,640]{1,0:T(8,128)(2,1)S(1)}, f32[1024,256]{1,0:T(8,128)S(1)}) custom-call(s32[8]{0:T(128)S(1)} %pad_add_fusion.1.qspan_ref, s32[1,8]{1,0:T(1,128)S(1)} %bitcast.20, bf16[1024,640]{1,0:T(8,128)(2,1)S(1)} %copy-done.4, bf16[1024,640]{1,0:T(8,128)(2,1)S(1)} %get-tuple-element.91.g_ref, f32[5,1,1024]{2,1,0:T(1,128)S(1)} %broadcast_in_dim.14.lse_ref, ...), custom_call_target="tpu_custom_call" | custom-call | flops 3355443200 | bytes 4194304 | tf_op jit(solution)/shard_map/pallas_call | solution.py:108
  159.5 8.9 %shard_map.109 = (bf16[512,640]{1,0:T(8,128)(2,1)S(1)}, f32[1024,256]{1,0:T(8,128)S(1)}) custom-call(s32[8]{0:T(128)S(1)} %pad_add_fusion.1.qspan_ref, s32[1,8]{1,0:T(1,128)S(1)} %bitcast.21, bf16[1024,640]{1,0:T(8,128)(2,1)S(1)} %copy-done.4, bf16[1024,640]{1,0:T(8,128)(2,1)S(1)} %get-tuple-element.91.g_ref, f32[5,1,1024]{2,1,0:T(1,128)S(1)} %broadcast_in_dim.14.lse_ref, ...), custom_call_target="tpu_custom_call" | custom-call | flops 3355443200 | bytes 4194304 | tf_op jit(solution)/shard_map/pallas_call | solution.py:108
  168.4 1.1 collective-permute-start.27
  170.0 1.8 collective-permute-start.29
  171.8 0.8 fusion.1
  172.6 9.2 %collective-permute-done.27.refs_2_ = bf16[1024,256]{1,0:T(8,128)(2,1)S(1)} collective-permute-done((bf16[1024,256]{1,0:T(8,128)(2,1)S(1)}, bf16[1024,256]{1,0:T(8,128)(2,1)S(1)}, u32[]{:S(2)}, u32[]{:S(2)}) %collective-permute-start.27) | collective-permute-done | bytes 524320 | tf_op jit(solution)/shard_map/ppermute | solution.py:213
  182.7 5.3 %collective-permute-done.28.refs_2_ = bf16[256,640]{1,0:T(8,128)(2,1)S(1)} collective-permute-done((bf16[256,640]{1,0:T(8,128)(2,1)S(1)}, bf16[256,640]{1,0:T(8,128)(2,1)S(1)}, u32[]{:S(2)}, u32[]{:S(2)}) %collective-permute-start.28) | collective-permute-done | bytes 327712 | tf_op jit(solution)/shard_map/ppermute | solution.py:217
  188.0 7.0 %collective-permute-done.29.refs_3_ = bf16[256,640]{1,0:T(8,128)(2,1)S(1)} collective-permute-done((bf16[256,640]{1,0:T(8,128)(2,1)S(1)}, bf16[256,640]{1,0:T(8,128)(2,1)S(1)}, u32[]{:S(2)}, u32[]{:S(2)}) %collective-permute-start.29) | collective-permute-done | bytes 327712 | tf_op jit(solution)/shard_map/ppermute | solution.py:217
  195.4 1.1 collective-permute-start.31
  197.2 0.7 copy-done.14
  197.9 2.4 %shard_map.111 = bf16[256,2560]{1,0:T(8,128)(2,1)} custom-call(s32[4]{0:T(128)} %copy-done.3, bf16[256,640]{1,0:T(8,128)(2,1)} %get-tuple-element.132.refs_0_, bf16[256,640]{1,0:T(8,128)(2,1)} %copy-done.14, bf16[256,640]{1,0:T(8,128)(2,1)} %copy-done.12, bf16[256,640]{1,0:T(8,128)(2,1)} %copy-done.13), custom_call_target="tpu_custom_call" | custom-call | bytes 2621440 | tf_op jit(solution)/shard_map/pallas_call | solution.py:176
  200.4 3.1 %collective-permute-done.32.refs_3_ = bf16[256,256]{1,0:T(8,128)(2,1)S(1)} collective-permute-done((bf16[256,256]{1,0:T(8,128)(2,1)S(1)}, bf16[256,256]{1,0:T(8,128)(2,1)S(1)}, u32[]{:S(2)}, u32[]{:S(2)}) %collective-permute-start.32) | collective-permute-done | bytes 131104 | tf_op jit(solution)/shard_map/ppermute | solution.py:217
  204.1 2.0 shard_map.112
  (117 shorter events, 7.2 us)
Async XLA Ops:
  7.2 86.8 %all-gather.2.cloned.1.call-start = ((), (), s32[]{:S(2)}) async-start(), calls=%async_computation | async-start | bytes 6963200 | tf_op jit(solution)/shard_map/all_gather | solution.py:369
  8.2 10.1 %collective-permute-start = (bf16[160,896]{1,0:T(8,128)(2,1)S(1)}, bf16[160,896]{1,0:T(8,128)(2,1)S(1)}, u32[]{:S(2)}, u32[]{:S(2)}) collective-permute-start(bf16[160,896]{1,0:T(8,128)(2,1)S(1)} %pad_maximum_fusion.1), channel_id=1, source_target_pairs={{0,4},{4,0},{1,5},{5,1},{2,6},{6,2},{3,7},{7,3},{8,12},{12,8},{9,1... | collective-permute-start | bytes 860168 | tf_op jit(solution)/shard_map/ppermute | solution.py:213
  18.3 61.6 %copy-start.23 = (f32[1024,5]{0,1:T(8,128)S(1)}, f32[1024,5]{0,1:T(8,128)}, u32[]{:S(2)}) copy-start(f32[1024,5]{0,1:T(8,128)} %param.14) | copy-start | bytes 61444
  18.3 62.4 %copy-start.22 = (s32[256]{0:T(256)S(1)}, s32[256]{0:T(256)}, u32[]{:S(2)}) copy-start(s32[256]{0:T(256)} %param.15) | copy-start | bytes 3076
  18.3 62.7 %copy-start.5 = (bf16[256,2560]{1,0:T(8,128)(2,1)S(1)}, bf16[256,2560]{1,0:T(8,128)(2,1)}, u32[]{:S(2)}) copy-start(bf16[256,2560]{1,0:T(8,128)(2,1)} %param.12) | copy-start | bytes 3932164
  20.2 57.2 %collective-permute-start.1 = (bf16[256,5120]{1,0:T(8,128)(2,1)}, bf16[256,5120]{1,0:T(8,128)(2,1)}, u32[]{:S(2)}, u32[]{:S(2)}) collective-permute-start(bf16[256,5120]{1,0:T(8,128)(2,1)} %refs_0_.3), channel_id=1, source_target_pairs={{0,64},{32,96},{64,0},{96,32},{1,65},{33,97},{65,1},{97,33},{2,66}... | collective-permute-start | bytes 7864328 | tf_op jit(solution)/shard_map/ppermute | solution.py:217
  23.2 6.6 %collective-permute-start.2 = (bf16[160,256]{1,0:T(8,128)(2,1)S(1)}, bf16[160,256]{1,0:T(8,128)(2,1)S(1)}, u32[]{:S(2)}, u32[]{:S(2)}) collective-permute-start(bf16[160,256]{1,0:T(8,128)(2,1)S(1)} %pad_maximum_fusion.2), channel_id=1, source_target_pairs={{0,1},{1,2},{2,3},{3,0},{4,5},{5,6},{6,7},{7,4},{8,9},{9,10},{10,1... | collective-permute-start | bytes 245768 | tf_op jit(solution)/shard_map/ppermute | solution.py:213
  24.9 4.9 %collective-permute-start.3 = (bf16[160,256]{1,0:T(8,128)(2,1)S(1)}, bf16[160,256]{1,0:T(8,128)(2,1)S(1)}, u32[]{:S(2)}, u32[]{:S(2)}) collective-permute-start(bf16[160,256]{1,0:T(8,128)(2,1)S(1)} %pad_maximum_fusion.2), channel_id=1, source_target_pairs={{0,3},{1,0},{2,1},{3,2},{4,7},{5,4},{6,5},{7,6},{8,11},{9,8},{10,9... | collective-permute-start | bytes 245768 | tf_op jit(solution)/shard_map/ppermute | solution.py:213
  27.1 4.5 %collective-permute-start.4 = (bf16[160,256]{1,0:T(8,128)(2,1)S(1)}, bf16[160,256]{1,0:T(8,128)(2,1)S(1)}, u32[]{:S(2)}, u32[]{:S(2)}) collective-permute-start(bf16[160,256]{1,0:T(8,128)(2,1)S(1)} %pad_maximum_fusion.3), channel_id=1, source_target_pairs={{0,8},{8,16},{16,24},{24,0},{1,9},{9,17},{17,25},{25,1},{2,10},{10... | collective-permute-start | bytes 245768 | tf_op jit(solution)/shard_map/ppermute | solution.py:213
  28.4 3.7 %collective-permute-start.5 = (bf16[160,256]{1,0:T(8,128)(2,1)S(1)}, bf16[160,256]{1,0:T(8,128)(2,1)S(1)}, u32[]{:S(2)}, u32[]{:S(2)}) collective-permute-start(bf16[160,256]{1,0:T(8,128)(2,1)S(1)} %pad_maximum_fusion.3), channel_id=1, source_target_pairs={{0,24},{8,0},{16,8},{24,16},{1,25},{9,1},{17,9},{25,17},{2,26},{10... | collective-permute-start | bytes 245768 | tf_op jit(solution)/shard_map/ppermute | solution.py:213
  32.1 5.4 %collective-permute-start.6 = (bf16[80,256]{1,0:T(8,128)(2,1)S(1)}, bf16[80,256]{1,0:T(8,128)(2,1)S(1)}, u32[]{:S(2)}, u32[]{:S(2)}) collective-permute-start(bf16[80,256]{1,0:T(8,128)(2,1)S(1)} %slice.61), channel_id=1, source_target_pairs={{0,1},{1,2},{2,3},{3,0},{4,5},{5,6},{6,7},{7,4},{8,9},{9,10},{10,1... | collective-permute-start | bytes 122888 | tf_op jit(solution)/shard_map/ppermute | solution.py:213
  32.1 5.4 %collective-permute-start.7 = (bf16[80,256]{1,0:T(8,128)(2,1)S(1)}, bf16[80,256]{1,0:T(8,128)(2,1)S(1)}, u32[]{:S(2)}, u32[]{:S(2)}) collective-permute-start(bf16[80,256]{1,0:T(8,128)(2,1)S(1)} %slice.62), channel_id=1, source_target_pairs={{0,3},{1,0},{2,1},{3,2},{4,7},{5,4},{6,5},{7,6},{8,11},{9,8},{10,9... | collective-permute-start | bytes 122888 | tf_op jit(solution)/shard_map/ppermute | solution.py:213
  34.7 5.0 %collective-permute-start.8 = (bf16[80,256]{1,0:T(8,128)(2,1)S(1)}, bf16[80,256]{1,0:T(8,128)(2,1)S(1)}, u32[]{:S(2)}, u32[]{:S(2)}) collective-permute-start(bf16[80,256]{1,0:T(8,128)(2,1)S(1)} %slice.63), channel_id=1, source_target_pairs={{0,8},{8,16},{16,24},{24,0},{1,9},{9,17},{17,25},{25,1},{2,10},{10... | collective-permute-start | bytes 122888 | tf_op jit(solution)/shard_map/ppermute | solution.py:213
  36.0 3.8 %collective-permute-start.9 = (bf16[80,256]{1,0:T(8,128)(2,1)S(1)}, bf16[80,256]{1,0:T(8,128)(2,1)S(1)}, u32[]{:S(2)}, u32[]{:S(2)}) collective-permute-start(bf16[80,256]{1,0:T(8,128)(2,1)S(1)} %slice.64), channel_id=1, source_target_pairs={{0,24},{8,0},{16,8},{24,16},{1,25},{9,1},{17,9},{25,17},{2,26},{10... | collective-permute-start | bytes 122888 | tf_op jit(solution)/shard_map/ppermute | solution.py:213
  39.7 42.5 %copy-start.10 = (bf16[640,256]{1,0:T(8,128)(2,1)}, bf16[640,256]{1,0:T(8,128)(2,1)S(1)}, u32[]{:S(2)}) copy-start(bf16[640,256]{1,0:T(8,128)(2,1)S(1)} %constant_dynamic-update-slice_fusion.8.refs_9_) | copy-start | bytes 983044
  39.8 12.7 %collective-permute-start.12 = (bf16[640,256]{1,0:T(8,128)(2,1)S(1)}, bf16[640,256]{1,0:T(8,128)(2,1)S(1)}, u32[]{:S(2)}, u32[]{:S(2)}) collective-permute-start(bf16[640,256]{1,0:T(8,128)(2,1)S(1)} %constant_dynamic-update-slice_fusion.8.refs_9_), channel_id=1, source_target_pairs={{0,1},{1,2},{2,3},{3,0},{4,5},{5,6},{6,7},{7,4},{8,9},{9,10},{10,1... | collective-permute-start | bytes 983048 | tf_op jit(solution)/shard_map/ppermute | solution.py:213
  39.8 12.6 %collective-permute-start.13 = (bf16[640,256]{1,0:T(8,128)(2,1)S(1)}, bf16[640,256]{1,0:T(8,128)(2,1)S(1)}, u32[]{:S(2)}, u32[]{:S(2)}) collective-permute-start(bf16[640,256]{1,0:T(8,128)(2,1)S(1)} %constant_dynamic-update-slice_fusion.8.refs_9_), channel_id=1, source_target_pairs={{0,3},{1,0},{2,1},{3,2},{4,7},{5,4},{6,5},{7,6},{8,11},{9,8},{10,9... | collective-permute-start | bytes 983048 | tf_op jit(solution)/shard_map/ppermute | solution.py:213
  42.5 9.9 %collective-permute-start.10 = (bf16[640,256]{1,0:T(8,128)(2,1)S(1)}, bf16[640,256]{1,0:T(8,128)(2,1)S(1)}, u32[]{:S(2)}, u32[]{:S(2)}) collective-permute-start(bf16[640,256]{1,0:T(8,128)(2,1)S(1)} %constant_dynamic-update-slice_fusion.2.refs_4_), channel_id=1, source_target_pairs={{0,8},{8,16},{16,24},{24,0},{1,9},{9,17},{17,25},{25,1},{2,10},{10... | collective-permute-start | bytes 983048 | tf_op jit(solution)/shard_map/ppermute | solution.py:213
  43.5 9.0 %collective-permute-start.11 = (bf16[640,256]{1,0:T(8,128)(2,1)S(1)}, bf16[640,256]{1,0:T(8,128)(2,1)S(1)}, u32[]{:S(2)}, u32[]{:S(2)}) collective-permute-start(bf16[640,256]{1,0:T(8,128)(2,1)S(1)} %constant_dynamic-update-slice_fusion.2.refs_4_), channel_id=1, source_target_pairs={{0,24},{8,0},{16,8},{24,16},{1,25},{9,1},{17,9},{25,17},{2,26},{10... | collective-permute-start | bytes 983048 | tf_op jit(solution)/shard_map/ppermute | solution.py:213
  52.4 32.3 %copy-start.6 = (bf16[640,256]{1,0:T(8,128)(2,1)}, bf16[640,256]{1,0:T(8,128)(2,1)S(1)}, u32[]{:S(2)}) copy-start(bf16[640,256]{1,0:T(8,128)(2,1)S(1)} %collective-permute-done.12.refs_10_) | copy-start | bytes 983044
  52.5 32.3 %copy-start.7 = (bf16[640,256]{1,0:T(8,128)(2,1)}, bf16[640,256]{1,0:T(8,128)(2,1)S(1)}, u32[]{:S(2)}) copy-start(bf16[640,256]{1,0:T(8,128)(2,1)S(1)} %collective-permute-done.13.refs_13_) | copy-start | bytes 983044
  52.5 29.6 %copy-start.8 = (bf16[640,256]{1,0:T(8,128)(2,1)}, bf16[640,256]{1,0:T(8,128)(2,1)S(1)}, u32[]{:S(2)}) copy-start(bf16[640,256]{1,0:T(8,128)(2,1)S(1)} %collective-permute-done.10.refs_5_) | copy-start | bytes 983044
  52.5 29.6 %copy-start.9 = (bf16[640,256]{1,0:T(8,128)(2,1)}, bf16[640,256]{1,0:T(8,128)(2,1)S(1)}, u32[]{:S(2)}) copy-start(bf16[640,256]{1,0:T(8,128)(2,1)S(1)} %collective-permute-done.11.refs_8_) | copy-start | bytes 983044
  52.5 5.7 %collective-permute-start.14 = (bf16[320,256]{1,0:T(8,128)(2,1)S(1)}, bf16[320,256]{1,0:T(8,128)(2,1)S(1)}, u32[]{:S(2)}, u32[]{:S(2)}) collective-permute-start(bf16[320,256]{1,0:T(8,128)(2,1)S(1)} %slice.65), channel_id=1, source_target_pairs={{0,8},{8,16},{16,24},{24,0},{1,9},{9,17},{17,25},{25,1},{2,10},{10... | collective-permute-start | bytes 491528 | tf_op jit(solution)/shard_map/ppermute | solution.py:213
  52.6 14.1 %collective-permute-start.15 = (bf16[320,256]{1,0:T(8,128)(2,1)S(1)}, bf16[320,256]{1,0:T(8,128)(2,1)S(1)}, u32[]{:S(2)}, u32[]{:S(2)}) collective-permute-start(bf16[320,256]{1,0:T(8,128)(2,1)S(1)} %slice.66), channel_id=1, source_target_pairs={{0,24},{8,0},{16,8},{24,16},{1,25},{9,1},{17,9},{25,17},{2,26},{10... | collective-permute-start | bytes 491528 | tf_op jit(solution)/shard_map/ppermute | solution.py:213
  55.4 11.3 %collective-permute-start.16 = (bf16[320,256]{1,0:T(8,128)(2,1)S(1)}, bf16[320,256]{1,0:T(8,128)(2,1)S(1)}, u32[]{:S(2)}, u32[]{:S(2)}) collective-permute-start(bf16[320,256]{1,0:T(8,128)(2,1)S(1)} %slice.67), channel_id=1, source_target_pairs={{0,1},{1,2},{2,3},{3,0},{4,5},{5,6},{6,7},{7,4},{8,9},{9,10},{10,1... | collective-permute-start | bytes 491528 | tf_op jit(solution)/shard_map/ppermute | solution.py:213
  55.5 11.2 %collective-permute-start.17 = (bf16[320,256]{1,0:T(8,128)(2,1)S(1)}, bf16[320,256]{1,0:T(8,128)(2,1)S(1)}, u32[]{:S(2)}, u32[]{:S(2)}) collective-permute-start(bf16[320,256]{1,0:T(8,128)(2,1)S(1)} %slice.68), channel_id=1, source_target_pairs={{0,3},{1,0},{2,1},{3,2},{4,7},{5,4},{6,5},{7,6},{8,11},{9,8},{10,9... | collective-permute-start | bytes 491528 | tf_op jit(solution)/shard_map/ppermute | solution.py:213
  58.2 26.6 %copy-start.15 = (bf16[320,256]{1,0:T(8,128)(2,1)}, bf16[320,256]{1,0:T(8,128)(2,1)S(1)}, u32[]{:S(2)}) copy-start(bf16[320,256]{1,0:T(8,128)(2,1)S(1)} %collective-permute-done.14.refs_6_) | copy-start | bytes 491524
  58.2 26.0 %collective-permute-start.21 = (bf16[256,5120]{1,0:T(8,128)(2,1)}, bf16[256,5120]{1,0:T(8,128)(2,1)}, u32[]{:S(2)}, u32[]{:S(2)}) collective-permute-start(bf16[256,5120]{1,0:T(8,128)(2,1)} %refs_0_.3), channel_id=1, source_target_pairs={{0,32},{32,0},{64,96},{96,64},{1,33},{33,1},{65,97},{97,65},{2,34}... | collective-permute-start | bytes 7864328 | tf_op jit(solution)/shard_map/ppermute | solution.py:217
  66.7 10.8 %copy-start.17 = (bf16[320,256]{1,0:T(8,128)(2,1)}, bf16[320,256]{1,0:T(8,128)(2,1)S(1)}, u32[]{:S(2)}) copy-start(bf16[320,256]{1,0:T(8,128)(2,1)S(1)} %collective-permute-done.16.refs_11_) | copy-start | bytes 491524
  67.3 12.5 %copy-start.18 = (bf16[320,256]{1,0:T(8,128)(2,1)}, bf16[320,256]{1,0:T(8,128)(2,1)S(1)}, u32[]{:S(2)}) copy-start(bf16[320,256]{1,0:T(8,128)(2,1)S(1)} %collective-permute-done.17.refs_12_) | copy-start | bytes 491524
  77.5 7.3 %collective-permute-start.22 = (bf16[256,5120]{1,0:T(8,128)(2,1)}, bf16[256,5120]{1,0:T(8,128)(2,1)}, u32[]{:S(2)}, u32[]{:S(2)}) collective-permute-start(bf16[256,5120]{1,0:T(8,128)(2,1)} %collective-permute-done.1.refs_2_), channel_id=1, source_target_pairs={{0,32},{32,0},{64,96},{96,64},{1,33},{33,1},{65,97},{97,65},{2,34}... | collective-permute-start | bytes 7864328 | tf_op jit(solution)/shard_map/ppermute | solution.py:217
  80.7 26.8 %copy-start.3 = (s32[4]{0:T(128)}, s32[4]{0:T(128)S(1)}, u32[]{:S(2)}) copy-start(s32[4]{0:T(128)S(1)} %pad_add_fusion.mine_ref) | copy-start | bytes 52
  82.1 25.4 %collective-permute-start.18 = (bf16[256,640]{1,0:T(8,128)(2,1)}, bf16[256,640]{1,0:T(8,128)(2,1)S(1)}, u32[]{:S(2)}, u32[]{:S(2)}) collective-permute-start(bf16[256,640]{1,0:T(8,128)(2,1)} %get-tuple-element.83), channel_id=1, source_target_pairs={{0,32},{32,0},{64,96},{96,64},{1,33},{33,1},{65,97},{97,65},{2,34}... | collective-permute-start | bytes 983048 | tf_op jit(solution)/shard_map/ppermute | solution.py:217
  82.3 25.2 %collective-permute-start.19 = (bf16[256,640]{1,0:T(8,128)(2,1)}, bf16[256,640]{1,0:T(8,128)(2,1)S(1)}, u32[]{:S(2)}, u32[]{:S(2)}) collective-permute-start(bf16[256,640]{1,0:T(8,128)(2,1)} %get-tuple-element.84), channel_id=1, source_target_pairs={{0,64},{32,96},{64,0},{96,32},{1,65},{33,97},{65,1},{97,33},{2,66}... | collective-permute-start | bytes 983048 | tf_op jit(solution)/shard_map/ppermute | solution.py:217
  83.6 23.9 %collective-permute-start.20 = (bf16[256,640]{1,0:T(8,128)(2,1)}, bf16[256,640]{1,0:T(8,128)(2,1)S(1)}, u32[]{:S(2)}, u32[]{:S(2)}) collective-permute-start(bf16[256,640]{1,0:T(8,128)(2,1)} %get-tuple-element.85), channel_id=1, source_target_pairs={{0,96},{32,64},{64,32},{96,0},{1,97},{33,65},{65,33},{97,1},{2,98}... | collective-permute-start | bytes 983048 | tf_op jit(solution)/shard_map/ppermute | solution.py:217
  92.1 15.4 %copy-start = (bf16[1024,640]{1,0:T(8,128)(2,1)S(1)}, bf16[1024,640]{1,0:T(8,128)(2,1)}, u32[]{:S(2)}) copy-start(bf16[1024,640]{1,0:T(8,128)(2,1)} %refs_4_.1) | copy-start | bytes 3932164
  92.1 21.1 %collective-permute-start.23 = (bf16[1024,256]{1,0:T(8,128)(2,1)}, bf16[1024,256]{1,0:T(8,128)(2,1)S(1)}, u32[]{:S(2)}, u32[]{:S(2)}) collective-permute-start(bf16[1024,256]{1,0:T(8,128)(2,1)} %shard_map.105.rest_0_), channel_id=1, source_target_pairs={{0,1},{1,2},{2,3},{3,4},{4,5},{5,6},{6,7},{7,8},{8,9},{9,10},{10,1... | collective-permute-start | bytes 1572872 | tf_op jit(solution)/shard_map/ppermute | solution.py:213
  113.2 22.4 %collective-permute-start.24 = (bf16[1024,256]{1,0:T(8,128)(2,1)S(1)}, bf16[1024,256]{1,0:T(8,128)(2,1)S(1)}, u32[]{:S(2)}, u32[]{:S(2)}) collective-permute-start(bf16[1024,256]{1,0:T(8,128)(2,1)S(1)} %collective-permute-done.23.rest_0_), channel_id=1, source_target_pairs={{0,1},{1,2},{2,3},{3,4},{4,5},{5,6},{6,7},{7,8},{8,9},{9,10},{10,1... | collective-permute-start | bytes 1572872 | tf_op jit(solution)/shard_map/ppermute | solution.py:213
  128.1 44.5 %collective-permute-start.26 = (bf16[1024,256]{1,0:T(8,128)(2,1)S(1)}, bf16[1024,256]{1,0:T(8,128)(2,1)S(1)}, u32[]{:S(2)}, u32[]{:S(2)}) collective-permute-start(bf16[1024,256]{1,0:T(8,128)(2,1)S(1)} %get-tuple-element.110), channel_id=1, source_target_pairs={{0,31},{1,0},{2,1},{3,2},{4,3},{5,4},{6,5},{7,6},{8,7},{9,8},{10,9... | collective-permute-start | bytes 1572872 | tf_op jit(solution)/shard_map/ppermute | solution.py:213
  135.6 15.0 %copy-start.1 = (bf16[1024,256]{1,0:T(8,128)(2,1)S(1)}, bf16[1024,256]{1,0:T(8,128)(2,1)}, u32[]{:S(2)}) copy-start(bf16[1024,256]{1,0:T(8,128)(2,1)} %shard_map.105.rest_0_) | copy-start | bytes 1572868
  168.4 13.5 %collective-permute-start.27 = (bf16[1024,256]{1,0:T(8,128)(2,1)S(1)}, bf16[1024,256]{1,0:T(8,128)(2,1)S(1)}, u32[]{:S(2)}, u32[]{:S(2)}) collective-permute-start(bf16[1024,256]{1,0:T(8,128)(2,1)S(1)} %get-tuple-element.111), channel_id=1, source_target_pairs={{0,30},{1,31},{2,0},{3,1},{4,2},{5,3},{6,4},{7,5},{8,6},{9,7},{10,... | collective-permute-start | bytes 1572872 | tf_op jit(solution)/shard_map/ppermute | solution.py:213
  169.6 18.4 %collective-permute-start.28 = (bf16[256,640]{1,0:T(8,128)(2,1)S(1)}, bf16[256,640]{1,0:T(8,128)(2,1)S(1)}, u32[]{:S(2)}, u32[]{:S(2)}) collective-permute-start(bf16[256,640]{1,0:T(8,128)(2,1)S(1)} %get-tuple-element.130), channel_id=1, source_target_pairs={{0,64},{32,96},{64,0},{96,32},{1,65},{33,97},{65,1},{97,33},{2,66}... | collective-permute-start | bytes 983048 | tf_op jit(solution)/shard_map/ppermute | solution.py:217
  170.0 25.0 %collective-permute-start.29 = (bf16[256,640]{1,0:T(8,128)(2,1)S(1)}, bf16[256,640]{1,0:T(8,128)(2,1)S(1)}, u32[]{:S(2)}, u32[]{:S(2)}) collective-permute-start(bf16[256,640]{1,0:T(8,128)(2,1)S(1)} %get-tuple-element.129), channel_id=1, source_target_pairs={{0,96},{32,64},{64,32},{96,0},{1,97},{33,65},{65,33},{97,1},{2,98}... | collective-permute-start | bytes 983048 | tf_op jit(solution)/shard_map/ppermute | solution.py:217
  172.6 24.6 %collective-permute-start.25 = (bf16[256,640]{1,0:T(8,128)(2,1)S(1)}, bf16[256,640]{1,0:T(8,128)(2,1)S(1)}, u32[]{:S(2)}, u32[]{:S(2)}) collective-permute-start(bf16[256,640]{1,0:T(8,128)(2,1)S(1)} %get-tuple-element.131), channel_id=1, source_target_pairs={{0,32},{32,0},{64,96},{96,64},{1,33},{33,1},{65,97},{97,65},{2,34}... | collective-permute-start | bytes 983048 | tf_op jit(solution)/shard_map/ppermute | solution.py:217
  195.0 5.3 %collective-permute-start.30 = (bf16[256,256]{1,0:T(8,128)(2,1)S(1)}, bf16[256,256]{1,0:T(8,128)(2,1)S(1)}, u32[]{:S(2)}, u32[]{:S(2)}) collective-permute-start(bf16[256,256]{1,0:T(8,128)(2,1)S(1)} %get-tuple-element.120), channel_id=1, source_target_pairs={{0,32},{32,0},{64,96},{96,64},{1,33},{33,1},{65,97},{97,65},{2,34}... | collective-permute-start | bytes 393224 | tf_op jit(solution)/shard_map/ppermute | solution.py:217
  195.4 5.0 %collective-permute-start.31 = (bf16[256,256]{1,0:T(8,128)(2,1)S(1)}, bf16[256,256]{1,0:T(8,128)(2,1)S(1)}, u32[]{:S(2)}, u32[]{:S(2)}) collective-permute-start(bf16[256,256]{1,0:T(8,128)(2,1)S(1)} %get-tuple-element.121), channel_id=1, source_target_pairs={{0,64},{32,96},{64,0},{96,32},{1,65},{33,97},{65,1},{97,33},{2,66}... | collective-permute-start | bytes 393224 | tf_op jit(solution)/shard_map/ppermute | solution.py:217
  196.5 7.0 %collective-permute-start.32 = (bf16[256,256]{1,0:T(8,128)(2,1)S(1)}, bf16[256,256]{1,0:T(8,128)(2,1)S(1)}, u32[]{:S(2)}, u32[]{:S(2)}) collective-permute-start(bf16[256,256]{1,0:T(8,128)(2,1)S(1)} %get-tuple-element.122), channel_id=1, source_target_pairs={{0,96},{32,64},{64,32},{96,0},{1,97},{33,65},{65,33},{97,1},{2,98}... | collective-permute-start | bytes 393224 | tf_op jit(solution)/shard_map/ppermute | solution.py:217
  (10 other events, 36.0 us)
Sparse Core Ops, SparseCore 0:
  20.3 69.1 all-gather.1
